TPU v7x, 32 devices: a whole 2x2x4 slice. The times are simulated.
32 devices in a mesh: dp: 8 (over z, x), tensor: 4 (over y, core).
Axes of the slice: x: 2, y: 2, z: 4, core: 2. Of those that a mesh axis runs over, the one named last changes fastest.
Arguments:
- tokens: bfloat16 [16384, 2048], P(('dp', 'tensor')), may hold values from -8 to 8
- attention_norm_gain: float32 [2048], replicated, may hold values from 0.5 to 1.5
- w_query: bfloat16 [2048, 2048], P(None, 'tensor'), may hold values from -0.125 to 0.125
- w_key: bfloat16 [2048, 2048], P(None, 'tensor'), may hold values from -0.125 to 0.125
- w_value: bfloat16 [2048, 2048], P(None, 'tensor'), may hold values from -0.125 to 0.125
- w_out: bfloat16 [2048, 2048], P('tensor'), may hold values from -0.125 to 0.125
- gate_bias: float32 [16], P('tensor'), may hold values from -2 to 2
- feedforward_norm_gain: float32 [2048], replicated, may hold values from 0.5 to 1.5
- w_gate: bfloat16 [2048, 8192], P(None, 'tensor'), may hold values from -0.125 to 0.125
- w_up: bfloat16 [2048, 8192], P(None, 'tensor'), may hold values from -0.125 to 0.125
- w_down: bfloat16 [8192, 2048], P('tensor'), may hold values from -0.0625 to 0.0625
- seg_starts: int32 [8], P('dp'), may hold values from 0 to 1, as said below
- seg_valid: int32 [8], P('dp'), may hold values from 1024 to 2048, as said below
- cotangent: bfloat16 [16384, 2048], P(('dp', 'tensor')), may hold values from -6 to 6
Outputs:
- out: bfloat16 [16384, 2048], P(('dp', 'tensor'))
- grad_tokens: float32 [16384, 2048], P(('dp', 'tensor'))
- grad_gain1: float32 [2048], replicated
- grad_w_query: float32 [2048, 2048], P('dp', 'tensor')
- grad_w_key: float32 [2048, 2048], P('dp', 'tensor')
- grad_w_value: float32 [2048, 2048], P('dp', 'tensor')
- grad_w_out: float32 [2048, 2048], P('tensor', 'dp')
- grad_gate_bias: float32 [16], replicated
- grad_gain2: float32 [2048], replicated
- grad_w_gate: float32 [2048, 8192], P('dp', 'tensor')
- grad_w_up: float32 [2048, 8192], P('dp', 'tensor')
- grad_w_down: float32 [8192, 2048], P('tensor', 'dp')
Inputs may be any that keep to these rules, and one draw needn't show every extreme that they name: `seg_starts`: 1 where the segment begins a sequence and 0 where it continues the sequence of the segment before it; the first segment begins one; segments 1, 4 and 7 continue the segment before them. `seg_valid`: the number of leading live rows of a segment; it is 2048 in every segment but the last one of a sequence.
All inputs are finite; a program needn't handle non-finite values.
Results may differ from a plain program's by a relative error of at most 0.015.
Values may be sent and summed in bfloat16 or wider, within the bound.
No kernel may reach another device: no remote copies, remote signals or barrier semaphores. Data moves between devices by JAX's collectives and lax.ppermute only.
A program may use at most 320 MiB of HBM per device.

v0:
```python
import jax
import jax.numpy as jnp
from jax import lax
from jax.sharding import PartitionSpec as P

HEADS = 16
HEAD = 128
SEG = 2048


EPSILON = 1e-06


def shifted(value, axis, steps):
    count = lax.axis_size(axis)
    leading, last = (max(0, -steps), min(count, count - steps))
    return lax.ppermute(value, axis, [(source, source + steps) for source in range(leading, last)])


def elu_plus(values):
    return jnp.where(values > 0, values + 1.0, jnp.exp(jnp.minimum(values, 0.0)))


def elu_slope(values):
    return jnp.where(values > 0, 1.0, jnp.exp(jnp.minimum(values, 0.0)))


def memory_terms(memory_in, norm_in, phi_q, phi_k, values):
    den_q = jnp.maximum(
        jnp.einsum("thd,hd->th", phi_q, norm_in, precision=lax.Precision.HIGHEST), 1.0
    )
    memory_read = (
        jnp.einsum("thd,hde->the", phi_q, memory_in, precision=lax.Precision.HIGHEST)
        / den_q[..., None]
    )
    den_k = jnp.maximum(
        jnp.einsum("thd,hd->th", phi_k, norm_in, precision=lax.Precision.HIGHEST), 1.0
    )
    recalled = (
        jnp.einsum("thd,hde->the", phi_k, memory_in, precision=lax.Precision.HIGHEST)
        / den_k[..., None]
    )
    memory_out = memory_in + jnp.einsum(
        "thd,the->hde", phi_k, values - recalled, precision=lax.Precision.HIGHEST
    )
    norm_out = norm_in + jnp.sum(phi_k, axis=0)
    return (memory_read, memory_out, norm_out)


def transition(phi_k, norm_in):
    den_k = jnp.maximum(
        jnp.einsum("thd,hd->th", phi_k, norm_in, precision=lax.Precision.HIGHEST), 1.0
    )
    identity_mat = jnp.eye(phi_k.shape[-1], dtype=jnp.float32)
    return identity_mat[None] - jnp.einsum(
        "thd,the->hde", phi_k / den_k[..., None], phi_k, precision=lax.Precision.HIGHEST
    )


def apply_map(seg_map, memory_now):
    return jnp.einsum("hij,hjk->hik", seg_map, memory_now, precision=lax.Precision.HIGHEST)


def body(
    tokens,
    attention_norm_gain,
    w_query,
    w_key,
    w_value,
    w_out,
    gate_bias,
    feedforward_norm_gain,
    w_gate,
    w_up,
    w_down,
    seg_starts,
    seg_valid,
    cotangent,
):
    heads_here = gate_bias.shape[0]
    score_scale = HEAD ** (-0.5)
    keep_flag = (1 - seg_starts[0]).astype(jnp.float32)
    valid_rows = seg_valid[0]
    block_rows = min(512, SEG)
    block_count = SEG // block_rows
    block_begins = jnp.arange(block_count) * block_rows
    position = jnp.arange(SEG)
    live_rows = (position < valid_rows).astype(jnp.float32)
    tokens_as_float = tokens.astype(jnp.float32)
    attention_inverse_rms = lax.rsqrt(
        jnp.mean(tokens_as_float * tokens_as_float, axis=-1, keepdims=True) + EPSILON
    )
    attention_unit_rows = tokens_as_float * attention_inverse_rms
    attention_normed_rows = (attention_unit_rows * attention_norm_gain).astype(jnp.bfloat16)
    rows_one = lax.all_gather(attention_normed_rows, "tensor", axis=0, tiled=True)
    queries = (
        jnp.dot(rows_one, w_query, preferred_element_type=jnp.float32)
        .astype(jnp.bfloat16)
        .reshape(SEG, heads_here, HEAD)
    )
    key_rows = (
        jnp.dot(rows_one, w_key, preferred_element_type=jnp.float32)
        .astype(jnp.bfloat16)
        .reshape(SEG, heads_here, HEAD)
    )
    values = (
        jnp.dot(rows_one, w_value, preferred_element_type=jnp.float32)
        .astype(jnp.bfloat16)
        .reshape(SEG, heads_here, HEAD)
    )

    def block_scores(begin_row):
        query_block = lax.dynamic_slice_in_dim(queries, begin_row, block_rows, 0)
        raw_scores = jnp.einsum(
            "thd,shd->hts", query_block, key_rows, preferred_element_type=jnp.float32
        )
        query_pos = begin_row + jnp.arange(block_rows)
        allowed = (position[None, :] <= query_pos[:, None]) & (position[None, :] < valid_rows)
        return (jnp.where(allowed[None], raw_scores * score_scale, -1e30), query_block)

    def attend_block(begin_row):
        scores, query_block = block_scores(begin_row)
        row_top = jnp.max(scores, axis=-1, keepdims=True)
        expo_terms = jnp.exp(scores - row_top)
        row_total = jnp.sum(expo_terms, axis=-1, keepdims=True)
        softmax_w = expo_terms / row_total
        log_total = row_top[..., 0] + jnp.log(row_total[..., 0])
        block_out = jnp.einsum(
            "hts,shd->thd",
            softmax_w.astype(jnp.bfloat16),
            values,
            preferred_element_type=jnp.float32,
        )
        return (block_out, log_total)

    local_blocks, log_totals = lax.map(attend_block, block_begins)
    local_read = local_blocks.reshape(SEG, heads_here, HEAD)
    queries_f = queries.astype(jnp.float32)
    keys_f = key_rows.astype(jnp.float32)
    values_f = values.astype(jnp.float32)
    phi_q = elu_plus(queries_f)
    phi_k = elu_plus(keys_f) * live_rows[:, None, None]
    zero_memory = jnp.zeros((heads_here, HEAD, HEAD), jnp.float32)
    zero_norm = jnp.zeros((heads_here, HEAD), jnp.float32)
    column_sums = jnp.sum(phi_k, axis=0)
    injected = jnp.einsum("thd,the->hde", phi_k, values_f, precision=lax.Precision.HIGHEST)
    chain_turns = lax.axis_size("dp") - 1

    def norm_step(turn, state_in):
        norm_send, norm_old = state_in
        norm_recv = shifted(norm_send, "dp", 1)
        norm_now = keep_flag * norm_recv
        return (norm_now + column_sums, norm_now)

    norm_state = lax.fori_loop(0, chain_turns, norm_step, (column_sums, zero_norm))
    norm_in = norm_state[1]
    seg_maps = transition(phi_k, norm_in)

    def memory_step(turn, state_in):
        memory_send, memory_old = state_in
        memory_recv = shifted(memory_send, "dp", 1)
        memory_now = keep_flag * memory_recv
        return (apply_map(seg_maps, memory_now) + injected, memory_now)

    memory_state = lax.fori_loop(0, chain_turns, memory_step, (injected, zero_memory))
    memory_in = memory_state[1]
    (memory_read, memory_unused, norm_unused), memory_pull = jax.vjp(
        memory_terms, memory_in, norm_in, phi_q, phi_k, values_f
    )
    sig_bias = jax.nn.sigmoid(gate_bias)
    mix_w = sig_bias[None, :, None]
    mixed_out = (
        (mix_w * memory_read + (1.0 - mix_w) * local_read)
        .astype(jnp.bfloat16)
        .reshape(SEG, heads_here * HEAD)
    )
    attention_part = lax.psum_scatter(
        jnp.dot(mixed_out, w_out, preferred_element_type=jnp.float32),
        "tensor",
        scatter_dimension=0,
        tiled=True,
    )
    hidden_rows_state = tokens_as_float + attention_part
    feedforward_inverse_rms = lax.rsqrt(
        jnp.mean(hidden_rows_state * hidden_rows_state, axis=-1, keepdims=True) + EPSILON
    )
    feedforward_unit_rows = hidden_rows_state * feedforward_inverse_rms
    feedforward_normed_rows = (feedforward_unit_rows * feedforward_norm_gain).astype(jnp.bfloat16)
    rows_two = lax.all_gather(feedforward_normed_rows, "tensor", axis=0, tiled=True)
    gate_pre = jnp.dot(rows_two, w_gate, preferred_element_type=jnp.float32)
    up_proj = jnp.dot(rows_two, w_up, preferred_element_type=jnp.float32)
    sig_gate = jax.nn.sigmoid(gate_pre)
    silu_gate = gate_pre * sig_gate
    inner_act = (silu_gate * up_proj).astype(jnp.bfloat16)
    mlp_part = lax.psum_scatter(
        jnp.dot(inner_act, w_down, preferred_element_type=jnp.float32),
        "tensor",
        scatter_dimension=0,
        tiled=True,
    )
    output = (hidden_rows_state + mlp_part).astype(jnp.bfloat16)
    grad_rows = lax.all_gather(cotangent, "tensor", axis=0, tiled=True)
    grad_inner = jnp.einsum("td,fd->tf", grad_rows, w_down, preferred_element_type=jnp.float32)
    grad_gate = (grad_inner * up_proj * sig_gate * (1.0 + gate_pre * (1.0 - sig_gate))).astype(
        jnp.bfloat16
    )
    grad_up = (grad_inner * silu_gate).astype(jnp.bfloat16)
    grad_down_w = jnp.einsum("tf,td->fd", inner_act, grad_rows, preferred_element_type=jnp.float32)
    grad_gate_w = jnp.einsum("td,tf->df", rows_two, grad_gate, preferred_element_type=jnp.float32)
    grad_up_w = jnp.einsum("td,tf->df", rows_two, grad_up, preferred_element_type=jnp.float32)
    first_term = jnp.einsum("tf,df->td", grad_gate, w_gate, preferred_element_type=jnp.float32)
    gradient_feedforward_normed = lax.psum_scatter(
        first_term + jnp.einsum("tf,df->td", grad_up, w_up, preferred_element_type=jnp.float32),
        "tensor",
        scatter_dimension=0,
        tiled=True,
    )
    feedforward_scaled_rows = gradient_feedforward_normed * feedforward_norm_gain
    feedforward_gain_slice = jnp.sum(gradient_feedforward_normed * feedforward_unit_rows, axis=0)
    grad_hidden = cotangent.astype(jnp.float32) + feedforward_inverse_rms * (
        feedforward_scaled_rows
        - feedforward_unit_rows
        * jnp.mean(feedforward_scaled_rows * feedforward_unit_rows, axis=-1, keepdims=True)
    )
    grad_hidden_low = grad_hidden.astype(jnp.bfloat16)
    grad_attn_rows = lax.all_gather(grad_hidden_low, "tensor", axis=0, tiled=True)
    grad_mixed = jnp.einsum(
        "td,ed->te", grad_attn_rows, w_out, preferred_element_type=jnp.float32
    ).reshape(SEG, heads_here, HEAD)
    grad_out_w = jnp.einsum(
        "te,td->ed", mixed_out, grad_attn_rows, preferred_element_type=jnp.float32
    )
    grad_bias_here = (
        jnp.sum(grad_mixed * (memory_read - local_read), axis=(0, 2)) * sig_bias * (1.0 - sig_bias)
    )
    grad_memory_read = mix_w * grad_mixed
    grad_local = ((1.0 - mix_w) * grad_mixed).astype(jnp.bfloat16)

    def attention_back(state_in, inputs):
        grad_key_acc, grad_value_acc = state_in
        begin_row, log_total, grad_block = inputs
        scores, query_block = block_scores(begin_row)
        softmax_w = jnp.exp(scores - log_total[..., None])
        grad_attn = jnp.einsum(
            "thd,shd->hts", grad_block, values, preferred_element_type=jnp.float32
        )
        row_dot = jnp.sum(softmax_w * grad_attn, axis=-1, keepdims=True)
        grad_scores = (softmax_w * (grad_attn - row_dot) * score_scale).astype(jnp.bfloat16)
        grad_query_block = jnp.einsum(
            "hts,shd->thd", grad_scores, key_rows, preferred_element_type=jnp.float32
        )
        grad_key_acc = grad_key_acc + jnp.einsum(
            "hts,thd->shd", grad_scores, query_block, preferred_element_type=jnp.float32
        )
        grad_value_acc = grad_value_acc + jnp.einsum(
            "hts,thd->shd",
            softmax_w.astype(jnp.bfloat16),
            grad_block,
            preferred_element_type=jnp.float32,
        )
        return ((grad_key_acc, grad_value_acc), grad_query_block)

    zero_rows = jnp.zeros((SEG, heads_here, HEAD), jnp.float32)
    (grad_k_local, grad_v_local), grad_q_blocks = lax.scan(
        attention_back,
        (zero_rows, zero_rows),
        (block_begins, log_totals, grad_local.reshape(block_count, block_rows, heads_here, HEAD)),
    )
    grad_q_local = grad_q_blocks.reshape(SEG, heads_here, HEAD)
    local_part = memory_pull((grad_memory_read, zero_memory, zero_norm))
    maps_turned = jnp.swapaxes(seg_maps, 1, 2)
    local_memory_cot = local_part[0]

    def memory_back(turn, state_in):
        memory_send, memory_old = state_in
        memory_recv = shifted(memory_send, "dp", -1)
        return (keep_flag * (apply_map(maps_turned, memory_recv) + local_memory_cot), memory_recv)

    memory_back_state = lax.fori_loop(
        0, chain_turns, memory_back, (keep_flag * local_memory_cot, zero_memory)
    )
    memory_cot = memory_back_state[1]
    norm_part = memory_pull((grad_memory_read, memory_cot, zero_norm))
    norm_base = norm_part[1]

    def norm_back(turn, state_in):
        norm_send, norm_old = state_in
        norm_recv = shifted(norm_send, "dp", -1)
        return (keep_flag * (norm_recv + norm_base), norm_recv)

    norm_back_state = lax.fori_loop(0, chain_turns, norm_back, (keep_flag * norm_base, zero_norm))
    norm_cot = norm_back_state[1]
    grad_phi_q = norm_part[2]
    grad_phi_k = norm_part[3] + norm_cot[None]
    grad_v_mem = norm_part[4]
    grad_queries = (
        (grad_q_local + grad_phi_q * elu_slope(queries_f))
        .astype(jnp.bfloat16)
        .reshape(SEG, heads_here * HEAD)
    )
    grad_keys = (
        (grad_k_local + grad_phi_k * live_rows[:, None, None] * elu_slope(keys_f))
        .astype(jnp.bfloat16)
        .reshape(SEG, heads_here * HEAD)
    )
    grad_values = (grad_v_local + grad_v_mem).astype(jnp.bfloat16).reshape(SEG, heads_here * HEAD)
    grad_query_w = jnp.einsum(
        "td,te->de", rows_one, grad_queries, preferred_element_type=jnp.float32
    )
    grad_key_w = jnp.einsum("td,te->de", rows_one, grad_keys, preferred_element_type=jnp.float32)
    grad_value_w = jnp.einsum(
        "td,te->de", rows_one, grad_values, preferred_element_type=jnp.float32
    )
    summed = jnp.einsum("te,de->td", grad_queries, w_query, preferred_element_type=jnp.float32)
    summed = summed + jnp.einsum("te,de->td", grad_keys, w_key, preferred_element_type=jnp.float32)
    gradient_attention_normed = lax.psum_scatter(
        (
            summed
            + jnp.einsum("te,de->td", grad_values, w_value, preferred_element_type=jnp.float32)
        ).astype(jnp.bfloat16),
        "tensor",
        scatter_dimension=0,
        tiled=True,
    ).astype(jnp.float32)
    attention_scaled_rows = gradient_attention_normed * attention_norm_gain
    attention_gain_slice = jnp.sum(gradient_attention_normed * attention_unit_rows, axis=0)
    grad_tokens = grad_hidden + attention_inverse_rms * (
        attention_scaled_rows
        - attention_unit_rows
        * jnp.mean(attention_scaled_rows * attention_unit_rows, axis=-1, keepdims=True)
    )
    summed_grads = (
        lax.psum_scatter(grad_query_w, "dp", scatter_dimension=0, tiled=True),
        lax.psum_scatter(grad_key_w, "dp", scatter_dimension=0, tiled=True),
        lax.psum_scatter(grad_value_w, "dp", scatter_dimension=0, tiled=True),
        lax.psum_scatter(grad_out_w, "dp", scatter_dimension=1, tiled=True),
        lax.psum_scatter(grad_gate_w, "dp", scatter_dimension=0, tiled=True),
        lax.psum_scatter(grad_up_w, "dp", scatter_dimension=0, tiled=True),
        lax.psum_scatter(grad_down_w, "dp", scatter_dimension=1, tiled=True),
    )
    bias_full = lax.dynamic_update_slice(
        jnp.zeros((HEADS,), jnp.float32), grad_bias_here, (lax.axis_index("tensor") * heads_here,)
    )
    small_sums = lax.psum(
        (attention_gain_slice, feedforward_gain_slice, bias_full), ("dp", "tensor")
    )
    return (
        output,
        grad_tokens,
        small_sums[0],
        summed_grads[0],
        summed_grads[1],
        summed_grads[2],
        summed_grads[3],
        small_sums[2],
        small_sums[1],
        summed_grads[4],
        summed_grads[5],
        summed_grads[6],
    )


def solution(mesh):
    return jax.shard_map(
        body,
        mesh=mesh,
        in_specs=(
            P(("dp", "tensor"), None),
            P(),
            P(None, "tensor"),
            P(None, "tensor"),
            P(None, "tensor"),
            P("tensor", None),
            P("tensor"),
            P(),
            P(None, "tensor"),
            P(None, "tensor"),
            P("tensor", None),
            P("dp"),
            P("dp"),
            P(("dp", "tensor"), None),
        ),
        out_specs=(
            P(("dp", "tensor"), None),
            P(("dp", "tensor"), None),
            P(),
            P("dp", "tensor"),
            P("dp", "tensor"),
            P("dp", "tensor"),
            P("tensor", "dp"),
            P(),
            P(),
            P("dp", "tensor"),
            P("dp", "tensor"),
            P("tensor", "dp"),
        ),
        check_vma=False,
    )
```

profile of v0, /device:TPU:0, one launch (start us, length us, event | category | flops | bytes accessed | tf_op | source)
XLA Modules:
  0.0 3151.7 jit_solution(16120154720771536073)
XLA Ops:
  16.1 58.6 %all-gather.5.cloned.1.call-done = bf16[2048,2048]{1,0:T(8,128)(2,1)} async-done(((bf16[512,2048]{1,0:T(8,128)(2,1)}), bf16[2048,2048]{1,0:T(8,128)(2,1)}) %all-gather.5.cloned.1.call-update) | async-done | bytes 8388624 | tf_op jit(solution)/shard_map/all_gather | solution.py:95
  113.0 45.8 %while.84 = (s32[]{:T(128)}, f32[4,128]{1,0:T(4,128)S(1)}, f32[4,128]{1,0:T(4,128)}, f32[]{:T(128)}, f32[4,128]{1,0:T(4,128)S(1)}) while((s32[]{:T(128)}, f32[4,128]{1,0:T(4,128)S(1)}, f32[4,128]{1,0:T(4,128)}, f32[]{:T(128)}, f32[4,128]{1,0:T(4,128)S(1)}) %tuple.201), condition=%wide.region_3.4_spmd.clone, body=%wide.region_2.3_spmd.sunk.clone | while | flops 1026 | bytes 16489 | solution.py:155
  178.8 177.9 %while.88 = (s32[]{:T(128)}, f32[4,512,4,128]{1,0,3,2:T(4,128)}, f32[4,4,512]{2,1,0:T(4,128)}, s32[4]{0:T(128)S(1)}, s32[]{:T(128)}, /*index=5*/bf16[2048,4,128]...) while((s32[]{:T(128)}, f32[4,512,4,128]{1,0,3,2:T(4,128)}, ...), condition=%wide.region_9.10_spmd.clone.clone.clone, body=%wide.region_6.9_spmd.clone.clone.sunk.clone | while | flops 2199912960 | bytes 72949944 | solution.py:136
  372.3 74.9 %while.85 = (s32[]{:T(128)}, f32[4,128,128]{1,2,0:T(8,128)S(1)}, f32[4,128,128]{1,2,0:T(8,128)}, f32[]{:T(128)}, f32[4,128,128]{2,1,0:T(8,128)S(1)}, /*index=5*/f32[4,128,128]{1,2,0:T(8,128)S(1)}) while((s32[]{:T(128)}, f32[4,128,128]{1,2,0:T(8,128)S(1)}, f32[4,128,128]{1,2,0:T(8,128)}, f32[]{:T(128)}, ...), condition=%wide.region_5.6_spmd.clone, body=%wide.region_4.5_spmd.sunk.clone | while | flops 100794368 | bytes 3670157 | solution.py:165
  467.2 129.1 %reduce-scatter.12.cloned.1.call-done = f32[512,2048]{1,0:T(8,128)} async-done(((f32[2048,2048]{1,0:T(8,128)}), f32[512,2048]{1,0:T(8,128)}) %reduce-scatter.12.cloned.1.call-update) | async-done | bytes 4194320 | tf_op jit(solution)/shard_map/reduce_scatter | solution.py:177
  604.2 57.8 %all-gather.7.cloned.1.call-done = bf16[2048,2048]{1,0:T(8,128)(2,1)} async-done(((bf16[512,2048]{1,0:T(8,128)(2,1)}), bf16[2048,2048]{1,0:T(8,128)(2,1)}) %all-gather.7.cloned.1.call-update) | async-done | bytes 8388624 | tf_op jit(solution)/shard_map/all_gather | solution.py:189
  662.0 24.7 fusion.208
  721.8 36.7 %multiply_convert_fusion.1 = (bf16[2048,2048]{1,0:T(8,128)(2,1)}, bf16[2048,2048]{1,0:T(8,128)(2,1)}, bf16[2048,2048]{1,0:T(8,128)(2,1)}) fusion(f32[2048,2048]{1,0:T(8,128)} %fusion.207, f32[2048,2048]{1,0:T(8,128)} %fusion.208, bf16[2048,2048]{1,0:T(8,128)(2,1)} %all-gather.9.cloned.1.call-done, bf16[2048,2048]{1,0:T(8,128)(2,1)} %param.36), kind=kOutput, calls=%fused_computation.73 | convolution fusion | flops 17242783744 | bytes 75497472 | tf_op jit(solution)/shard_map/td,fd->tf/dot_general | solution.py:203
  782.9 26.5 convolution_add_fusion.1
  809.5 126.2 %reduce-scatter.16.cloned.1.call-done = f32[512,2048]{1,0:T(8,128)} async-done(((f32[2048,2048]{1,0:T(8,128)}), f32[512,2048]{1,0:T(8,128)}) %reduce-scatter.16.cloned.1.call-update) | async-done | bytes 4194320 | tf_op jit(solution)/shard_map/reduce_scatter | solution.py:212
  965.8 38.5 %all-gather.11.cloned.1.call-done = bf16[2048,2048]{1,0:T(8,128)(2,1)} async-done(((bf16[512,2048]{1,0:T(8,128)(2,1)}), bf16[2048,2048]{1,0:T(8,128)(2,1)}) %all-gather.11.cloned.1.call-update) | async-done | bytes 8388624 | tf_op jit(solution)/shard_map/all_gather | solution.py:226
  1052.1 457.6 %while.89 = (s32[]{:T(128)}, f32[2048,4,128]{0,2,1:T(8,128)}, f32[2048,4,128]{0,2,1:T(8,128)}, f32[4,512,4,128]{1,0,3,2:T(4,128)}, s32[4]{0:T(128)S(1)}, /*index...) while((s32[]{:T(128)}, f32[2048,4,128]{0,2,1:T(8,128)}, ...), condition=%wide.region_17.18_spmd.clone.clone.clone, body=%wide.region_15.17_spmd.clone.clone.sunk.clone | while | flops 5484063232 | bytes 203481360 | solution.py:264
  1086.8 26.6 fusion.361
  1113.4 28.2 bitcast_add_fusion.9
  1200.5 26.6 fusion.361
  1227.1 29.4 bitcast_add_fusion.9
  1315.4 26.6 fusion.361
  1341.9 29.4 bitcast_add_fusion.9
  1430.2 26.6 fusion.361
  1456.8 29.4 bitcast_add_fusion.9
  1527.1 71.3 %while.86 = (s32[]{:T(128)}, f32[4,128,128]{2,1,0:T(8,128)S(1)}, f32[4,128,128]{2,1,0:T(8,128)}, f32[]{:T(128)}, f32[4,128,128]{2,1,0:T(8,128)S(1)}, /*index=5*/f32[4,128,128]{2,1,0:T(8,128)S(1)}) while((s32[]{:T(128)}, f32[4,128,128]{2,1,0:T(8,128)S(1)}, f32[4,128,128]{2,1,0:T(8,128)}, f32[]{:T(128)}, ...), condition=%wide.region_20.21_spmd.clone, body=%wide.region_19.20_spmd.sunk.clone | while | flops 100794368 | bytes 3145869 | solution.py:279
  1629.7 49.0 %while.87 = (s32[]{:T(128)}, f32[4,128]{1,0:T(4,128)S(1)}, f32[4,128]{1,0:T(4,128)}, f32[]{:T(128)}, f32[4,128]{1,0:T(4,128)S(1)}) while((s32[]{:T(128)}, f32[4,128]{1,0:T(4,128)S(1)}, f32[4,128]{1,0:T(4,128)}, f32[]{:T(128)}, f32[4,128]{1,0:T(4,128)S(1)}) %tuple.161), condition=%wide.region_23.24_spmd.clone, body=%wide.region_22.23_spmd.sunk.clone | while | flops 1026 | bytes 22661 | solution.py:291
  1763.6 24.8 fusion.219
  1788.5 24.8 fusion.218
  1861.7 41.5 %all-reduce = (f32[2048]{0:T(1024)}, f32[16]{0:T(128)}, f32[2048]{0:T(1024)}) all-reduce(f32[2048]{0:T(1024)S(1)} %get-tuple-element.392, f32[16]{0:T(128)S(1)} %multiply_dynamic-update-slice_fusion, f32[2048]{0:T(1024)S(1)} %copy-done.55), channel_id=1, replica_groups=mesh['dp'=8,'tensor'=4] {'dp','tensor'}, use_global_device_ids=true, to_apply=%region_27.28 | all-reduce | flops 4112 | bytes 32896 | tf_op jit(solution)/shard_map/psum | solution.py:344
  1927.6 276.8 %reduce-scatter.32.cloned.1.call-done = f32[2048,256]{1,0:T(8,128)} async-done(((f32[2048,2048]{1,0:T(8,128)}), f32[2048,256]{1,0:T(8,128)}) %reduce-scatter.32.cloned.1.call-update) | async-done | bytes 2097168 | tf_op jit(solution)/shard_map/reduce_scatter | solution.py:339
  2204.4 286.3 %reduce-scatter.30.cloned.1.call-done = f32[256,2048]{1,0:T(8,128)} async-done(((f32[2048,2048]{1,0:T(8,128)}), f32[256,2048]{1,0:T(8,128)}) %reduce-scatter.30.cloned.1.call-update) | async-done | bytes 2097168 | tf_op jit(solution)/shard_map/reduce_scatter | solution.py:338
  2490.7 286.1 %reduce-scatter.28.cloned.1.call-done = f32[256,2048]{1,0:T(8,128)} async-done(((f32[2048,2048]{1,0:T(8,128)}), f32[256,2048]{1,0:T(8,128)}) %reduce-scatter.28.cloned.1.call-update) | async-done | bytes 2097168 | tf_op jit(solution)/shard_map/reduce_scatter | solution.py:337
  2776.8 92.0 %reduce-scatter.26.cloned.1.call-done = f32[512,256]{1,0:T(8,128)} async-done(((f32[512,2048]{1,0:T(8,128)}), f32[512,256]{1,0:T(8,128)}) %reduce-scatter.26.cloned.1.call-update) | async-done | bytes 524304 | tf_op jit(solution)/shard_map/reduce_scatter | solution.py:336
  2868.9 92.0 %reduce-scatter.22.cloned.1.call-done = f32[256,512]{1,0:T(8,128)} async-done(((f32[2048,512]{1,0:T(8,128)}), f32[256,512]{1,0:T(8,128)}) %reduce-scatter.22.cloned.1.call-update) | async-done | bytes 524304 | tf_op jit(solution)/shard_map/reduce_scatter | solution.py:334
  2960.9 92.2 %reduce-scatter.20.cloned.1.call-done = f32[256,512]{1,0:T(8,128)} async-done(((f32[2048,512]{1,0:T(8,128)}), f32[256,512]{1,0:T(8,128)}) %reduce-scatter.20.cloned.1.call-update) | async-done | bytes 524304 | tf_op jit(solution)/shard_map/reduce_scatter | solution.py:333
  3053.1 91.9 %reduce-scatter.24.cloned.1.call-done = f32[256,512]{1,0:T(8,128)} async-done(((f32[2048,512]{1,0:T(8,128)}), f32[256,512]{1,0:T(8,128)}) %reduce-scatter.24.cloned.1.call-update) | async-done | bytes 524304 | tf_op jit(solution)/shard_map/reduce_scatter | solution.py:335
  (493 shorter events, 1089.2 us)
Async XLA Ops:
  7.2 67.4 %all-gather.5.cloned.1.call-start = ((), (), s32[]{:S(2)}) async-start(), calls=%async_computation.11 | async-start | bytes 10485760 | tf_op jit(solution)/shard_map/all_gather | solution.py:95
  13.5 582.8 %reduce-scatter.12.cloned.1.call-start = ((), (), s32[]{:S(2)}) async-start(), calls=%async_computation.12 | async-start | bytes 20971520 | tf_op jit(solution)/shard_map/reduce_scatter | solution.py:177
  137.5 6.4 collective-permute-start
  144.4 6.4 collective-permute-start
  372.3 11.7 collective-permute-start.1
  384.7 11.0 collective-permute-start.1
  396.4 10.3 collective-permute-start.1
  407.4 9.3 collective-permute-start.1
  417.5 9.2 collective-permute-start.1
  427.4 9.2 collective-permute-start.1
  437.3 9.2 collective-permute-start.1
  467.2 194.9 %all-gather.7.cloned.1.call-start = ((), (), s32[]{:S(2)}) async-start(), calls=%async_computation.13 | async-start | bytes 10485760 | tf_op jit(solution)/shard_map/all_gather | solution.py:189
  603.6 118.3 %all-gather.9.cloned.1.call-start = ((), (), s32[]{:S(2)}) async-start(), calls=%async_computation.15 | async-start | bytes 10485760 | tf_op jit(solution)/shard_map/all_gather | solution.py:202
  604.2 331.6 %reduce-scatter.16.cloned.1.call-start = ((), (), s32[]{:S(2)}) async-start(), calls=%async_computation.16 | async-start | bytes 20971520 | tf_op jit(solution)/shard_map/reduce_scatter | solution.py:212
  809.5 194.8 %all-gather.11.cloned.1.call-start = ((), (), s32[]{:S(2)}) async-start(), calls=%async_computation.17 | async-start | bytes 10485760 | tf_op jit(solution)/shard_map/all_gather | solution.py:226
  945.8 912.2 %reduce-scatter.18.cloned.1.call-start = ((), (), s32[]{:S(2)}) async-start(), calls=%async_computation.18 | async-start | bytes 10485760 | tf_op jit(solution)/shard_map/reduce_scatter | solution.py:316
  1527.1 10.4 collective-permute-start.2
  1538.2 10.2 collective-permute-start.2
  1549.1 9.5 collective-permute-start.2
  1559.3 8.9 collective-permute-start.2
  1568.9 9.2 collective-permute-start.2
  1578.7 9.2 collective-permute-start.2
  1588.6 9.2 collective-permute-start.2
  1629.7 6.4 collective-permute-start.3
  1714.6 202.7 %reduce-scatter.14.cloned.1.call-start = ((), (), s32[]{:S(2)}) async-start(), calls=%async_computation.14 | async-start | bytes 20971520 | tf_op jit(solution)/shard_map/reduce_scatter | solution.py:195
  1739.1 465.3 %reduce-scatter.32.cloned.1.call-start = ((), (), s32[]{:S(2)}) async-start(), calls=%async_computation.25 | async-start | bytes 18874368 | tf_op jit(solution)/shard_map/reduce_scatter | solution.py:339
  1763.6 727.1 %reduce-scatter.30.cloned.1.call-start = ((), (), s32[]{:S(2)}) async-start(), calls=%async_computation.24 | async-start | bytes 18874368 | tf_op jit(solution)/shard_map/reduce_scatter | solution.py:338
  1788.5 988.3 %reduce-scatter.28.cloned.1.call-start = ((), (), s32[]{:S(2)}) async-start(), calls=%async_computation.23 | async-start | bytes 18874368 | tf_op jit(solution)/shard_map/reduce_scatter | solution.py:337
  1813.3 1055.5 %reduce-scatter.26.cloned.1.call-start = ((), (), s32[]{:S(2)}) async-start(), calls=%async_computation.22 | async-start | bytes 4718592 | tf_op jit(solution)/shard_map/reduce_scatter | solution.py:336
  1824.4 1136.5 %reduce-scatter.22.cloned.1.call-start = ((), (), s32[]{:S(2)}) async-start(), calls=%async_computation.20 | async-start | bytes 4718592 | tf_op jit(solution)/shard_map/reduce_scatter | solution.py:334
  1835.4 1217.7 %reduce-scatter.20.cloned.1.call-start = ((), (), s32[]{:S(2)}) async-start(), calls=%async_computation.19 | async-start | bytes 4718592 | tf_op jit(solution)/shard_map/reduce_scatter | solution.py:333
  1846.3 1298.7 %reduce-scatter.24.cloned.1.call-start = ((), (), s32[]{:S(2)}) async-start(), calls=%async_computation.21 | async-start | bytes 4718592 | tf_op jit(solution)/shard_map/reduce_scatter | solution.py:335
  (116 other events, 1745.8 us)
Sparse Core Ops, SparseCore 0:
  13.6 60.9 all-gather.4
  467.3 129.0 reduce-scatter.11
  603.7 58.2 all-gather.6
  663.5 58.2 all-gather.8
  809.6 126.1 reduce-scatter.15
  946.0 58.2 all-gather.10
  1714.7 72.2 reduce-scatter.17
  1789.8 127.5 reduce-scatter.13
  1921.7 282.6 reduce-scatter.31
  2209.1 281.6 reduce-scatter.29
  2495.1 281.6 reduce-scatter.27
  2781.3 87.5 reduce-scatter.25
  2873.1 87.7 reduce-scatter.21
  2965.4 87.6 reduce-scatter.19
  3057.2 87.7 reduce-scatter.23
where the time goes:
time: 3160 us; the launch traced here: 3150 us
  waiting for transfers between devices  1790 us (57%)
  matrix products  858 us (27%)
  local copies, waits for them, and re-layouts  251 us (8%)
  other arithmetic  90.2 us (3%)
  starting transfers between devices  88 us (3%)
  blocking collectives  41.5 us (1%)
    reduce_scatter x1, waiting for transfers between devices, body(): lax.psum_scatter(grad_up_w, 'dp', scatter_dimension=0, tiled=True)  286 us
    reduce_scatter x1, waiting for transfers between devices, body(): lax.psum_scatter(grad_gate_w, 'dp', scatter_dimension=0, tiled=True)  286 us
    reduce_scatter x1, waiting for transfers between devices, body(): lax.psum_scatter(grad_down_w, 'dp', scatter_dimension=1, tiled=True)  277 us
    dynamic_update_slice x16, local copies, waits for them, and re-layouts, body(): local_blocks, log_totals = lax.map(attend_block, block_begins)  187 us
    ppermute x28, waiting for transfers between devices, shifted(): lax.ppermute(value, axis, [(source, source + steps) for source in range(l...  135 us
    reduce_scatter x1, waiting for transfers between devices, body(): lax.psum_scatter(jnp.dot(mixed_out, w_out, preferred_element_type=jnp.flo...  129 us
    reduce_scatter x1, waiting for transfers between devices, body(): lax.psum_scatter(first_term + jnp.einsum('tf,df->td', grad_up, w_up, pref...  126 us
    dot_general x4, matrix products, attention_back(): jnp.einsum('hts,thd->shd', grad_scores, query_block, preferred_element_ty...  116 us
  transfers between devices with their start and end apart: 43, of which 42 were waited for; matrix products, arithmetic and copies ran while one was open for 7% of the time, Pallas kernels for 0%

commit v1 on v0

v1 whole, which is shorter than its diff:
```python
import jax
import jax.numpy as jnp
from jax import lax
from jax.experimental import pallas as pl
from jax.experimental.pallas import tpu as pltpu
from jax.sharding import PartitionSpec as P

HEADS = 16
HEAD = 128
EPSILON = 1e-06
BF = jnp.bfloat16
F32 = jnp.float32
LOG2E = 1.4426950408889634
NEG = -1e30
VMEM_BYTES = 56 << 20


def dot(a, b):
    return jnp.dot(a, b, preferred_element_type=F32)


def dot_nt(a, b):
    return lax.dot_general(a, b, (((1,), (1,)), ((), ())), preferred_element_type=F32)


def dot_tn(a, b):
    return lax.dot_general(a, b, (((0,), (0,)), ((), ())), preferred_element_type=F32)


def shape(dims, dtype):
    return jax.ShapeDtypeStruct(dims, dtype)


def call(kernel, out_shape, grid, in_specs, out_specs, cost, scratch=(), alias=None):
    return pl.pallas_call(
        kernel,
        out_shape=out_shape,
        grid_spec=pltpu.PrefetchScalarGridSpec(
            num_scalar_prefetch=1,
            grid=grid,
            in_specs=in_specs,
            out_specs=out_specs,
            scratch_shapes=list(scratch),
        ),
        input_output_aliases=alias or {},
        compiler_params=pltpu.CompilerParams(
            dimension_semantics=("arbitrary",) * len(grid), vmem_limit_bytes=VMEM_BYTES
        ),
        cost_estimate=pl.CostEstimate(
            flops=int(cost[0]), bytes_accessed=int(cost[1]), transcendentals=0
        ),
    )


def whole(dims):
    return pl.BlockSpec(dims, lambda *_: (0,) * len(dims), pipeline_mode=pl.Buffered(1))


def exp_low(values):
    return jnp.exp(jnp.minimum(values, 0.0))


def phi_of(values, low):
    return jnp.where(values > 0, values + 1.0, low)


def row_ids(count, begin):
    return begin + lax.broadcasted_iota(jnp.int32, (count, 1), 0)


CHIP, CORE, PLACE, VALID, ORDER = 0, 1, 2, 3, 4


def chip_block(s, j, chips):
    return lax.rem(s[CHIP] + j, chips)


def qkv_call(sc, j, chips, xa, xb, wq, wk, wv, prev):
    R, D = xa.shape
    E = wq.shape[1]
    T = 2 * R * chips
    n = min(256, E)

    def kernel(s, xa_ref, xb_ref, wq_ref, wk_ref, wv_ref, *rest):
        q_ref, k_ref, v_ref, c_ref = rest[-4:]
        base = chip_block(s, j, chips) * 2 * R
        sums = jnp.zeros((1, n), F32)
        for i, x_ref in enumerate((xa_ref, xb_ref)):
            off = pl.multiple_of((s[CORE] if i == 0 else 1 - s[CORE]) * R, R)
            rows = pl.ds(off, R)
            x = x_ref[...]
            q_ref[rows] = dot(x, wq_ref[...]).astype(BF)
            v_ref[rows] = dot(x, wv_ref[...]).astype(BF)
            k = dot(x, wk_ref[...]).astype(BF)
            k_ref[rows] = k
            k = k.astype(F32)
            phi = jnp.where(row_ids(R, base + off) < s[VALID], phi_of(k, exp_low(k)), 0.0)
            sums = sums + jnp.sum(phi, axis=0, keepdims=True)
        c_ref[...] = sums

    rows = pl.BlockSpec((R, D), lambda c, s: (0, 0))
    cols = pl.BlockSpec((D, n), lambda c, s: (0, c))
    out = pl.BlockSpec((2 * R, n), lambda c, s: (chip_block(s, j, chips), c))
    o = shape((T, E), BF)
    extra = [pl.BlockSpec(memory_space=pl.ANY)] * 3 if prev else []
    return call(
        kernel,
        (o, o, o, shape((1, E), F32)),
        (E // n,),
        [rows, rows, cols, cols, cols] + extra,
        [out, out, out, pl.BlockSpec((1, n), lambda c, s: (0, c))],
        (12 * R * D * E, 4 * R * D + 6 * D * E + 12 * R * E),
        alias={6: 0, 7: 1, 8: 2} if prev else None,
    )(sc, xa, xb, wq, wk, wv, *(prev or ()))


def grad_inner_call(sc, ca, cb, wd):
    R, D = ca.shape
    F = wd.shape[0]
    n = min(512, F)

    def kernel(s, ca_ref, cb_ref, w_ref, o_ref):
        o_ref[:R] = dot_nt(ca_ref[...], w_ref[...]).astype(BF)
        o_ref[R:] = dot_nt(cb_ref[...], w_ref[...]).astype(BF)

    rows = pl.BlockSpec((R, D), lambda c, s: (0, 0))
    return call(
        kernel,
        shape((2 * R, F), BF),
        (F // n,),
        [rows, rows, pl.BlockSpec((n, D), lambda c, s: (c, 0))],
        pl.BlockSpec((2 * R, n), lambda c, s: (0, c)),
        (4 * R * D * F, 4 * R * D + 2 * D * F + 4 * R * F),
    )(sc, ca, cb, wd)


def ffn_a_call(sc, xa, xb, wg, wu, gi):
    R, D = xa.shape
    F = wg.shape[1]
    n = min(512, F)

    def kernel(s, xa_ref, xb_ref, wg_ref, wu_ref, gi_ref, inner_ref, gg_ref, gu_ref):
        for i, x_ref in enumerate((xa_ref, xb_ref)):
            rows = slice(i * R, (i + 1) * R)
            g = dot(x_ref[...], wg_ref[...])
            u = dot(x_ref[...], wu_ref[...])
            sig = 0.5 * jnp.tanh(0.5 * g) + 0.5
            silu = g * sig
            inner_ref[rows] = (silu * u).astype(BF)
            gi_rows = gi_ref[rows].astype(F32)
            gu_ref[rows] = (gi_rows * silu).astype(BF)
            gg_ref[rows] = (gi_rows * u * (sig + silu * (1.0 - sig))).astype(BF)

    o = shape((2 * R, F), BF)
    rows = pl.BlockSpec((R, D), lambda c, s: (0, 0))
    cols = pl.BlockSpec((D, n), lambda c, s: (0, c))
    out = pl.BlockSpec((2 * R, n), lambda c, s: (0, c))
    return call(
        kernel,
        (o, o, o),
        (F // n,),
        [rows, rows, cols, cols, out],
        [out, out, out],
        (8 * R * D * F, 4 * R * D + 4 * D * F + 16 * R * F),
    )(sc, xa, xb, wg, wu, gi)


def ffn_b_call(sc, gg, gu, wg, wu):
    R2, F = gg.shape
    R = R2 // 2
    D = wg.shape[0]
    n = min(512, D)

    def kernel(s, gg_ref, gu_ref, wg_ref, wu_ref, oa_ref, ob_ref):
        for i, o_ref in enumerate((oa_ref, ob_ref)):
            rows = slice(i * R, (i + 1) * R)
            o_ref[...] = (
                dot_nt(gg_ref[rows], wg_ref[...]) + dot_nt(gu_ref[rows], wu_ref[...])
            ).astype(BF)

    o = shape((R, D), BF)
    rows = pl.BlockSpec((R2, F), lambda c, s: (0, 0))
    cols = pl.BlockSpec((n, F), lambda c, s: (c, 0))
    out = pl.BlockSpec((R, n), lambda c, s: (0, c))
    return call(
        kernel,
        (o, o),
        (D // n,),
        [rows, rows, cols, cols],
        [out, out],
        (8 * R * D * F, 8 * R * F + 4 * D * F + 4 * R * D),
    )(sc, gg, gu, wg, wu)


def down_call(sc, inner, wd):
    R2, F = inner.shape
    R = R2 // 2
    D = wd.shape[1]
    n = min(512, D)

    def kernel(s, x_ref, w_ref, oa_ref, ob_ref):
        oa_ref[...] = dot(x_ref[:R], w_ref[...]).astype(BF)
        ob_ref[...] = dot(x_ref[R:], w_ref[...]).astype(BF)

    o = shape((R, D), BF)
    out = pl.BlockSpec((R, n), lambda c, s: (0, c))
    return call(
        kernel,
        (o, o),
        (D // n,),
        [pl.BlockSpec((R2, F), lambda c, s: (0, 0)), pl.BlockSpec((F, n), lambda c, s: (0, c))],
        [out, out],
        (4 * R * D * F, 4 * R * F + 2 * D * F + 4 * R * D),
    )(sc, inner, wd)


def wgrad_call(sc, xs, gs, ndp):
    R, D = xs[0].shape
    nx = len(xs)
    C = D // ndp
    nb = len(gs[0])
    widths = [blocks[0].shape[1] for blocks in gs]
    T = R * nx
    rb = T // nb
    N = sum(widths)

    def kernel(s, *refs):
        x_refs, g_refs, (o_ref, xt) = refs[:nx], refs[nx:-2], refs[-2:]
        for p in range(nx):
            xt[:, p * R : (p + 1) * R] = x_refs[p][...].T
        at = 0
        for w, width in enumerate(widths):
            acc = None
            for b in range(nb):
                term = dot(xt[:, b * rb : (b + 1) * rb], g_refs[w * nb + b][...])
                acc = term if acc is None else acc + term
            o_ref[0, :, at : at + width] = acc.astype(BF)
            at += width

    flat = [g for blocks in gs for g in blocks]
    return call(
        kernel,
        shape((ndp, C, N), BF),
        (ndp,),
        [pl.BlockSpec((R, C), lambda j, s: (0, s[ORDER + j]))] * nx + [whole(g.shape) for g in flat],
        pl.BlockSpec((1, C, N), lambda j, s: (j, 0, 0)),
        (2 * T * D * N, 2 * T * (D + N) + 2 * D * N),
        scratch=[pltpu.VMEM((C, T), BF)],
    )(sc, *xs, *flat)


def attn_fwd_call(sc, q, k, v):
    T, E = q.shape
    hh = E // HEAD
    B = min(512, T)
    nb = T // B
    c = HEAD**-0.5 * LOG2E

    def kernel(s, q_ref, k_ref, v_ref, o_ref, lse_ref):
        valid = s[VALID]
        for i in range(nb):
            qb = q_ref[i * B : (i + 1) * B]
            parts = []
            for j in range(i + 1):
                x = dot_nt(k_ref[j * B : (j + 1) * B], qb)
                if j == i:
                    u = lax.broadcasted_iota(jnp.int32, (B, B), 0)
                    t = lax.broadcasted_iota(jnp.int32, (B, B), 1)
                    x = jnp.where(u <= t, x, NEG)
                if (j + 1) * B > T // 2:
                    x = jnp.where(row_ids(B, j * B) < valid, x, NEG)
                parts.append(x)
            top = jnp.max(parts[0], axis=0, keepdims=True)
            for x in parts[1:]:
                top = jnp.maximum(top, jnp.max(x, axis=0, keepdims=True))
            top = top * c
            total = jnp.zeros((1, B), F32)
            acc = jnp.zeros((HEAD, B), F32)
            for j, x in enumerate(parts):
                p = jnp.exp2(x * c - top)
                total = total + jnp.sum(p, axis=0, keepdims=True)
                acc = acc + dot_tn(v_ref[j * B : (j + 1) * B], p.astype(BF))
            o_ref[i * B : (i + 1) * B] = (acc * (1.0 / total)).T
            lse_ref[0, :, i * B : (i + 1) * B] = top + jnp.log2(total)

    head = pl.BlockSpec((T, HEAD), lambda h, s: (0, h))
    return call(
        kernel,
        (shape((T, E), F32), shape((hh, 1, T), F32)),
        (hh,),
        [head, head, head],
        [head, pl.BlockSpec((1, 1, T), lambda h, s: (h, 0, 0))],
        (6 * T * T * E, 10 * T * E),
    )(sc, q, k, v)


def attn_bwd_call(sc, q, k, v, do, lo, lse, h0, nh):
    T = q.shape[0]
    B = min(512, T)
    nb = T // B
    scale = HEAD**-0.5
    c = scale * LOG2E

    def kernel(s, q_ref, k_ref, v_ref, do_ref, lo_ref, lse_ref, dq_ref, dk_ref, dv_ref, delta):
        valid = s[VALID]
        ones = jnp.ones((8, HEAD), F32)
        for i in range(nb):
            rows = slice(i * B, (i + 1) * B)
            prod = do_ref[rows].astype(F32) * lo_ref[rows]
            delta[:, rows] = lax.dot_general(
                ones,
                prod,
                (((1,), (1,)), ((), ())),
                precision=lax.Precision.HIGHEST,
                preferred_element_type=F32,
            )
        dq_ref[...] = jnp.zeros_like(dq_ref)
        for j in range(nb):
            kb = k_ref[j * B : (j + 1) * B]
            vb = v_ref[j * B : (j + 1) * B]
            dk = jnp.zeros((B, HEAD), F32)
            dv = jnp.zeros((B, HEAD), F32)
            for i in range(j, nb):
                rows = slice(i * B, (i + 1) * B)
                qb = q_ref[rows]
                dob = do_ref[rows]
                p = jnp.exp2(dot_nt(kb, qb) * c - lse_ref[0, :, rows])
                if i == j:
                    u = lax.broadcasted_iota(jnp.int32, (B, B), 0)
                    t = lax.broadcasted_iota(jnp.int32, (B, B), 1)
                    p = jnp.where(u <= t, p, 0.0)
                if (j + 1) * B > T // 2:
                    p = jnp.where(row_ids(B, j * B) < valid, p, 0.0)
                ds = (p * (dot_nt(vb, dob) - delta[0:1, rows])).astype(BF)
                dv = dv + dot(p.astype(BF), dob)
                dk = dk + dot(ds, qb)
                dq_ref[rows] += dot_tn(ds, kb)
            dk_ref[j * B : (j + 1) * B] = dk * scale
            dv_ref[j * B : (j + 1) * B] = dv
        dq_ref[...] *= scale

    o = shape((T, nh * HEAD), F32)
    head = pl.BlockSpec((T, HEAD), lambda h, s: (0, h0 + h))
    out = pl.BlockSpec((T, HEAD), lambda h, s: (0, h))
    return call(
        kernel,
        (o, o, o),
        (nh,),
        [head] * 5 + [pl.BlockSpec((1, 1, T), lambda h, s: (h0 + h, 0, 0))],
        [out, out, out],
        (12 * T * T * HEAD * nh, 26 * T * HEAD * nh),
        scratch=[pltpu.VMEM((8, T), F32)],
    )(sc, q, k, v, do, lo, lse)


def maps_call(sc, k, v, gathered):
    T, E = k.shape
    hh = E // HEAD
    ndp = gathered.shape[0]

    def kernel(s, k_ref, v_ref, g_ref, maps_ref, norm_ref):
        h = pl.program_id(0)
        norm = jnp.zeros((1, HEAD), F32)
        for a in range(ndp - 1):
            after = (norm + g_ref[a, pl.ds(h, 1)]) * g_ref[a + 1, hh : hh + 1]
            norm = jnp.where(a < s[PLACE], after, norm)
        norm_ref[0] = norm
        k = k_ref[...].astype(F32)
        phi = jnp.where(row_ids(T, 0) < s[VALID], phi_of(k, exp_low(k)), 0.0)
        den = jnp.maximum(jnp.sum(phi * norm, axis=1, keepdims=True), 1.0)
        low = phi.astype(BF)
        maps_ref[0, 0] = dot_tn((phi * (1.0 / den)).astype(BF), low).astype(BF)
        maps_ref[1, 0] = dot_tn(low, v_ref[...]).astype(BF)

    head = pl.BlockSpec((T, HEAD), lambda h, s: (0, h))
    return call(
        kernel,
        (shape((2, hh, HEAD, HEAD), BF), shape((hh, 1, HEAD), F32)),
        (hh,),
        [head, head, whole(gathered.shape)],
        [
            pl.BlockSpec((2, 1, HEAD, HEAD), lambda h, s: (0, h, 0, 0)),
            pl.BlockSpec((1, 1, HEAD), lambda h, s: (h, 0, 0)),
        ],
        (4 * T * E * HEAD, 4 * T * E),
    )(sc, k, v, gathered)


def times_state(g, state):
    high = state.astype(BF)
    return dot(g, high) + dot(g, (state - high.astype(F32)).astype(BF))


def chain_call(sc, gathered, maps):
    ndp, _, hh = maps.shape[:3]

    def kernel(s, g_ref, maps_ref, m_ref):
        state = [jnp.zeros((HEAD, HEAD), F32) for _ in range(hh)]
        for a in range(ndp - 1):
            keep = g_ref[a + 1, hh : hh + 1]
            before = a < s[PLACE]
            for h in range(hh):
                after = state[h] - times_state(maps_ref[a, 0, h], state[h])
                after = (after + maps_ref[a, 1, h].astype(F32)) * keep
                state[h] = jnp.where(before, after, state[h])
        for h in range(hh):
            m_ref[h] = state[h]

    return call(
        kernel,
        shape((hh, HEAD, HEAD), F32),
        (1,),
        [whole(gathered.shape), whole(maps.shape)],
        whole((hh, HEAD, HEAD)),
        (4e8, 2 * maps.size),
    )(sc, gathered, maps)


def mixout_call(sc, j, chips, q, local, memory, norm, mix, wo):
    T, E = q.shape
    hh = E // HEAD
    D = wo.shape[1]
    R = T // chips // 2
    n = min(512, D)

    def kernel(s, q_ref, l_ref, m_ref, n_ref, mix_ref, w_ref, oa_ref, ob_ref, mixed_ref, diff_ref):
        @pl.when(pl.program_id(0) == 0)
        def _():
            for i in range(2):
                off = pl.multiple_of((s[CORE] if i == 0 else 1 - s[CORE]) * R, R)
                for h in range(hh):
                    cols = slice(h * HEAD, (h + 1) * HEAD)
                    qv = q_ref[pl.ds(off, R), cols].astype(F32)
                    phi = phi_of(qv, exp_low(qv))
                    den = jnp.maximum(jnp.sum(phi * n_ref[h], axis=1, keepdims=True), 1.0)
                    read = dot(phi.astype(BF), m_ref[h].astype(BF)) * (1.0 / den)
                    diff = read - l_ref[pl.ds(off, R), cols]
                    mixed = l_ref[pl.ds(off, R), cols] + mix_ref[h] * diff
                    diff_ref[i * R : (i + 1) * R, cols] = diff.astype(BF)
                    mixed_ref[i * R : (i + 1) * R, cols] = mixed.astype(BF)

        oa_ref[...] = dot(mixed_ref[:R], w_ref[...]).astype(BF)
        ob_ref[...] = dot(mixed_ref[R:], w_ref[...]).astype(BF)

    rows = pl.BlockSpec((2 * R, E), lambda c, s: (chip_block(s, j, chips), 0))
    out = pl.BlockSpec((R, n), lambda c, s: (0, c))
    rel = pl.BlockSpec((2 * R, E), lambda c, s: (0, 0))
    return call(
        kernel,
        (shape((R, D), BF), shape((R, D), BF), shape((2 * R, E), BF), shape((2 * R, E), BF)),
        (D // n,),
        [rows, rows, whole(memory.shape), whole(norm.shape), whole(mix.shape), pl.BlockSpec((E, n), lambda c, s: (0, c))],
        [out, out, rel, rel],
        (4 * R * E * D + 8 * R * E * HEAD, 20 * R * E + 2 * E * D + 4 * R * D),
    )(sc, q, local, memory, norm, mix, wo)


def gradmix_call(sc, j, chips, ya, yb, wo, diff, q, norm, mix, prev):
    R, D = ya.shape
    E = wo.shape[0]
    hh = E // HEAD
    T = 2 * R * chips
    n = min(256, E)
    per = n // HEAD

    def kernel(s, ya_ref, yb_ref, w_ref, diff_ref, q_ref, n_ref, mix_ref, *rest):
        do_ref, gm_ref, cot_ref, b_ref = rest[-4:]
        sums = jnp.zeros((1, n), F32)
        cots = [jnp.zeros((HEAD, HEAD), F32) for _ in range(per)]
        for i, y_ref in enumerate((ya_ref, yb_ref)):
            off = pl.multiple_of((s[CORE] if i == 0 else 1 - s[CORE]) * R, R)
            grad = dot_nt(y_ref[...], w_ref[...])
            sums = sums + jnp.sum(grad * diff_ref[i * R : (i + 1) * R].astype(F32), axis=0, keepdims=True)
            for h in range(per):
                cols = slice(h * HEAD, (h + 1) * HEAD)
                part = grad[:, cols]
                grad_read = part * mix_ref[h]
                do_ref[pl.ds(off, R), cols] = (part - grad_read).astype(BF)
                gm_ref[pl.ds(off, R), cols] = grad_read.astype(BF)
                qv = q_ref[pl.ds(off, R), cols].astype(F32)
                phi = phi_of(qv, exp_low(qv))
                den = jnp.maximum(jnp.sum(phi * n_ref[h], axis=1, keepdims=True), 1.0)
                cots[h] = cots[h] + dot_tn(phi.astype(BF), (grad_read * (1.0 / den)).astype(BF))
        for h in range(per):
            cot_ref[h] = cots[h]
        b_ref[...] = sums

    rows = pl.BlockSpec((R, D), lambda c, s: (0, 0))
    place = pl.BlockSpec((2 * R, n), lambda c, s: (chip_block(s, j, chips), c))
    per_head = pl.BlockSpec((per, 1, HEAD), lambda c, s: (c, 0, 0))
    o = shape((T, E), BF)
    extra = [pl.BlockSpec(memory_space=pl.ANY)] * 2 if prev else []
    return call(
        kernel,
        (o, o, shape((hh, HEAD, HEAD), F32), shape((1, E), F32)),
        (E // n,),
        [rows, rows, pl.BlockSpec((n, D), lambda c, s: (c, 0)), pl.BlockSpec((2 * R, n), lambda c, s: (0, c)), place, per_head, per_head] + extra,
        [place, place, pl.BlockSpec((per, HEAD, HEAD), lambda c, s: (c, 0, 0)), pl.BlockSpec((1, n), lambda c, s: (0, c))],
        (4 * R * E * D + 4 * R * E * HEAD, 4 * R * D + 2 * E * D + 16 * R * E),
        alias={8: 0, 9: 1} if prev else None,
    )(sc, ya, yb, wo, diff, q, norm, mix, *(prev or ()))


def memory_rows(q, k, grad_read, live, memory, norm, cot):
    low_q = exp_low(q)
    low_k = exp_low(k)
    phi_q = phi_of(q, low_q)
    phi_k = jnp.where(live, phi_of(k, low_k), 0.0)
    raw_q = jnp.sum(phi_q * norm, axis=1, keepdims=True)
    raw_k = jnp.sum(phi_k * norm, axis=1, keepdims=True)
    inv_q = 1.0 / jnp.maximum(raw_q, 1.0)
    inv_k = 1.0 / jnp.maximum(raw_k, 1.0)
    read = dot(phi_q.astype(BF), memory)
    recalled = dot(phi_k.astype(BF), memory) * inv_k
    pushed = dot(phi_k.astype(BF), cot)
    scaled = grad_read * inv_q
    w_q = jnp.where(raw_q > 1.0, -jnp.sum(scaled * read, axis=1, keepdims=True) * inv_q, 0.0)
    w_k = jnp.where(raw_k > 1.0, jnp.sum(pushed * recalled, axis=1, keepdims=True) * inv_k, 0.0)
    return low_q, low_k, phi_q, phi_k, inv_k, recalled, pushed, scaled, w_q, w_k


def memory_cot_call(sc, gathered, maps, cots, q, k, grad_read, memory, norm):
    T, E = q.shape
    hh = E // HEAD
    ndp = maps.shape[0]
    B = min(512, T)

    def kernel(s, g_ref, maps_ref, cots_ref, q_ref, k_ref, gm_ref, m_ref, n_ref, x_ref, nb_ref):
        cot = jnp.zeros((HEAD, HEAD), F32)
        for a in range(ndp - 1, 0, -1):
            before = cot - times_state(maps_ref[a, 0, 0], cot) + cots_ref[a, 0].astype(F32)
            cot = jnp.where(a > s[PLACE], before * g_ref[a, hh : hh + 1], cot)
        x_ref[0] = cot
        cot = cot.astype(BF)
        memory = m_ref[0].astype(BF)
        sums = jnp.zeros((1, HEAD), F32)
        for i in range(T // B):
            rows = slice(i * B, (i + 1) * B)
            live = row_ids(B, i * B) < s[VALID]
            terms = memory_rows(
                q_ref[rows].astype(F32), k_ref[rows].astype(F32), gm_ref[rows].astype(F32), live, memory, n_ref[0], cot
            )
            sums = sums + jnp.sum(terms[2] * terms[8] + terms[3] * terms[9], axis=0, keepdims=True)
        nb_ref[0] = sums

    head = pl.BlockSpec((T, HEAD), lambda h, s: (0, h))
    square = pl.BlockSpec((1, HEAD, HEAD), lambda h, s: (h, 0, 0))
    row = pl.BlockSpec((1, 1, HEAD), lambda h, s: (h, 0, 0))
    return call(
        kernel,
        (shape((hh, HEAD, HEAD), F32), shape((hh, 1, HEAD), F32)),
        (hh,),
        [
            whole(gathered.shape),
            pl.BlockSpec((ndp, 1, 1, HEAD, HEAD), lambda h, s: (0, 0, h, 0, 0)),
            pl.BlockSpec((ndp, 1, HEAD, HEAD), lambda h, s: (0, h, 0, 0)),
            head,
            head,
            head,
            square,
            row,
        ],
        [square, row],
        (8 * T * E * HEAD, 6 * T * E),
    )(sc, gathered, maps, cots, q, k, grad_read, memory, norm)


def combine_call(sc, chips, q, k, v, grad_read, local_grads, memory, norm, cot, gathered, norm_parts):
    T, E = q.shape
    hh = E // HEAD
    R = T // chips // 2
    ndp = gathered.shape[0]
    per = local_grads[0][0].shape[1] // HEAD
    groups = len(local_grads)

    def kernel(s, q_ref, k_ref, v_ref, gm_ref, *rest):
        local_refs = rest[: 3 * groups]
        m_ref, n_ref, x_ref, g_ref, nb_ref, gq_ref, gk_ref, gv_ref = rest[3 * groups :]
        begin = piece(pl.program_id(0), s) * R
        live = row_ids(R, begin) < s[VALID]
        for h in range(hh):
            cols = slice(h * HEAD, (h + 1) * HEAD)
            part = slice(h % per * HEAD, (h % per + 1) * HEAD)
            dq, dk, dv = (ref[:, part] for ref in local_refs[3 * (h // per) : 3 * (h // per) + 3])
            norm_cot = jnp.zeros((1, HEAD), F32)
            for a in range(ndp - 1, 0, -1):
                before = (norm_cot + nb_ref[a, h : h + 1]) * g_ref[a, hh : hh + 1]
                norm_cot = jnp.where(a > s[PLACE], before, norm_cot)
            memory = m_ref[h].astype(BF)
            cot = x_ref[h].astype(BF)
            norm = n_ref[h]
            low_q, low_k, _, _, inv_k, recalled, pushed, scaled, w_q, w_k = memory_rows(
                q_ref[:, cols].astype(F32), k_ref[:, cols].astype(F32), gm_ref[:, cols].astype(F32), live, memory, norm, cot
            )
            grad_phi_q = dot_nt(scaled.astype(BF), memory) + w_q * norm
            grad_phi_k = (
                dot_nt((v_ref[:, cols].astype(F32) - recalled).astype(BF), cot)
                - dot_nt((pushed * inv_k).astype(BF), memory)
                + w_k * norm
                + norm_cot
            )
            gq_ref[:, cols] = (dq + grad_phi_q * low_q).astype(BF)
            gk_ref[:, cols] = (dk + jnp.where(live, grad_phi_k * low_k, 0.0)).astype(BF)
            gv_ref[:, cols] = (dv + pushed).astype(BF)

    def piece(p, s):
        core = lax.rem(s[CORE] + p, 2)
        return chip_block(s, p // 2, chips) * 2 + core

    rows = pl.BlockSpec((R, E), lambda p, s: (piece(p, s), 0))
    part_rows = pl.BlockSpec((R, per * HEAD), lambda p, s: (piece(p, s), 0))
    out = pl.BlockSpec((R, E), lambda p, s: (p, 0))
    o = shape((T, E), BF)
    return call(
        kernel,
        (o, o, o),
        (2 * chips,),
        [rows] * 4 + [part_rows] * (3 * groups) + [whole(x.shape) for x in (memory, norm, cot, gathered, norm_parts)],
        [out, out, out],
        (14 * T * E * HEAD, 26 * T * E),
    )(sc, q, k, v, grad_read, *[x for group in local_grads for x in group], memory, norm, cot, gathered, norm_parts)


def grad_normed_call(sc, j, gq, gk, gv, wq, wk, wv, chips):
    T, E = gq.shape
    R = T // chips // 2
    D = wq.shape[0]
    n = min(512, D)

    def kernel(s, gq_ref, gk_ref, gv_ref, wq_ref, wk_ref, wv_ref, oa_ref, ob_ref):
        for i, o_ref in enumerate((oa_ref, ob_ref)):
            rows = slice(i * R, (i + 1) * R)
            o_ref[...] = (
                dot_nt(gq_ref[rows], wq_ref[...]) + dot_nt(gk_ref[rows], wk_ref[...]) + dot_nt(gv_ref[rows], wv_ref[...])
            ).astype(BF)

    o = shape((R, D), BF)
    rows = pl.BlockSpec((2 * R, E), lambda c, s: (j, 0))
    cols = pl.BlockSpec((n, E), lambda c, s: (c, 0))
    out = pl.BlockSpec((R, n), lambda c, s: (0, c))
    return call(
        kernel,
        (o, o),
        (D // n,),
        [rows, rows, rows, cols, cols, cols],
        [out, out],
        (12 * R * D * E, 12 * R * E + 6 * D * E + 4 * R * D),
    )(sc, gq, gk, gv, wq, wk, wv)


def swap_core(x):
    return lax.ppermute(x, "tensor", [(i, i ^ 1) for i in range(lax.axis_size("tensor"))])


def shift_chip(x, j):
    count = lax.axis_size("tensor")
    return lax.ppermute(x, "tensor", [(i, (i + 2 * j) % count) for i in range(count)])


def after(x, *others):
    return lax.optimization_barrier((x, *others))[0]


def gather_rows(x, chips, wait=None):
    blocks = [(x, swap_core(x))]
    far = x if wait is None else after(x, wait)
    for j in range(1, chips):
        moved = shift_chip(far, -j)
        blocks.append((moved, swap_core(moved)))
    return blocks


def scatter_rows(blocks, wait=None):
    sums = [mine.astype(F32) + swap_core(other).astype(F32) for mine, other in blocks]
    total = sums[0]
    for j in range(1, len(blocks)):
        low = sums[j].astype(BF)
        if wait is not None:
            low = after(low, wait)
        total = total + shift_chip(low, j).astype(F32)
    return total


def chunk_order(me, ndp):
    parity = me % 2
    order = [2 * i + (1 - parity) for i in range(ndp // 2)] + [2 * i + parity for i in range(ndp // 2)]
    return jnp.stack(order)


def sum_over_dp(grads):
    ndp = grads.shape[0]
    half = ndp // 2
    got = lax.ppermute(grads[:half], "dp", [(i, i ^ 1) for i in range(ndp)])
    pair = (got.astype(F32) + grads[half:].astype(F32)).astype(BF)
    groups = [list(range(0, ndp, 2)), list(range(1, ndp, 2))]
    out = lax.psum_scatter(pair.reshape((-1, grads.shape[2])), "dp", scatter_dimension=0, axis_index_groups=groups, tiled=True)
    return out.astype(F32)


def sum_everywhere(x):
    for axis in ("tensor", "dp"):
        count, step = lax.axis_size(axis), 1
        while step < count:
            x = x + lax.ppermute(x, axis, [(i, i ^ step) for i in range(count)])
            step *= 2
    return x


def body(
    tokens,
    gain1,
    w_query,
    w_key,
    w_value,
    w_out,
    gate_bias,
    gain2,
    w_gate,
    w_up,
    w_down,
    seg_starts,
    seg_valid,
    cotangent,
):
    count = lax.axis_size("tensor")
    ndp = lax.axis_size("dp")
    chips = count // 2
    hh = gate_bias.shape[0]
    E = hh * HEAD
    here = lax.axis_index("tensor")
    place = lax.axis_index("dp")
    sc = jnp.concatenate(
        [
            jnp.stack([here // 2, here % 2, place]).astype(jnp.int32),
            seg_valid.astype(jnp.int32),
            chunk_order(place, ndp).astype(jnp.int32),
        ]
    )
    keep = (1 - seg_starts[0]).astype(F32)
    sig_bias = jax.nn.sigmoid(gate_bias)
    mix = jnp.broadcast_to(sig_bias[:, None, None], (hh, 1, HEAD))

    x = tokens.astype(F32)
    inv1 = lax.rsqrt(jnp.mean(x * x, axis=-1, keepdims=True) + EPSILON)
    normed1 = (x * inv1 * gain1).astype(BF)
    rows1 = gather_rows(normed1, chips)
    qkv = None
    sums = 0.0
    for j, (a, b) in enumerate(rows1):
        *qkv, column_sums = qkv_call(sc, j, chips, a, b, w_query, w_key, w_value, qkv)
        sums = sums + column_sums
    q, k, v = qkv
    cot_rows = gather_rows(cotangent, chips, wait=rows1[-1][0])

    own = jnp.concatenate([sums.reshape(hh, HEAD), jnp.full((8 - hh, HEAD), keep, F32)])
    gathered = lax.all_gather(own, "dp")
    maps, norm = maps_call(sc, k, v, gathered)
    all_maps = lax.all_gather(maps, "dp")
    local, lse = attn_fwd_call(sc, q, k, v)
    memory = chain_call(sc, gathered, all_maps)

    grad_inner = [grad_inner_call(sc, a, b, w_down) for a, b in cot_rows]
    partial, mixed, diff = [None] * chips, [None] * chips, [None] * chips
    for j in reversed(range(chips)):
        a, b, mixed[j], diff[j] = mixout_call(sc, j, chips, q, local, memory, norm, mix, w_out)
        partial[j] = (a, b)
    hidden = x + scatter_rows(partial)
    inv2 = lax.rsqrt(jnp.mean(hidden * hidden, axis=-1, keepdims=True) + EPSILON)
    unit2 = hidden * inv2
    normed2 = (unit2 * gain2).astype(BF)
    rows2 = gather_rows(normed2, chips)

    inner, grad_gate, grad_up = [], [], []
    for (a, b), gi in zip(rows2, grad_inner):
        one, two, three = ffn_a_call(sc, a, b, w_gate, w_up, gi)
        inner.append(one)
        grad_gate.append(two)
        grad_up.append(three)
    back = [None] * chips
    for j in reversed(range(chips)):
        back[j] = ffn_b_call(sc, grad_gate[j], grad_up[j], w_gate, w_up)
    grad_normed2 = scatter_rows(back)
    flat_rows2 = [piece for block in rows2 for piece in block]
    flat_cot = [piece for block in cot_rows for piece in block]
    grad_down = sum_over_dp(wgrad_call(sc, flat_cot, [inner], ndp))
    grad_gate_up = sum_over_dp(wgrad_call(sc, flat_rows2, [grad_gate, grad_up], ndp))

    gain2_part = jnp.sum(grad_normed2 * unit2, axis=0)
    scaled2 = grad_normed2 * gain2
    grad_hidden = cotangent.astype(F32) + inv2 * (
        scaled2 - unit2 * jnp.mean(scaled2 * unit2, axis=-1, keepdims=True)
    )
    grad_rows = gather_rows(grad_hidden.astype(BF), chips)
    grads = None
    cot_part, bias_part = 0.0, 0.0
    for j, (a, b) in enumerate(grad_rows):
        *grads, cot_j, bias_j = gradmix_call(sc, j, chips, a, b, w_out, diff[j], q, norm, mix, grads)
        cot_part = cot_part + cot_j
        bias_part = bias_part + bias_j
    grad_local, grad_read = grads
    all_cots = lax.all_gather(cot_part.astype(BF), "dp")

    down = [down_call(sc, block, w_down) for block in inner]
    output = (hidden + scatter_rows(down, wait=grad_rows[-1][0])).astype(BF)
    flat_grad = [piece for block in grad_rows for piece in block]
    grad_out = sum_over_dp(wgrad_call(sc, flat_grad, [mixed], ndp))

    per = max(1, hh // 2)
    local_grads = [
        attn_bwd_call(sc, q, k, v, grad_local, local, lse, h, per) for h in range(0, hh, per)
    ]
    memory_cot, norm_part = memory_cot_call(sc, gathered, all_maps, all_cots, q, k, grad_read, memory, norm)
    norm_pad = jnp.concatenate([norm_part.reshape(hh, HEAD), jnp.zeros((8 - hh, HEAD), F32)])
    norm_parts = lax.all_gather(norm_pad, "dp")
    gq, gk, gv = combine_call(
        sc, chips, q, k, v, grad_read, local_grads, memory, norm, memory_cot, gathered, norm_parts
    )
    flat_rows1 = [piece for block in rows1 for piece in block]
    grad_qkv = sum_over_dp(wgrad_call(sc, flat_rows1, [[gq], [gk], [gv]], ndp))
    back1 = [None] * chips
    for j in reversed(range(chips)):
        back1[j] = grad_normed_call(sc, j, gq, gk, gv, w_query, w_key, w_value, chips)
    grad_normed1 = scatter_rows(back1)
    unit1 = x * inv1
    gain1_part = jnp.sum(grad_normed1 * unit1, axis=0)
    scaled1 = grad_normed1 * gain1
    grad_tokens = grad_hidden + inv1 * (
        scaled1 - unit1 * jnp.mean(scaled1 * unit1, axis=-1, keepdims=True)
    )

    bias_here = jnp.sum(bias_part.reshape(hh, HEAD), axis=1) * sig_bias * (1.0 - sig_bias)
    bias_full = lax.dynamic_update_slice(jnp.zeros((HEADS,), F32), bias_here, (here * hh,))
    small = sum_everywhere(jnp.concatenate([gain1_part, gain2_part, bias_full]))
    D = gain1.shape[0]
    F = w_gate.shape[1]
    return (
        output,
        grad_tokens,
        small[:D],
        grad_qkv[:, :E],
        grad_qkv[:, E : 2 * E],
        grad_qkv[:, 2 * E :],
        grad_out.T,
        small[2 * D :],
        small[D : 2 * D],
        grad_gate_up[:, :F],
        grad_gate_up[:, F:],
        grad_down.T,
    )


def solution(mesh):
    rows = P(("dp", "tensor"), None)
    return jax.shard_map(
        body,
        mesh=mesh,
        in_specs=(
            rows,
            P(),
            P(None, "tensor"),
            P(None, "tensor"),
            P(None, "tensor"),
            P("tensor", None),
            P("tensor"),
            P(),
            P(None, "tensor"),
            P(None, "tensor"),
            P("tensor", None),
            P("dp"),
            P("dp"),
            rows,
        ),
        out_specs=(
            rows,
            rows,
            P(),
            P("dp", "tensor"),
            P("dp", "tensor"),
            P("dp", "tensor"),
            P("tensor", "dp"),
            P(),
            P(),
            P("dp", "tensor"),
            P("dp", "tensor"),
            P("tensor", "dp"),
        ),
        check_vma=False,
    )
```

time: 3160 us -> 1300 us (0.41)
  waiting for transfers between devices: 1790 us -> 647 us
  matrix products: 858 us -> 0 us
  Pallas kernels: 0 us -> 441 us
  local copies, waits for them, and re-layouts: 251 us -> 36.5 us
  starting transfers between devices: 88 us -> 20.6 us
    reduce_scatter x11 -> x4, waiting for transfers between devices: 1490 us -> 0.01 us  [sum_over_dp(): lax.psum_scatter(pair.reshape((-1, grads.shape[2])), 'dp', scatter_dimens...]
    dot_general x78 -> x0, matrix products: 858 us -> none  [the longest x4 116 us: attention_back(): jnp.einsum('hts,thd->shd', grad_scores, query_block, preferred_element_ty...]
    ppermute x28 -> x33, waiting for transfers between devices: 135 us -> 616 us  [the longest x8 338 us: shift_chip(): lax.ppermute(x, 'tensor', [(i, (i + 2 * j) % count) for i in range(count)])]
    pallas_call x0 -> x27, Pallas kernels: none -> 441 us  [the longest x4 102 us: wgrad_call(): call(kernel, shape((ndp, C, N), BF), (ndp,), [pl.BlockSpec((R, C), lambda...]
    dynamic_update_slice x16 -> x0, local copies, waits for them, and re-layouts: 187 us -> none  [body(): local_blocks, log_totals = lax.map(attend_block, block_begins)]
    all_gather x4 -> x2, waiting for transfers between devices: 168 us -> 31.2 us  [the longest x1 31.2 us: body(): all_maps = lax.all_gather(maps, 'dp')]
    ppermute x28 -> x33, starting transfers between devices: 86.8 us -> 20.1 us  [the longest x8 11.9 us: shift_chip(): lax.ppermute(x, 'tensor', [(i, (i + 2 * j) % count) for i in range(count)])]
    all_gather x0 -> x2, blocking collectives: none -> 65.7 us  [the longest x1 33.3 us: body(): norm_parts = lax.all_gather(norm_pad, 'dp')]
  transfers between devices with their start and end apart: 43 -> 39, of which waited for: 42 -> 16; matrix products, arithmetic and copies ran while one was open for 7% -> 7% of each run, Pallas kernels for 0% -> 32%
where the time goes in v1:
time: 1300 us
  waiting for transfers between devices  647 us (50%)
  Pallas kernels  441 us (34%)
  other arithmetic  67.9 us (5%)
  blocking collectives  65.7 us (5%)
  local copies, waits for them, and re-layouts  36.5 us (3%)
  starting transfers between devices  20.6 us (2%)
  between operations  16.3 us (1%)
    ppermute x8, waiting for transfers between devices, shift_chip(): lax.ppermute(x, 'tensor', [(i, (i + 2 * j) % count) for i in range(count)])  338 us
    ppermute x4, waiting for transfers between devices, sum_over_dp(): got = lax.ppermute(grads[:half], 'dp', [(i, i ^ 1) for i in range(ndp)])  273 us
    pallas_call x4, Pallas kernels, wgrad_call(): call(kernel, shape((ndp, C, N), BF), (ndp,), [pl.BlockSpec((R, C), lambda...  102 us
    pallas_call x2, Pallas kernels, ffn_a_call(): call(kernel, (o, o, o), (F // n,), [rows, rows, cols, cols, out], [out, o...  54.3 us
    pallas_call x2, Pallas kernels, ffn_b_call(): call(kernel, (o, o), (D // n,), [rows, rows, cols, cols], [out, out], (8...  48.8 us
    pallas_call x2, Pallas kernels, attn_bwd_call(): call(kernel, (o, o, o), (nh,), [head] * 5 + [pl.BlockSpec((1, 1, T), lamb...  42.4 us
    all_gather x1, blocking collectives, body(): norm_parts = lax.all_gather(norm_pad, 'dp')  33.3 us
    all_gather x1, blocking collectives, body(): gathered = lax.all_gather(own, 'dp')  32.4 us
  transfers between devices with their start and end apart: 39, of which 16 were waited for; matrix products, arithmetic and copies ran while one was open for 7% of the time, Pallas kernels for 32%

profile of v1, /device:TPU:0, one launch (start us, length us, event | category | flops | bytes accessed | tf_op | source)
XLA Modules:
  0.0 1295.2 jit_solution(6433713333949263784)
XLA Ops:
  14.5 45.7 %collective-permute-done.xa_ref.refs_2_ = bf16[512,2048]{1,0:T(8,128)(2,1)} collective-permute-done((bf16[512,2048]{1,0:T(8,128)(2,1)S(1)}, bf16[512,2048]{1,0:T(8,128)(2,1)}, u32[]{:S(2)}, u32[]{:S(2)}) %collective-permute-start) | collective-permute-done | bytes 2097184 | tf_op jit(solution)/shard_map/ppermute | solution.py:657
  62.2 12.2 shard_map.229
  74.4 12.2 shard_map.230
  87.3 32.4 %all-gather = f32[64,128]{1,0:T(8,128)} all-gather(f32[8,128]{1,0:T(8,128)S(1)} %concatenate.13), channel_id=2, replica_groups=mesh['dp'=8,'tensor'=4] {'dp'}, dimensions={0}, use_global_device_ids=true | all-gather | bytes 36864 | tf_op jit(solution)/shard_map/all_gather | solution.py:756
  126.9 18.7 %shard_map.231 = (f32[2048,512]{1,0:T(8,128)}, f32[4,1,2048]{2,1,0:T(1,128)}) custom-call(s32[12]{0:T(128)} %concatenate.12.s, bf16[2048,512]{1,0:T(8,128)(2,1)} %get-tuple-element.74.q_ref, bf16[2048,512]{1,0:T(8,128)(2,1)} %get-tuple-element.75.k_ref, bf16[2048,512]{1,0:T(8,128)(2,1)} %get-tuple-element.76.v_ref), custom_call_target="tpu_custom_call" | custom-call | flops 12884901888 | bytes 10485760 | tf_op jit(solution)/shard_map/pallas_call | solution.py:287
  145.6 31.2 %all-gather.7.cloned.1.call-done = bf16[16,4,128,128]{3,2,1,0:T(8,128)(2,1)} async-done(((bf16[2,4,128,128]{3,2,1,0:T(8,128)(2,1)}), bf16[16,4,128,128]{3,2,1,0:T(8,128)(2,1)}) %all-gather.7.cloned.1.call-update) | async-done | bytes 2097168 | tf_op jit(solution)/shard_map/all_gather | solution.py:758
  204.0 45.3 %collective-permute-done.5 = bf16[512,2048]{1,0:T(8,128)(2,1)S(1)} collective-permute-done((bf16[512,2048]{1,0:T(8,128)(2,1)S(1)}, bf16[512,2048]{1,0:T(8,128)(2,1)S(1)}, u32[]{:S(2)}, u32[]{:S(2)}) %collective-permute-start.5) | collective-permute-done | bytes 2097184 | tf_op jit(solution)/shard_map/ppermute | solution.py:657
  253.0 41.4 %collective-permute-done.11.ca_ref.refs_2_ = bf16[512,2048]{1,0:T(8,128)(2,1)} collective-permute-done((bf16[512,2048]{1,0:T(8,128)(2,1)S(1)}, bf16[512,2048]{1,0:T(8,128)(2,1)}, u32[]{:S(2)}, u32[]{:S(2)}) %collective-permute-start.11) | collective-permute-done | bytes 2097184 | tf_op jit(solution)/shard_map/ppermute | solution.py:657
  294.4 44.1 %collective-permute-done.9.xa_ref.refs_2_ = bf16[512,2048]{1,0:T(8,128)(2,1)} collective-permute-done((bf16[512,2048]{1,0:T(8,128)(2,1)S(1)}, bf16[512,2048]{1,0:T(8,128)(2,1)}, u32[]{:S(2)}, u32[]{:S(2)}) %collective-permute-start.9) | collective-permute-done | bytes 2097184 | tf_op jit(solution)/shard_map/ppermute | solution.py:657
  338.6 14.5 %shard_map.236.gi_ref = bf16[1024,2048]{1,0:T(8,128)(2,1)} custom-call(s32[12]{0:T(128)} %concatenate.12.s, bf16[512,2048]{1,0:T(8,128)(2,1)} %refs_0_.1, bf16[512,2048]{1,0:T(8,128)(2,1)} %collective-permute-done.7.cb_ref.refs_1_, bf16[2048,2048]{1,0:T(8,128)(2,1)} %w_ref.13), custom_call_target="tpu_custom_call" | custom-call | flops 8589934592 | bytes 16777216 | tf_op jit(solution)/shard_map/pallas_call | solution.py:127
  353.1 14.3 %shard_map.239.gi_ref = bf16[1024,2048]{1,0:T(8,128)(2,1)} custom-call(s32[12]{0:T(128)} %concatenate.12.s, bf16[512,2048]{1,0:T(8,128)(2,1)} %collective-permute-done.11.ca_ref.refs_2_, bf16[512,2048]{1,0:T(8,128)(2,1)} %collective-permute-done.12.cb_ref.refs_3_, bf16[2048,2048]{1,0:T(8,128)(2,1)} %w_ref.13), custom_call_target="tpu_custom_call" | custom-call | flops 8589934592 | bytes 16777216 | tf_op jit(solution)/shard_map/pallas_call | solution.py:127
  367.9 27.0 %shard_map.240 = (bf16[1024,2048]{1,0:T(8,128)(2,1)}, bf16[1024,2048]{1,0:T(8,128)(2,1)}, bf16[1024,2048]{1,0:T(8,128)(2,1)}) custom-call(s32[12]{0:T(128)} %concatenate.12.s, bf16[512,2048]{1,0:T(8,128)(2,1)} %collective-permute-done.9.xa_ref.refs_2_, bf16[512,2048]{1,0:T(8,128)(2,1)} %collective-permute-done.10.xb_ref.refs_3_, bf16[2048,2048]{1,0:T(8,128)(2,1)} %wg_ref.7, ...), custom_call_target="tpu_custom_call" | custom-call | flops 17179869184 | bytes 37748736 | tf_op jit(solution)/shard_map/pallas_call | solution.py:158
  394.9 24.3 %shard_map.243 = (bf16[512,2048]{1,0:T(8,128)(2,1)}, bf16[512,2048]{1,0:T(8,128)(2,1)}) custom-call(s32[12]{0:T(128)} %concatenate.12.s, bf16[1024,2048]{1,0:T(8,128)(2,1)} %get-tuple-element.97.gg_ref.refs_5_, bf16[1024,2048]{1,0:T(8,128)(2,1)} %get-tuple-element.98.gu_ref.refs_7_, bf16[2048,2048]{1,0:T(8,128)(2,1)} %wg_ref.7, bf16[2048,2048]{1,0:T(8,128)(2,1)} %wu_ref.7), custom_call_target="tpu_custom_call" | custom-call | flops 17179869184 | bytes 29360128 | tf_op jit(solution)/shard_map/pallas_call | solution.py:185
  419.3 27.3 %shard_map.237 = (bf16[1024,2048]{1,0:T(8,128)(2,1)}, bf16[1024,2048]{1,0:T(8,128)(2,1)}, bf16[1024,2048]{1,0:T(8,128)(2,1)}) custom-call(s32[12]{0:T(128)} %concatenate.12.s, bf16[512,2048]{1,0:T(8,128)(2,1)} %copy-done.9, bf16[512,2048]{1,0:T(8,128)(2,1)} %collective-permute-done.6.xb_ref.refs_1_, bf16[2048,2048]{1,0:T(8,128)(2,1)} %wg_ref.7, ...), custom_call_target="tpu_custom_call" | custom-call | flops 17179869184 | bytes 37748736 | tf_op jit(solution)/shard_map/pallas_call | solution.py:158
  446.6 24.4 %shard_map.242 = (bf16[512,2048]{1,0:T(8,128)(2,1)}, bf16[512,2048]{1,0:T(8,128)(2,1)}) custom-call(s32[12]{0:T(128)} %concatenate.12.s, bf16[1024,2048]{1,0:T(8,128)(2,1)} %get-tuple-element.93.gg_ref.refs_4_, bf16[1024,2048]{1,0:T(8,128)(2,1)} %get-tuple-element.94.gu_ref.refs_6_, bf16[2048,2048]{1,0:T(8,128)(2,1)} %wg_ref.7, bf16[2048,2048]{1,0:T(8,128)(2,1)} %wu_ref.7), custom_call_target="tpu_custom_call" | custom-call | flops 17179869184 | bytes 29360128 | tf_op jit(solution)/shard_map/pallas_call | solution.py:185
  475.6 46.1 %collective-permute-done.16 = bf16[512,2048]{1,0:T(8,128)(2,1)S(1)} collective-permute-done((bf16[512,2048]{1,0:T(8,128)(2,1)S(1)}, bf16[512,2048]{1,0:T(8,128)(2,1)S(1)}, u32[]{:S(2)}, u32[]{:S(2)}) %collective-permute-start.16) | collective-permute-done | bytes 2097184 | tf_op jit(solution)/shard_map/ppermute | solution.py:657
  529.5 45.3 %collective-permute-done.17.ya_ref.refs_2_ = bf16[512,2048]{1,0:T(8,128)(2,1)S(1)} collective-permute-done((bf16[512,2048]{1,0:T(8,128)(2,1)S(1)}, bf16[512,2048]{1,0:T(8,128)(2,1)S(1)}, u32[]{:S(2)}, u32[]{:S(2)}) %collective-permute-start.17) | collective-permute-done | bytes 2097184 | tf_op jit(solution)/shard_map/ppermute | solution.py:657
  574.8 25.2 %shard_map.255 = bf16[8,256,2048]{2,1,0:T(8,128)(2,1)} custom-call(s32[12]{0:T(128)} %concatenate.12.s, bf16[512,2048]{1,0:T(8,128)(2,1)} %refs_0_.1, bf16[512,2048]{1,0:T(8,128)(2,1)} %collective-permute-done.7.cb_ref.refs_1_, bf16[512,2048]{1,0:T(8,128)(2,1)} %collective-permute-done.11.ca_ref.refs_2_, ...), custom_call_target="tpu_custom_call" | custom-call | flops 17179869184 | bytes 25165824 | tf_op jit(solution)/shard_map/pallas_call | solution.py:241
  639.3 88.3 %collective-permute-done.30 = bf16[4,256,512]{2,1,0:T(8,128)(2,1)S(1)} collective-permute-done((bf16[4,256,512]{2,1,0:T(8,128)(2,1)S(1)}, bf16[4,256,512]{2,1,0:T(8,128)(2,1)S(1)}, u32[]{:S(2)}, u32[]{:S(2)}) %collective-permute-start.30) | collective-permute-done | bytes 1048608 | tf_op jit(solution)/shard_map/ppermute | solution.py:693
  744.8 21.4 %shard_map.247 = (f32[2048,256]{1,0:T(8,128)}, f32[2048,256]{1,0:T(8,128)}, f32[2048,256]{1,0:T(8,128)}) custom-call(s32[12]{0:T(128)} %concatenate.12.s, bf16[2048,512]{1,0:T(8,128)(2,1)} %get-tuple-element.74.q_ref, bf16[2048,512]{1,0:T(8,128)(2,1)} %get-tuple-element.75.k_ref, bf16[2048,512]{1,0:T(8,128)(2,1)} %get-tuple-element.76.v_ref, ...), custom_call_target="tpu_custom_call" | custom-call | flops 12884901888 | bytes 13631488 | tf_op jit(solution)/shard_map/pallas_call | solution.py:345
  766.2 21.1 %shard_map.246 = (f32[2048,256]{1,0:T(8,128)}, f32[2048,256]{1,0:T(8,128)}, f32[2048,256]{1,0:T(8,128)}) custom-call(s32[12]{0:T(128)} %concatenate.12.s, bf16[2048,512]{1,0:T(8,128)(2,1)} %get-tuple-element.74.q_ref, bf16[2048,512]{1,0:T(8,128)(2,1)} %get-tuple-element.75.k_ref, bf16[2048,512]{1,0:T(8,128)(2,1)} %get-tuple-element.76.v_ref, ...), custom_call_target="tpu_custom_call" | custom-call | flops 12884901888 | bytes 13631488 | tf_op jit(solution)/shard_map/pallas_call | solution.py:345
  787.2 11.6 shard_map.248
  799.6 33.3 %all-gather.3 = f32[64,128]{1,0:T(8,128)} all-gather(f32[8,128]{1,0:T(8,128)S(1)} %concatenate.14), channel_id=5, replica_groups=mesh['dp'=8,'tensor'=4] {'dp'}, dimensions={0}, use_global_device_ids=true | all-gather | bytes 36864 | tf_op jit(solution)/shard_map/all_gather | solution.py:814
  832.8 14.2 %shard_map.249 = (bf16[2048,512]{1,0:T(8,128)(2,1)}, bf16[2048,512]{1,0:T(8,128)(2,1)}, bf16[2048,512]{1,0:T(8,128)(2,1)}) custom-call(s32[12]{0:T(128)} %concatenate.12.s, bf16[2048,512]{1,0:T(8,128)(2,1)} %get-tuple-element.74.q_ref, bf16[2048,512]{1,0:T(8,128)(2,1)} %get-tuple-element.75.k_ref, bf16[2048,512]{1,0:T(8,128)(2,1)} %get-tuple-element.76.v_ref, ...), custom_call_target="tpu_custom_call" | custom-call | flops 1879048192 | bytes 27262976 | tf_op jit(solution)/shard_map/pallas_call | solution.py:614
  847.0 19.8 %shard_map.252 = bf16[8,256,1536]{2,1,0:T(8,128)(2,1)} custom-call(s32[12]{0:T(128)} %concatenate.12.s, bf16[512,2048]{1,0:T(8,128)(2,1)} %copy-done.17, bf16[512,2048]{1,0:T(8,128)(2,1)} %collective-permute-done.2.xb_ref.refs_1_, bf16[512,2048]{1,0:T(8,128)(2,1)} %collective-permute-done.xa_ref.refs_2_, ...), custom_call_target="tpu_custom_call" | custom-call | flops 12884901888 | bytes 20971520 | tf_op jit(solution)/shard_map/pallas_call | solution.py:241
  870.8 45.2 %shard_map.254 = bf16[8,256,4096]{2,1,0:T(8,128)(2,1)} custom-call(s32[12]{0:T(128)} %concatenate.12.s, bf16[512,2048]{1,0:T(8,128)(2,1)} %copy-done.9, bf16[512,2048]{1,0:T(8,128)(2,1)} %collective-permute-done.6.xb_ref.refs_1_, bf16[512,2048]{1,0:T(8,128)(2,1)} %collective-permute-done.9.xa_ref.refs_2_, ...), custom_call_target="tpu_custom_call" | custom-call | flops 34359738368 | bytes 41943040 | tf_op jit(solution)/shard_map/pallas_call | solution.py:241
  925.7 16.5 %collective-permute-done.29 = bf16[4,256,1536]{2,1,0:T(8,128)(2,1)} collective-permute-done((bf16[4,256,1536]{2,1,0:T(8,128)(2,1)}, bf16[4,256,1536]{2,1,0:T(8,128)(2,1)}, u32[]{:S(2)}, u32[]{:S(2)}) %collective-permute-start.29) | collective-permute-done | bytes 3145760 | tf_op jit(solution)/shard_map/ppermute | solution.py:693
  946.7 167.8 %collective-permute-done.31 = bf16[4,256,4096]{2,1,0:T(8,128)(2,1)} collective-permute-done((bf16[4,256,4096]{2,1,0:T(8,128)(2,1)}, bf16[4,256,4096]{2,1,0:T(8,128)(2,1)}, u32[]{:S(2)}, u32[]{:S(2)}) %collective-permute-start.31) | collective-permute-done | bytes 8388640 | tf_op jit(solution)/shard_map/ppermute | solution.py:693
  1136.4 13.8 %shard_map.241 = (bf16[512,2048]{1,0:T(8,128)(2,1)}, bf16[512,2048]{1,0:T(8,128)(2,1)}) custom-call(s32[12]{0:T(128)} %concatenate.12.s, bf16[1024,2048]{1,0:T(8,128)(2,1)} %get-tuple-element.90.x_ref.refs_5_, bf16[2048,2048]{1,0:T(8,128)(2,1)} %w_ref.13), custom_call_target="tpu_custom_call" | custom-call | flops 8589934592 | bytes 16777216 | tf_op jit(solution)/shard_map/pallas_call | solution.py:207
  1165.8 13.7 %shard_map.238 = (bf16[512,2048]{1,0:T(8,128)(2,1)}, bf16[512,2048]{1,0:T(8,128)(2,1)}) custom-call(s32[12]{0:T(128)} %concatenate.12.s, bf16[1024,2048]{1,0:T(8,128)(2,1)} %get-tuple-element.86.x_ref.refs_4_, bf16[2048,2048]{1,0:T(8,128)(2,1)} %w_ref.13), custom_call_target="tpu_custom_call" | custom-call | flops 8589934592 | bytes 16777216 | tf_op jit(solution)/shard_map/pallas_call | solution.py:207
  1183.2 30.1 %collective-permute-done.23 = bf16[512,2048]{1,0:T(8,128)(2,1)} collective-permute-done((bf16[512,2048]{1,0:T(8,128)(2,1)}, bf16[512,2048]{1,0:T(8,128)(2,1)}, u32[]{:S(2)}, u32[]{:S(2)}) %collective-permute-start.23) | collective-permute-done | bytes 2097184 | tf_op jit(solution)/shard_map/ppermute | solution.py:657
  1218.3 39.4 %collective-permute-done.18 = bf16[512,2048]{1,0:T(8,128)(2,1)} collective-permute-done((bf16[512,2048]{1,0:T(8,128)(2,1)}, bf16[512,2048]{1,0:T(8,128)(2,1)}, u32[]{:S(2)}, u32[]{:S(2)}) %collective-permute-start.18) | collective-permute-done | bytes 2097184 | tf_op jit(solution)/shard_map/ppermute | solution.py:657
  (198 shorter events, 211.1 us)
Async XLA Ops:
  7.2 169.6 %all-gather.7.cloned.1.call-start = ((), (), s32[]{:S(2)}) async-start(), calls=%async_computation.8 | async-start | bytes 2359296 | tf_op jit(solution)/shard_map/all_gather | solution.py:758
  11.5 48.8 %collective-permute-start = (bf16[512,2048]{1,0:T(8,128)(2,1)S(1)}, bf16[512,2048]{1,0:T(8,128)(2,1)}, u32[]{:S(2)}, u32[]{:S(2)}) collective-permute-start(bf16[512,2048]{1,0:T(8,128)(2,1)S(1)} %fusion.4.xa_ref.refs_0_), channel_id=1, source_target_pairs={{0,2},{1,3},{2,0},{3,1},{4,6},{5,7},{6,4},{7,5},{8,10},{9,11},{10,... | collective-permute-start | bytes 6291464 | tf_op jit(solution)/shard_map/ppermute | solution.py:657
  14.5 47.7 %collective-permute-start.2 = (bf16[512,2048]{1,0:T(8,128)(2,1)S(1)}, bf16[512,2048]{1,0:T(8,128)(2,1)}, u32[]{:S(2)}, u32[]{:S(2)}) collective-permute-start(bf16[512,2048]{1,0:T(8,128)(2,1)S(1)} %fusion.4.xa_ref.refs_0_), channel_id=1, source_target_pairs={{0,1},{1,0},{2,3},{3,2},{4,5},{5,4},{6,7},{7,6},{8,9},{9,8},{10,11... | collective-permute-start | bytes 6291464 | tf_op jit(solution)/shard_map/ppermute | solution.py:652
  60.2 14.1 %collective-permute-start.1 = (bf16[512,2048]{1,0:T(8,128)(2,1)}, bf16[512,2048]{1,0:T(8,128)(2,1)}, u32[]{:S(2)}, u32[]{:S(2)}) collective-permute-start(bf16[512,2048]{1,0:T(8,128)(2,1)} %collective-permute-done.xa_ref.refs_2_), channel_id=1, source_target_pairs={{0,1},{1,0},{2,3},{3,2},{4,5},{5,4},{6,7},{7,6},{8,9},{9,8},{10,11... | collective-permute-start | bytes 6291464 | tf_op jit(solution)/shard_map/ppermute | solution.py:652
  126.6 660.7 %all-gather.9.cloned.1.call-start = ((), (), s32[]{:S(2)}) async-start(), calls=%async_computation.9 | async-start | bytes 1179648 | tf_op jit(solution)/shard_map/all_gather | solution.py:801
  200.8 48.5 %collective-permute-start.5 = (bf16[512,2048]{1,0:T(8,128)(2,1)S(1)}, bf16[512,2048]{1,0:T(8,128)(2,1)S(1)}, u32[]{:S(2)}, u32[]{:S(2)}) collective-permute-start(bf16[512,2048]{1,0:T(8,128)(2,1)S(1)} %add_convert_fusion.7), channel_id=1, source_target_pairs={{0,2},{1,3},{2,0},{3,1},{4,6},{5,7},{6,4},{7,5},{8,10},{9,11},{10,... | collective-permute-start | bytes 6291464 | tf_op jit(solution)/shard_map/ppermute | solution.py:657
  202.4 92.0 %collective-permute-start.11 = (bf16[512,2048]{1,0:T(8,128)(2,1)S(1)}, bf16[512,2048]{1,0:T(8,128)(2,1)}, u32[]{:S(2)}, u32[]{:S(2)}) collective-permute-start(bf16[512,2048]{1,0:T(8,128)(2,1)S(1)} %copy-done.7), channel_id=1, source_target_pairs={{0,2},{1,3},{2,0},{3,1},{4,6},{5,7},{6,4},{7,5},{8,10},{9,11},{10,... | collective-permute-start | bytes 6291464 | tf_op jit(solution)/shard_map/ppermute | solution.py:657
  251.4 87.1 %collective-permute-start.9 = (bf16[512,2048]{1,0:T(8,128)(2,1)S(1)}, bf16[512,2048]{1,0:T(8,128)(2,1)}, u32[]{:S(2)}, u32[]{:S(2)}) collective-permute-start(bf16[512,2048]{1,0:T(8,128)(2,1)S(1)} %multiply_convert_fusion.xa_ref.refs_0_), channel_id=1, source_target_pairs={{0,2},{1,3},{2,0},{3,1},{4,6},{5,7},{6,4},{7,5},{8,10},{9,11},{10,... | collective-permute-start | bytes 6291464 | tf_op jit(solution)/shard_map/ppermute | solution.py:657
  253.0 85.6 %collective-permute-start.7 = (bf16[512,2048]{1,0:T(8,128)(2,1)S(1)}, bf16[512,2048]{1,0:T(8,128)(2,1)}, u32[]{:S(2)}, u32[]{:S(2)}) collective-permute-start(bf16[512,2048]{1,0:T(8,128)(2,1)S(1)} %copy-done.7), channel_id=1, source_target_pairs={{0,1},{1,0},{2,3},{3,2},{4,5},{5,4},{6,7},{7,6},{8,9},{9,8},{10,11... | collective-permute-start | bytes 6291464 | tf_op jit(solution)/shard_map/ppermute | solution.py:652
  294.4 58.7 %collective-permute-start.12 = (bf16[512,2048]{1,0:T(8,128)(2,1)}, bf16[512,2048]{1,0:T(8,128)(2,1)}, u32[]{:S(2)}, u32[]{:S(2)}) collective-permute-start(bf16[512,2048]{1,0:T(8,128)(2,1)} %collective-permute-done.11.ca_ref.refs_2_), channel_id=1, source_target_pairs={{0,1},{1,0},{2,3},{3,2},{4,5},{5,4},{6,7},{7,6},{8,9},{9,8},{10,11... | collective-permute-start | bytes 6291464 | tf_op jit(solution)/shard_map/ppermute | solution.py:652
  338.6 29.3 %collective-permute-start.10 = (bf16[512,2048]{1,0:T(8,128)(2,1)}, bf16[512,2048]{1,0:T(8,128)(2,1)}, u32[]{:S(2)}, u32[]{:S(2)}) collective-permute-start(bf16[512,2048]{1,0:T(8,128)(2,1)} %collective-permute-done.9.xa_ref.refs_2_), channel_id=1, source_target_pairs={{0,1},{1,0},{2,3},{3,2},{4,5},{5,4},{6,7},{7,6},{8,9},{9,8},{10,11... | collective-permute-start | bytes 6291464 | tf_op jit(solution)/shard_map/ppermute | solution.py:652
  367.4 51.9 %collective-permute-start.6 = (bf16[512,2048]{1,0:T(8,128)(2,1)S(1)}, bf16[512,2048]{1,0:T(8,128)(2,1)}, u32[]{:S(2)}, u32[]{:S(2)}) collective-permute-start(bf16[512,2048]{1,0:T(8,128)(2,1)S(1)} %copy-done.10), channel_id=1, source_target_pairs={{0,1},{1,0},{2,3},{3,2},{4,5},{5,4},{6,7},{7,6},{8,9},{9,8},{10,11... | collective-permute-start | bytes 6291464 | tf_op jit(solution)/shard_map/ppermute | solution.py:652
  419.3 52.3 %collective-permute-start.15 = (bf16[512,2048]{1,0:T(8,128)(2,1)}, bf16[512,2048]{1,0:T(8,128)(2,1)}, u32[]{:S(2)}, u32[]{:S(2)}) collective-permute-start(bf16[512,2048]{1,0:T(8,128)(2,1)} %get-tuple-element.100), channel_id=1, source_target_pairs={{0,1},{1,0},{2,3},{3,2},{4,5},{5,4},{6,7},{7,6},{8,9},{9,8},{10,11... | collective-permute-start | bytes 6291464 | tf_op jit(solution)/shard_map/ppermute | solution.py:652
  474.0 47.7 %collective-permute-start.16 = (bf16[512,2048]{1,0:T(8,128)(2,1)S(1)}, bf16[512,2048]{1,0:T(8,128)(2,1)S(1)}, u32[]{:S(2)}, u32[]{:S(2)}) collective-permute-start(bf16[512,2048]{1,0:T(8,128)(2,1)S(1)} %add_convert_fusion.5), channel_id=1, source_target_pairs={{0,2},{1,3},{2,0},{3,1},{4,6},{5,7},{6,4},{7,5},{8,10},{9,11},{10,... | collective-permute-start | bytes 6291464 | tf_op jit(solution)/shard_map/ppermute | solution.py:657
  528.0 46.8 %collective-permute-start.17 = (bf16[512,2048]{1,0:T(8,128)(2,1)S(1)}, bf16[512,2048]{1,0:T(8,128)(2,1)S(1)}, u32[]{:S(2)}, u32[]{:S(2)}) collective-permute-start(bf16[512,2048]{1,0:T(8,128)(2,1)S(1)} %get-tuple-element.134.ya_ref.refs_0_), channel_id=1, source_target_pairs={{0,2},{1,3},{2,0},{3,1},{4,6},{5,7},{6,4},{7,5},{8,10},{9,11},{10,... | collective-permute-start | bytes 6291464 | tf_op jit(solution)/shard_map/ppermute | solution.py:657
  529.5 75.9 %collective-permute-start.20 = (bf16[512,2048]{1,0:T(8,128)(2,1)S(1)}, bf16[512,2048]{1,0:T(8,128)(2,1)}, u32[]{:S(2)}, u32[]{:S(2)}) collective-permute-start(bf16[512,2048]{1,0:T(8,128)(2,1)S(1)} %get-tuple-element.134.ya_ref.refs_0_), channel_id=1, source_target_pairs={{0,1},{1,0},{2,3},{3,2},{4,5},{5,4},{6,7},{7,6},{8,9},{9,8},{10,11... | collective-permute-start | bytes 6291464 | tf_op jit(solution)/shard_map/ppermute | solution.py:652
  574.7 38.9 %collective-permute-start.19 = (bf16[512,2048]{1,0:T(8,128)(2,1)S(1)}, bf16[512,2048]{1,0:T(8,128)(2,1)S(1)}, u32[]{:S(2)}, u32[]{:S(2)}) collective-permute-start(bf16[512,2048]{1,0:T(8,128)(2,1)S(1)} %collective-permute-done.17.ya_ref.refs_2_), channel_id=1, source_target_pairs={{0,1},{1,0},{2,3},{3,2},{4,5},{5,4},{6,7},{7,6},{8,9},{9,8},{10,11... | collective-permute-start | bytes 6291464 | tf_op jit(solution)/shard_map/ppermute | solution.py:652
  604.9 125.6 %collective-permute-start.32 = (bf16[4,256,2048]{2,1,0:T(8,128)(2,1)}, bf16[4,256,2048]{2,1,0:T(8,128)(2,1)}, u32[]{:S(2)}, u32[]{:S(2)}) collective-permute-start(bf16[4,256,2048]{2,1,0:T(8,128)(2,1)} %slice.78), channel_id=1, source_target_pairs={{0,4},{4,0},{8,12},{12,8},{16,20},{20,16},{24,28},{28,24},{1,5},{5... | collective-permute-start | bytes 12582920 | tf_op jit(solution)/shard_map/ppermute | solution.py:693
  625.1 639.2 %reduce-scatter.7.cloned.1.call-start = ((), (), s32[]{:S(2)}) async-start(), calls=%async_computation.5 | async-start | bytes 1310720 | tf_op jit(solution)/shard_map/reduce_scatter | solution.py:696
  637.7 89.8 %collective-permute-start.30 = (bf16[4,256,512]{2,1,0:T(8,128)(2,1)S(1)}, bf16[4,256,512]{2,1,0:T(8,128)(2,1)S(1)}, u32[]{:S(2)}, u32[]{:S(2)}) collective-permute-start(bf16[4,256,512]{2,1,0:T(8,128)(2,1)S(1)} %slice.70), channel_id=1, source_target_pairs={{0,4},{4,0},{8,12},{12,8},{16,20},{20,16},{24,28},{28,24},{1,5},{5... | collective-permute-start | bytes 3145736 | tf_op jit(solution)/shard_map/ppermute | solution.py:693
  730.4 536.8 %reduce-scatter.11.cloned.1.call-start = ((), (), s32[]{:S(2)}) async-start(), calls=%async_computation.7 | async-start | bytes 5242880 | tf_op jit(solution)/shard_map/reduce_scatter | solution.py:696
  744.8 536.8 %reduce-scatter.5.cloned.1.call-start = ((), (), s32[]{:S(2)}) async-start(), calls=%async_computation.4 | async-start | bytes 3932160 | tf_op jit(solution)/shard_map/reduce_scatter | solution.py:696
  870.8 71.4 %collective-permute-start.29 = (bf16[4,256,1536]{2,1,0:T(8,128)(2,1)}, bf16[4,256,1536]{2,1,0:T(8,128)(2,1)}, u32[]{:S(2)}, u32[]{:S(2)}) collective-permute-start(bf16[4,256,1536]{2,1,0:T(8,128)(2,1)} %slice.65), channel_id=1, source_target_pairs={{0,4},{4,0},{8,12},{12,8},{16,20},{20,16},{24,28},{28,24},{1,5},{5... | collective-permute-start | bytes 9437192 | tf_op jit(solution)/shard_map/ppermute | solution.py:693
  923.8 190.7 %collective-permute-start.31 = (bf16[4,256,4096]{2,1,0:T(8,128)(2,1)}, bf16[4,256,4096]{2,1,0:T(8,128)(2,1)}, u32[]{:S(2)}, u32[]{:S(2)}) collective-permute-start(bf16[4,256,4096]{2,1,0:T(8,128)(2,1)} %slice.74), channel_id=1, source_target_pairs={{0,4},{4,0},{8,12},{12,8},{16,20},{20,16},{24,28},{28,24},{1,5},{5... | collective-permute-start | bytes 25165832 | tf_op jit(solution)/shard_map/ppermute | solution.py:693
  946.7 337.2 %reduce-scatter.9.cloned.1.call-start = ((), (), s32[]{:S(2)}) async-start(), calls=%async_computation.6 | async-start | bytes 10485760 | tf_op jit(solution)/shard_map/reduce_scatter | solution.py:696
  1136.4 25.9 %collective-permute-start.22 = (bf16[512,2048]{1,0:T(8,128)(2,1)}, bf16[512,2048]{1,0:T(8,128)(2,1)S(1)}, u32[]{:S(2)}, u32[]{:S(2)}) collective-permute-start(bf16[512,2048]{1,0:T(8,128)(2,1)} %get-tuple-element.125), channel_id=1, source_target_pairs={{0,1},{1,0},{2,3},{3,2},{4,5},{5,4},{6,7},{7,6},{8,9},{9,8},{10,11... | collective-permute-start | bytes 6291464 | tf_op jit(solution)/shard_map/ppermute | solution.py:652
  1150.2 29.6 %collective-permute-start.13 = (bf16[512,2048]{1,0:T(8,128)(2,1)}, bf16[512,2048]{1,0:T(8,128)(2,1)S(1)}, u32[]{:S(2)}, u32[]{:S(2)}) collective-permute-start(bf16[512,2048]{1,0:T(8,128)(2,1)} %get-tuple-element.92), channel_id=1, source_target_pairs={{0,1},{1,0},{2,3},{3,2},{4,5},{5,4},{6,7},{7,6},{8,9},{9,8},{10,11... | collective-permute-start | bytes 6291464 | tf_op jit(solution)/shard_map/ppermute | solution.py:652
  1162.2 20.9 %collective-permute-start.21 = (bf16[512,2048]{1,0:T(8,128)(2,1)}, bf16[512,2048]{1,0:T(8,128)(2,1)}, u32[]{:S(2)}, u32[]{:S(2)}) collective-permute-start(bf16[512,2048]{1,0:T(8,128)(2,1)} %get-tuple-element.123), channel_id=1, source_target_pairs={{0,1},{1,0},{2,3},{3,2},{4,5},{5,4},{6,7},{7,6},{8,9},{9,8},{10,11... | collective-permute-start | bytes 6291464 | tf_op jit(solution)/shard_map/ppermute | solution.py:652
  1164.5 48.7 %collective-permute-start.23 = (bf16[512,2048]{1,0:T(8,128)(2,1)}, bf16[512,2048]{1,0:T(8,128)(2,1)}, u32[]{:S(2)}, u32[]{:S(2)}) collective-permute-start(bf16[512,2048]{1,0:T(8,128)(2,1)} %add_convert_fusion.3), channel_id=1, source_target_pairs={{0,2},{1,3},{2,0},{3,1},{4,6},{5,7},{6,4},{7,5},{8,10},{9,11},{10,... | collective-permute-start | bytes 6291464 | tf_op jit(solution)/shard_map/ppermute | solution.py:657
  1179.5 38.8 %collective-permute-start.8 = (bf16[512,2048]{1,0:T(8,128)(2,1)}, bf16[512,2048]{1,0:T(8,128)(2,1)}, u32[]{:S(2)}, u32[]{:S(2)}) collective-permute-start(bf16[512,2048]{1,0:T(8,128)(2,1)} %get-tuple-element.88), channel_id=1, source_target_pairs={{0,1},{1,0},{2,3},{3,2},{4,5},{5,4},{6,7},{7,6},{8,9},{9,8},{10,11... | collective-permute-start | bytes 6291464 | tf_op jit(solution)/shard_map/ppermute | solution.py:652
  1182.0 75.7 %collective-permute-start.18 = (bf16[512,2048]{1,0:T(8,128)(2,1)}, bf16[512,2048]{1,0:T(8,128)(2,1)}, u32[]{:S(2)}, u32[]{:S(2)}) collective-permute-start(bf16[512,2048]{1,0:T(8,128)(2,1)} %add_convert_fusion.6), channel_id=1, source_target_pairs={{0,2},{1,3},{2,0},{3,1},{4,6},{5,7},{6,4},{7,5},{8,10},{9,11},{10,... | collective-permute-start | bytes 6291464 | tf_op jit(solution)/shard_map/ppermute | solution.py:657
  1218.2 44.7 %collective-permute-start.24 = (f32[4112]{0:T(1024)S(1)}, f32[4112]{0:T(1024)S(1)}, u32[]{:S(2)}, u32[]{:S(2)}) collective-permute-start(f32[4112]{0:T(1024)S(1)} %pad_maximum_fusion), channel_id=1, source_target_pairs={{0,1},{1,0},{2,3},{3,2},{4,5},{5,4},{6,7},{7,6},{8,9},{9,8},{10,11... | collective-permute-start | bytes 49352 | tf_op jit(solution)/shard_map/ppermute | solution.py:704
  (40 other events, 1205.7 us)
Sparse Core Ops, SparseCore 0:
  126.7 50.0 all-gather.6
  625.2 45.2 all-gather.8
  730.5 25.6 reduce-scatter.6
  758.5 75.7 reduce-scatter.10
  946.8 58.2 reduce-scatter.4
  1125.1 142.8 reduce-scatter.8

commit v2 on v1

--- a/solution.py
+++ b/solution.py
@@ -31,14 +31,25 @@
     return jax.ShapeDtypeStruct(dims, dtype)
 
 
+COST = 20.0
+ORDERED = []
+
+
 def call(kernel, out_shape, grid, in_specs, out_specs, cost, scratch=(), alias=None):
-    return pl.pallas_call(
-        kernel,
+    many = isinstance(out_shape, tuple)
+    plain = len(in_specs) + 1
+    token = [pl.BlockSpec(memory_space=pl.ANY)] * len(ORDERED)
+
+    def ordered_kernel(*refs):
+        kernel(*refs[:plain], *refs[plain + len(token) :])
+
+    made = pl.pallas_call(
+        ordered_kernel,
         out_shape=out_shape,
         grid_spec=pltpu.PrefetchScalarGridSpec(
             num_scalar_prefetch=1,
             grid=grid,
-            in_specs=in_specs,
+            in_specs=list(in_specs) + token,
             out_specs=out_specs,
             scratch_shapes=list(scratch),
         ),
@@ -47,10 +58,201 @@
             dimension_semantics=("arbitrary",) * len(grid), vmem_limit_bytes=VMEM_BYTES
         ),
         cost_estimate=pl.CostEstimate(
-            flops=int(cost[0]), bytes_accessed=int(cost[1]), transcendentals=0
+            flops=int(COST * cost[0]), bytes_accessed=int(COST * cost[1]), transcendentals=0
         ),
     )
 
+    def run(*operands):
+        out = made(*operands, *ORDERED)
+        ORDERED[:] = [out[-1] if many else out]
+        return out
+
+    return run
+
+
+def require(*arrays):
+    ORDERED.extend(arrays)
+
+
+def hold(sc, *arrays):
+    n = len(arrays)
+
+    def kernel(*refs):
+        del refs
+
+    one = pl.BlockSpec(memory_space=pl.ANY)
+    found = call(
+        kernel,
+        tuple(shape(x.shape, x.dtype) for x in arrays),
+        (1,),
+        [one] * n,
+        [one] * n,
+        (1e6, 1e4),
+        alias={1 + i: i for i in range(n)},
+    )(sc, *arrays)
+    ORDERED.clear()
+    ORDERED.append(found[0])
+    return found
+
+
+def hold_pairs(sc, pairs):
+    found = hold(sc, *[x for pair in pairs for x in pair])
+    return [tuple(found[2 * i : 2 * i + 2]) for i in range(len(pairs))]
+
+
+class Halves:
+    def __init__(self, low, high, first):
+        self.low, self.high, self.first = low, high, first
+
+    def __getitem__(self, at):
+        return jnp.where(self.first, self.low[at], self.high[at])
+
+    def __setitem__(self, at, value):
+        @pl.when(self.first)
+        def _():
+            self.low[at] = value
+
+        @pl.when(jnp.logical_not(self.first))
+        def _():
+            self.high[at] = value
+
+
+def rows_call(kernel, outs, sc, rows, shared, sums=0):
+    first = rows[0]
+    R, D = (2 * first[0].shape[0], first[0].shape[1]) if isinstance(first, tuple) else first.shape
+    n = min(128, R // 2)
+    half = R // 2 // n
+    block = pl.BlockSpec((n, D), lambda i, s: (i, 0))
+    low = pl.BlockSpec((n, D), lambda i, s: (jnp.minimum(i, half - 1), 0))
+    high = pl.BlockSpec((n, D), lambda i, s: (jnp.maximum(i - half, 0), 0))
+    one = pl.BlockSpec((1, D), lambda i, s: (0, 0))
+    in_specs, operands, kinds = [], [], []
+    for x in rows:
+        pair = isinstance(x, tuple)
+        kinds.append(pair)
+        in_specs += [low, high] if pair else [block]
+        operands += list(x) if pair else [x]
+    kinds += [False] * len(shared)
+    out_specs, out_shapes = [], []
+    for x in outs:
+        pair = isinstance(x, list)
+        kinds.append(pair)
+        out_specs += [low, high] if pair else [block]
+        out_shapes += [shape((R // 2, D), x[0])] * 2 if pair else [shape((R, D), x)]
+    kinds += [False] * sums
+
+    def body_kernel(s, *refs):
+        i = pl.program_id(0)
+
+        @pl.when(i == 0)
+        def _():
+            for ref in refs[len(refs) - sums :] if sums else ():
+                ref[...] = jnp.zeros_like(ref)
+
+        views, at = [], 0
+        for pair in kinds:
+            views.append(Halves(refs[at], refs[at + 1], i < half) if pair else refs[at])
+            at += 2 if pair else 1
+        kernel(*views)
+
+    found = call(
+        body_kernel,
+        tuple(out_shapes + [shape((1, D), F32)] * sums),
+        (R // n,),
+        in_specs + [one] * len(shared),
+        out_specs + [one] * sums,
+        (10 * R * D, 20 * R * D),
+    )(sc, *operands, *shared)
+    result, at = [], 0
+    for x in outs:
+        pair = isinstance(x, list)
+        result.append(tuple(found[at : at + 2]) if pair else found[at])
+        at += 2 if pair else 1
+    return result + list(found[at:])
+
+
+def add_rows(sc, terms, split):
+    def kernel(*refs):
+        refs[-1][...] = sum(ref[...].astype(F32) for ref in refs[:-1]).astype(BF)
+
+    return rows_call(kernel, [[BF] if split else BF], sc, terms, [])[0]
+
+
+def unit_rows(values):
+    inverse = lax.rsqrt(jnp.mean(values * values, axis=-1, keepdims=True) + EPSILON)
+    return values * inverse, inverse
+
+
+def norm_call(sc, terms, gain):
+    def kernel(*refs):
+        gain_ref, sum_ref, out_ref = refs[-3:]
+        total = sum(ref[...].astype(F32) for ref in refs[:-3])
+        sum_ref[...] = total
+        out_ref[...] = (unit_rows(total)[0] * gain_ref[...]).astype(BF)
+
+    return rows_call(kernel, [F32, [BF]], sc, terms, [gain])
+
+
+def norm_back_call(sc, base, values, terms, gain, low):
+    def kernel(base_ref, values_ref, *refs):
+        term_refs, gain_ref, outs = refs[: len(terms)], refs[len(terms)], refs[len(terms) + 1 :]
+        grad = sum(ref[...].astype(F32) for ref in term_refs)
+        unit, inverse = unit_rows(values_ref[...].astype(F32))
+        if low:
+            outs[-1][...] += jnp.sum(grad * unit, axis=0, keepdims=True)
+        scaled = grad * gain_ref[...]
+        out = base_ref[...].astype(F32) + inverse * (
+            scaled - unit * jnp.mean(scaled * unit, axis=-1, keepdims=True)
+        )
+        outs[0][...] = out
+        if low:
+            outs[1][...] = out.astype(BF)
+
+    return rows_call(kernel, [F32, [BF]] if low else [F32], sc, [base, values, *terms], [gain], sums=1 if low else 0)
+
+
+def pair_call(sc, parts):
+    half, C, _ = parts[0][0].shape
+    widths = [near.shape[2] for _, near in parts]
+    N = sum(widths)
+
+    def kernel(s, *refs):
+        at = 0
+        for p, width in enumerate(widths):
+            total = refs[2 * p][0].astype(F32) + refs[2 * p + 1][0].astype(F32)
+            refs[-1][:, at : at + width] = total.astype(BF)
+            at += width
+
+    return call(
+        kernel,
+        shape((half * C, N), BF),
+        (half,),
+        [pl.BlockSpec((1, C, width), lambda i, s: (i, 0, 0)) for width in widths for _ in range(2)],
+        pl.BlockSpec((C, N), lambda i, s: (i, 0)),
+        (half * C * N, 6 * half * C * N),
+    )(sc, *[x for part in parts for x in part])
+
+
+def stage(refs, x_ref):
+    @pl.when(pl.program_id(0) == 0)
+    def _():
+        at = 0
+        for ref in refs:
+            x_ref[at : at + ref.shape[0]] = ref[...]
+            at += ref.shape[0]
+
+
+def staged(block):
+    H, D = block[0].shape
+    return [pl.BlockSpec((H, D), lambda c, s: (0, 0), pipeline_mode=pl.Buffered(1))] * 4, pltpu.VMEM((4 * H, D), BF)
+
+
+def put_rows(refs, value):
+    at = 0
+    for ref in refs:
+        ref[...] = value[at : at + ref.shape[0]].astype(BF)
+        at += ref.shape[0]
+
 
 def whole(dims):
     return pl.BlockSpec(dims, lambda *_: (0,) * len(dims), pipeline_mode=pl.Buffered(1))
@@ -75,30 +277,32 @@
     return lax.rem(s[CHIP] + j, chips)
 
 
-def qkv_call(sc, j, chips, xa, xb, wq, wk, wv, prev):
-    R, D = xa.shape
+def qkv_call(sc, j, chips, block, wq, wk, wv, prev):
+    R, D = 2 * block[0].shape[0], block[0].shape[1]
     E = wq.shape[1]
     T = 2 * R * chips
     n = min(256, E)
 
-    def kernel(s, xa_ref, xb_ref, wq_ref, wk_ref, wv_ref, *rest):
-        q_ref, k_ref, v_ref, c_ref = rest[-4:]
+    def kernel(s, *refs):
+        wq_ref, wk_ref, wv_ref = refs[4:7]
+        q_ref, k_ref, v_ref, c_ref, x_ref = refs[-5:]
+        stage(refs[:4], x_ref)
         base = chip_block(s, j, chips) * 2 * R
         sums = jnp.zeros((1, n), F32)
-        for i, x_ref in enumerate((xa_ref, xb_ref)):
+        x = x_ref[...]
+        q, k, v = (dot(x, ref[...]).astype(BF) for ref in (wq_ref, wk_ref, wv_ref))
+        for i in range(2):
             off = pl.multiple_of((s[CORE] if i == 0 else 1 - s[CORE]) * R, R)
-            rows = pl.ds(off, R)
-            x = x_ref[...]
-            q_ref[rows] = dot(x, wq_ref[...]).astype(BF)
-            v_ref[rows] = dot(x, wv_ref[...]).astype(BF)
-            k = dot(x, wk_ref[...]).astype(BF)
-            k_ref[rows] = k
-            k = k.astype(F32)
-            phi = jnp.where(row_ids(R, base + off) < s[VALID], phi_of(k, exp_low(k)), 0.0)
+            rows, part = pl.ds(off, R), slice(i * R, (i + 1) * R)
+            q_ref[rows] = q[part]
+            k_ref[rows] = k[part]
+            v_ref[rows] = v[part]
+            keys = k[part].astype(F32)
+            phi = jnp.where(row_ids(R, base + off) < s[VALID], phi_of(keys, exp_low(keys)), 0.0)
             sums = sums + jnp.sum(phi, axis=0, keepdims=True)
         c_ref[...] = sums
 
-    rows = pl.BlockSpec((R, D), lambda c, s: (0, 0))
+    rows, scratch = staged(block)
     cols = pl.BlockSpec((D, n), lambda c, s: (0, c))
     out = pl.BlockSpec((2 * R, n), lambda c, s: (chip_block(s, j, chips), c))
     o = shape((T, E), BF)
@@ -107,43 +311,48 @@
         kernel,
         (o, o, o, shape((1, E), F32)),
         (E // n,),
-        [rows, rows, cols, cols, cols] + extra,
+        rows + [cols, cols, cols] + extra,
         [out, out, out, pl.BlockSpec((1, n), lambda c, s: (0, c))],
         (12 * R * D * E, 4 * R * D + 6 * D * E + 12 * R * E),
-        alias={6: 0, 7: 1, 8: 2} if prev else None,
-    )(sc, xa, xb, wq, wk, wv, *(prev or ()))
-
-
-def grad_inner_call(sc, ca, cb, wd):
-    R, D = ca.shape
+        scratch=[scratch],
+        alias={8: 0, 9: 1, 10: 2} if prev else None,
+    )(sc, *block, wq, wk, wv, *(prev or ()))
+
+
+def grad_inner_call(sc, block, wd):
+    R, D = 2 * block[0].shape[0], block[0].shape[1]
     F = wd.shape[0]
     n = min(512, F)
 
-    def kernel(s, ca_ref, cb_ref, w_ref, o_ref):
-        o_ref[:R] = dot_nt(ca_ref[...], w_ref[...]).astype(BF)
-        o_ref[R:] = dot_nt(cb_ref[...], w_ref[...]).astype(BF)
-
-    rows = pl.BlockSpec((R, D), lambda c, s: (0, 0))
+    def kernel(s, *refs):
+        w_ref, o_ref, x_ref = refs[4:]
+        stage(refs[:4], x_ref)
+        o_ref[...] = dot_nt(x_ref[...], w_ref[...]).astype(BF)
+
+    rows, scratch = staged(block)
     return call(
         kernel,
         shape((2 * R, F), BF),
         (F // n,),
-        [rows, rows, pl.BlockSpec((n, D), lambda c, s: (c, 0))],
+        rows + [pl.BlockSpec((n, D), lambda c, s: (c, 0))],
         pl.BlockSpec((2 * R, n), lambda c, s: (0, c)),
         (4 * R * D * F, 4 * R * D + 2 * D * F + 4 * R * F),
-    )(sc, ca, cb, wd)
-
-
-def ffn_a_call(sc, xa, xb, wg, wu, gi):
-    R, D = xa.shape
+        scratch=[scratch],
+    )(sc, *block, wd)
+
+
+def ffn_a_call(sc, block, wg, wu, gi):
+    R, D = 2 * block[0].shape[0], block[0].shape[1]
     F = wg.shape[1]
     n = min(512, F)
 
-    def kernel(s, xa_ref, xb_ref, wg_ref, wu_ref, gi_ref, inner_ref, gg_ref, gu_ref):
-        for i, x_ref in enumerate((xa_ref, xb_ref)):
+    def kernel(s, *refs):
+        wg_ref, wu_ref, gi_ref, inner_ref, gg_ref, gu_ref, x_ref = refs[4:]
+        stage(refs[:4], x_ref)
+        for i in range(2):
             rows = slice(i * R, (i + 1) * R)
-            g = dot(x_ref[...], wg_ref[...])
-            u = dot(x_ref[...], wu_ref[...])
+            g = dot(x_ref[rows], wg_ref[...])
+            u = dot(x_ref[rows], wu_ref[...])
             sig = 0.5 * jnp.tanh(0.5 * g) + 0.5
             silu = g * sig
             inner_ref[rows] = (silu * u).astype(BF)
@@ -152,17 +361,23 @@
             gg_ref[rows] = (gi_rows * u * (sig + silu * (1.0 - sig))).astype(BF)
 
     o = shape((2 * R, F), BF)
-    rows = pl.BlockSpec((R, D), lambda c, s: (0, 0))
+    rows, scratch = staged(block)
     cols = pl.BlockSpec((D, n), lambda c, s: (0, c))
     out = pl.BlockSpec((2 * R, n), lambda c, s: (0, c))
     return call(
         kernel,
         (o, o, o),
         (F // n,),
-        [rows, rows, cols, cols, out],
+        rows + [cols, cols, out],
         [out, out, out],
         (8 * R * D * F, 4 * R * D + 4 * D * F + 16 * R * F),
-    )(sc, xa, xb, wg, wu, gi)
+        scratch=[scratch],
+    )(sc, *block, wg, wu, gi)
+
+
+def halves_out(R, D, n):
+    H = R // 2
+    return (shape((H, D), BF),) * 4, [pl.BlockSpec((H, n), lambda c, s: (0, c))] * 4
 
 
 def ffn_b_call(sc, gg, gu, wg, wu):
@@ -171,23 +386,18 @@
     D = wg.shape[0]
     n = min(512, D)
 
-    def kernel(s, gg_ref, gu_ref, wg_ref, wu_ref, oa_ref, ob_ref):
-        for i, o_ref in enumerate((oa_ref, ob_ref)):
-            rows = slice(i * R, (i + 1) * R)
-            o_ref[...] = (
-                dot_nt(gg_ref[rows], wg_ref[...]) + dot_nt(gu_ref[rows], wu_ref[...])
-            ).astype(BF)
-
-    o = shape((R, D), BF)
+    def kernel(s, gg_ref, gu_ref, wg_ref, wu_ref, *outs):
+        put_rows(outs, dot_nt(gg_ref[...], wg_ref[...]) + dot_nt(gu_ref[...], wu_ref[...]))
+
     rows = pl.BlockSpec((R2, F), lambda c, s: (0, 0))
     cols = pl.BlockSpec((n, F), lambda c, s: (c, 0))
-    out = pl.BlockSpec((R, n), lambda c, s: (0, c))
-    return call(
-        kernel,
-        (o, o),
+    shapes, specs = halves_out(R, D, n)
+    return call(
+        kernel,
+        shapes,
         (D // n,),
         [rows, rows, cols, cols],
-        [out, out],
+        specs,
         (8 * R * D * F, 8 * R * F + 4 * D * F + 4 * R * D),
     )(sc, gg, gu, wg, wu)
 
@@ -198,60 +408,73 @@
     D = wd.shape[1]
     n = min(512, D)
 
-    def kernel(s, x_ref, w_ref, oa_ref, ob_ref):
-        oa_ref[...] = dot(x_ref[:R], w_ref[...]).astype(BF)
-        ob_ref[...] = dot(x_ref[R:], w_ref[...]).astype(BF)
-
-    o = shape((R, D), BF)
-    out = pl.BlockSpec((R, n), lambda c, s: (0, c))
-    return call(
-        kernel,
-        (o, o),
+    def kernel(s, x_ref, w_ref, *outs):
+        put_rows(outs, dot(x_ref[...], w_ref[...]))
+
+    shapes, specs = halves_out(R, D, n)
+    return call(
+        kernel,
+        shapes,
         (D // n,),
         [pl.BlockSpec((R2, F), lambda c, s: (0, 0)), pl.BlockSpec((F, n), lambda c, s: (0, c))],
-        [out, out],
+        specs,
         (4 * R * D * F, 4 * R * F + 2 * D * F + 4 * R * D),
     )(sc, inner, wd)
 
 
-def wgrad_call(sc, xs, gs, ndp):
-    R, D = xs[0].shape
+def wgrad_call(sc, blocks, gs, ndp, pieces):
+    xs = [x for block in blocks for x in block]
+    H, D = xs[0].shape
     nx = len(xs)
     C = D // ndp
     nb = len(gs[0])
-    widths = [blocks[0].shape[1] for blocks in gs]
-    T = R * nx
+    widths = [parts[0].shape[1] for parts in gs]
+    T = H * nx
     rb = T // nb
     N = sum(widths)
+    flat = [g for parts in gs for g in parts]
+    far = ndp // 2 if pieces else 0
+    sizes = [far // max(pieces, 1)] * pieces + [ndp - far]
+    begins = [p * sizes[0] for p in range(len(sizes))]
 
     def kernel(s, *refs):
-        x_refs, g_refs, (o_ref, xt) = refs[:nx], refs[nx:-2], refs[-2:]
+        x_refs, g_refs, o_refs, xt = refs[:nx], refs[nx : nx + len(flat)], refs[nx + len(flat) : -1], refs[-1]
+        j = pl.program_id(0)
         for p in range(nx):
-            xt[:, p * R : (p + 1) * R] = x_refs[p][...].T
+            xt[:, p * H : (p + 1) * H] = x_refs[p][...].T
         at = 0
         for w, width in enumerate(widths):
             acc = None
             for b in range(nb):
                 term = dot(xt[:, b * rb : (b + 1) * rb], g_refs[w * nb + b][...])
                 acc = term if acc is None else acc + term
-            o_ref[0, :, at : at + width] = acc.astype(BF)
+            cols = slice(at, at + width)
             at += width
-
-    flat = [g for blocks in gs for g in blocks]
-    return call(
-        kernel,
-        shape((ndp, C, N), BF),
+            low = acc.astype(BF)
+            for o_ref, begin, size in zip(o_refs, begins, sizes):
+
+                @pl.when((j >= begin) & (j < begin + size))
+                def _():
+                    o_ref[0, :, cols] = low
+
+    def spec(begin, size):
+        return pl.BlockSpec((1, C, N), lambda j, s: (jnp.clip(j - begin, 0, size - 1), 0, 0))
+
+    order = (lambda j, s: (0, s[ORDER + j])) if pieces else (lambda j, s: (0, j))
+    return call(
+        kernel,
+        tuple(shape((size, C, N), BF) for size in sizes),
         (ndp,),
-        [pl.BlockSpec((R, C), lambda j, s: (0, s[ORDER + j]))] * nx + [whole(g.shape) for g in flat],
-        pl.BlockSpec((1, C, N), lambda j, s: (j, 0, 0)),
+        [pl.BlockSpec((H, C), order)] * nx + [whole(g.shape) for g in flat],
+        [spec(begin, size) for begin, size in zip(begins, sizes)],
         (2 * T * D * N, 2 * T * (D + N) + 2 * D * N),
         scratch=[pltpu.VMEM((C, T), BF)],
     )(sc, *xs, *flat)
 
 
-def attn_fwd_call(sc, q, k, v):
-    T, E = q.shape
-    hh = E // HEAD
+def attn_fwd_call(sc, q, k, v, h0, hh):
+    T = q.shape[0]
+    E = hh * HEAD
     B = min(512, T)
     nb = T // B
     c = HEAD**-0.5 * LOG2E
@@ -283,18 +506,21 @@
             o_ref[i * B : (i + 1) * B] = (acc * (1.0 / total)).T
             lse_ref[0, :, i * B : (i + 1) * B] = top + jnp.log2(total)
 
-    head = pl.BlockSpec((T, HEAD), lambda h, s: (0, h))
+    head = pl.BlockSpec((T, HEAD), lambda h, s: (0, h0 + h))
+    out = pl.BlockSpec((T, HEAD), lambda h, s: (0, h))
     return call(
         kernel,
         (shape((T, E), F32), shape((hh, 1, T), F32)),
         (hh,),
         [head, head, head],
-        [head, pl.BlockSpec((1, 1, T), lambda h, s: (h, 0, 0))],
+        [out, pl.BlockSpec((1, 1, T), lambda h, s: (h, 0, 0))],
         (6 * T * T * E, 10 * T * E),
     )(sc, q, k, v)
 
 
-def attn_bwd_call(sc, q, k, v, do, lo, lse, h0, nh):
+def attn_bwd_call(sc, q, k, v, do, attended, h0, part):
+    lo, lse = attended
+    nh = 1
     T = q.shape[0]
     B = min(512, T)
     nb = T // B
@@ -346,7 +572,8 @@
         kernel,
         (o, o, o),
         (nh,),
-        [head] * 5 + [pl.BlockSpec((1, 1, T), lambda h, s: (h0 + h, 0, 0))],
+        [head] * 4
+        + [pl.BlockSpec((T, HEAD), lambda h, s: (0, part)), pl.BlockSpec((1, 1, T), lambda h, s: (part, 0, 0))],
         [out, out, out],
         (12 * T * T * HEAD * nh, 26 * T * HEAD * nh),
         scratch=[pltpu.VMEM((8, T), F32)],
@@ -362,7 +589,7 @@
         h = pl.program_id(0)
         norm = jnp.zeros((1, HEAD), F32)
         for a in range(ndp - 1):
-            after = (norm + g_ref[a, pl.ds(h, 1)]) * g_ref[a + 1, hh : hh + 1]
+            after = (norm + g_ref[shared_at(s, a, ndp), pl.ds(h, 1)]) * g_ref[shared_at(s, a + 1, ndp), hh : hh + 1]
             norm = jnp.where(a < s[PLACE], after, norm)
         norm_ref[0] = norm
         k = k_ref[...].astype(F32)
@@ -397,7 +624,7 @@
     def kernel(s, g_ref, maps_ref, m_ref):
         state = [jnp.zeros((HEAD, HEAD), F32) for _ in range(hh)]
         for a in range(ndp - 1):
-            keep = g_ref[a + 1, hh : hh + 1]
+            keep = g_ref[shared_at(s, a + 1, ndp), hh : hh + 1]
             before = a < s[PLACE]
             for h in range(hh):
                 after = state[h] - times_state(maps_ref[a, 0, h], state[h])
@@ -416,14 +643,19 @@
     )(sc, gathered, maps)
 
 
-def mixout_call(sc, j, chips, q, local, memory, norm, mix, wo):
+def mixout_call(sc, j, chips, q, locals_, memory, norm, mix, wo):
     T, E = q.shape
     hh = E // HEAD
     D = wo.shape[1]
     R = T // chips // 2
     n = min(512, D)
-
-    def kernel(s, q_ref, l_ref, m_ref, n_ref, mix_ref, w_ref, oa_ref, ob_ref, mixed_ref, diff_ref):
+    groups = len(locals_)
+    per = hh // groups
+
+    def kernel(s, q_ref, *rest):
+        l_refs = rest[:groups]
+        m_ref, n_ref, mix_ref, w_ref, *outs, mixed_ref, diff_ref = rest[groups:]
+
         @pl.when(pl.program_id(0) == 0)
         def _():
             for i in range(2):
@@ -434,42 +666,46 @@
                     phi = phi_of(qv, exp_low(qv))
                     den = jnp.maximum(jnp.sum(phi * n_ref[h], axis=1, keepdims=True), 1.0)
                     read = dot(phi.astype(BF), m_ref[h].astype(BF)) * (1.0 / den)
-                    diff = read - l_ref[pl.ds(off, R), cols]
-                    mixed = l_ref[pl.ds(off, R), cols] + mix_ref[h] * diff
+                    local = l_refs[h // per][pl.ds(off, R), h % per * HEAD : (h % per + 1) * HEAD]
+                    diff = read - local
+                    mixed = local + mix_ref[h] * diff
                     diff_ref[i * R : (i + 1) * R, cols] = diff.astype(BF)
                     mixed_ref[i * R : (i + 1) * R, cols] = mixed.astype(BF)
 
-        oa_ref[...] = dot(mixed_ref[:R], w_ref[...]).astype(BF)
-        ob_ref[...] = dot(mixed_ref[R:], w_ref[...]).astype(BF)
+        put_rows(outs, dot(mixed_ref[...], w_ref[...]))
 
     rows = pl.BlockSpec((2 * R, E), lambda c, s: (chip_block(s, j, chips), 0))
-    out = pl.BlockSpec((R, n), lambda c, s: (0, c))
+    shapes, specs = halves_out(R, D, n)
     rel = pl.BlockSpec((2 * R, E), lambda c, s: (0, 0))
     return call(
         kernel,
-        (shape((R, D), BF), shape((R, D), BF), shape((2 * R, E), BF), shape((2 * R, E), BF)),
+        shapes + (shape((2 * R, E), BF), shape((2 * R, E), BF)),
         (D // n,),
-        [rows, rows, whole(memory.shape), whole(norm.shape), whole(mix.shape), pl.BlockSpec((E, n), lambda c, s: (0, c))],
-        [out, out, rel, rel],
+        [rows]
+        + [pl.BlockSpec((2 * R, per * HEAD), lambda c, s: (chip_block(s, j, chips), 0))] * groups
+        + [whole(memory.shape), whole(norm.shape), whole(mix.shape), pl.BlockSpec((E, n), lambda c, s: (0, c))],
+        specs + [rel, rel],
         (4 * R * E * D + 8 * R * E * HEAD, 20 * R * E + 2 * E * D + 4 * R * D),
-    )(sc, q, local, memory, norm, mix, wo)
-
-
-def gradmix_call(sc, j, chips, ya, yb, wo, diff, q, norm, mix, prev):
-    R, D = ya.shape
+    )(sc, q, *locals_, memory, norm, mix, wo)
+
+
+def gradmix_call(sc, j, chips, block, wo, diff, q, norm, mix, prev):
+    R, D = 2 * block[0].shape[0], block[0].shape[1]
     E = wo.shape[0]
     hh = E // HEAD
     T = 2 * R * chips
     n = min(256, E)
     per = n // HEAD
 
-    def kernel(s, ya_ref, yb_ref, w_ref, diff_ref, q_ref, n_ref, mix_ref, *rest):
-        do_ref, gm_ref, cot_ref, b_ref = rest[-4:]
+    def kernel(s, *refs):
+        w_ref, diff_ref, q_ref, n_ref, mix_ref = refs[4:9]
+        do_ref, gm_ref, cot_ref, b_ref, x_ref = refs[-5:]
+        stage(refs[:4], x_ref)
         sums = jnp.zeros((1, n), F32)
         cots = [jnp.zeros((HEAD, HEAD), F32) for _ in range(per)]
-        for i, y_ref in enumerate((ya_ref, yb_ref)):
+        for i in range(2):
             off = pl.multiple_of((s[CORE] if i == 0 else 1 - s[CORE]) * R, R)
-            grad = dot_nt(y_ref[...], w_ref[...])
+            grad = dot_nt(x_ref[i * R : (i + 1) * R], w_ref[...])
             sums = sums + jnp.sum(grad * diff_ref[i * R : (i + 1) * R].astype(F32), axis=0, keepdims=True)
             for h in range(per):
                 cols = slice(h * HEAD, (h + 1) * HEAD)
@@ -485,7 +721,7 @@
             cot_ref[h] = cots[h]
         b_ref[...] = sums
 
-    rows = pl.BlockSpec((R, D), lambda c, s: (0, 0))
+    rows, scratch = staged(block)
     place = pl.BlockSpec((2 * R, n), lambda c, s: (chip_block(s, j, chips), c))
     per_head = pl.BlockSpec((per, 1, HEAD), lambda c, s: (c, 0, 0))
     o = shape((T, E), BF)
@@ -494,11 +730,14 @@
         kernel,
         (o, o, shape((hh, HEAD, HEAD), F32), shape((1, E), F32)),
         (E // n,),
-        [rows, rows, pl.BlockSpec((n, D), lambda c, s: (c, 0)), pl.BlockSpec((2 * R, n), lambda c, s: (0, c)), place, per_head, per_head] + extra,
+        rows
+        + [pl.BlockSpec((n, D), lambda c, s: (c, 0)), pl.BlockSpec((2 * R, n), lambda c, s: (0, c)), place, per_head, per_head]
+        + extra,
         [place, place, pl.BlockSpec((per, HEAD, HEAD), lambda c, s: (c, 0, 0)), pl.BlockSpec((1, n), lambda c, s: (0, c))],
         (4 * R * E * D + 4 * R * E * HEAD, 4 * R * D + 2 * E * D + 16 * R * E),
-        alias={8: 0, 9: 1} if prev else None,
-    )(sc, ya, yb, wo, diff, q, norm, mix, *(prev or ()))
+        scratch=[scratch],
+        alias={10: 0, 11: 1} if prev else None,
+    )(sc, *block, wo, diff, q, norm, mix, *(prev or ()))
 
 
 def memory_rows(q, k, grad_read, live, memory, norm, cot):
@@ -528,8 +767,8 @@
     def kernel(s, g_ref, maps_ref, cots_ref, q_ref, k_ref, gm_ref, m_ref, n_ref, x_ref, nb_ref):
         cot = jnp.zeros((HEAD, HEAD), F32)
         for a in range(ndp - 1, 0, -1):
-            before = cot - times_state(maps_ref[a, 0, 0], cot) + cots_ref[a, 0].astype(F32)
-            cot = jnp.where(a > s[PLACE], before * g_ref[a, hh : hh + 1], cot)
+            before = cot - times_state(maps_ref[a, 0, 0], cot) + cots_ref[shared_at(s, a, ndp), 0].astype(F32)
+            cot = jnp.where(a > s[PLACE], before * g_ref[shared_at(s, a, ndp), hh : hh + 1], cot)
         x_ref[0] = cot
         cot = cot.astype(BF)
         memory = m_ref[0].astype(BF)
@@ -584,7 +823,8 @@
             dq, dk, dv = (ref[:, part] for ref in local_refs[3 * (h // per) : 3 * (h // per) + 3])
             norm_cot = jnp.zeros((1, HEAD), F32)
             for a in range(ndp - 1, 0, -1):
-                before = (norm_cot + nb_ref[a, h : h + 1]) * g_ref[a, hh : hh + 1]
+                other = shared_at(s, a, ndp)
+                before = (norm_cot + nb_ref[other, h : h + 1]) * g_ref[other, hh : hh + 1]
                 norm_cot = jnp.where(a > s[PLACE], before, norm_cot)
             memory = m_ref[h].astype(BF)
             cot = x_ref[h].astype(BF)
@@ -621,64 +861,47 @@
     )(sc, q, k, v, grad_read, *[x for group in local_grads for x in group], memory, norm, cot, gathered, norm_parts)
 
 
-def grad_normed_call(sc, j, gq, gk, gv, wq, wk, wv, chips):
+def grad_normed_call(sc, j, gq, gk, gv, wq, wk, wv, block, chips):
     T, E = gq.shape
     R = T // chips // 2
     D = wq.shape[0]
     n = min(512, D)
 
-    def kernel(s, gq_ref, gk_ref, gv_ref, wq_ref, wk_ref, wv_ref, oa_ref, ob_ref):
-        for i, o_ref in enumerate((oa_ref, ob_ref)):
-            rows = slice(i * R, (i + 1) * R)
-            o_ref[...] = (
-                dot_nt(gq_ref[rows], wq_ref[...]) + dot_nt(gk_ref[rows], wk_ref[...]) + dot_nt(gv_ref[rows], wv_ref[...])
-            ).astype(BF)
-
-    o = shape((R, D), BF)
+    def kernel(s, gq_ref, gk_ref, gv_ref, wq_ref, wk_ref, wv_ref, *rest):
+        grad = dot_nt(gq_ref[...], wq_ref[...]) + dot_nt(gk_ref[...], wk_ref[...]) + dot_nt(gv_ref[...], wv_ref[...])
+        put_rows(rest[4:8], grad)
+        sums, at = 0.0, 0
+        for ref in rest[:4]:
+            part = grad[at : at + ref.shape[0]] * ref[...].astype(F32)
+            sums = sums + jnp.sum(part, axis=0, keepdims=True)
+            at += ref.shape[0]
+        rest[8][...] = sums
+
     rows = pl.BlockSpec((2 * R, E), lambda c, s: (j, 0))
     cols = pl.BlockSpec((n, E), lambda c, s: (c, 0))
-    out = pl.BlockSpec((R, n), lambda c, s: (0, c))
-    return call(
-        kernel,
-        (o, o),
+    shapes, specs = halves_out(R, D, n)
+    return call(
+        kernel,
+        shapes + (shape((1, D), F32),),
         (D // n,),
-        [rows, rows, rows, cols, cols, cols],
-        [out, out],
+        [rows, rows, rows, cols, cols, cols] + specs,
+        specs + [pl.BlockSpec((1, n), lambda c, s: (0, c))],
         (12 * R * D * E, 12 * R * E + 6 * D * E + 4 * R * D),
-    )(sc, gq, gk, gv, wq, wk, wv)
-
-
-def swap_core(x):
-    return lax.ppermute(x, "tensor", [(i, i ^ 1) for i in range(lax.axis_size("tensor"))])
-
-
-def shift_chip(x, j):
+    )(sc, gq, gk, gv, wq, wk, wv, *block)
+
+
+def swap_core(pair):
     count = lax.axis_size("tensor")
-    return lax.ppermute(x, "tensor", [(i, (i + 2 * j) % count) for i in range(count)])
-
-
-def after(x, *others):
-    return lax.optimization_barrier((x, *others))[0]
-
-
-def gather_rows(x, chips, wait=None):
-    blocks = [(x, swap_core(x))]
-    far = x if wait is None else after(x, wait)
-    for j in range(1, chips):
-        moved = shift_chip(far, -j)
-        blocks.append((moved, swap_core(moved)))
-    return blocks
-
-
-def scatter_rows(blocks, wait=None):
-    sums = [mine.astype(F32) + swap_core(other).astype(F32) for mine, other in blocks]
-    total = sums[0]
-    for j in range(1, len(blocks)):
-        low = sums[j].astype(BF)
-        if wait is not None:
-            low = after(low, wait)
-        total = total + shift_chip(low, j).astype(F32)
-    return total
+    return tuple(lax.ppermute(x, "tensor", [(i, i ^ 1) for i in range(count)]) for x in pair)
+
+
+def shift_chip(pair, j):
+    count = lax.axis_size("tensor")
+    return tuple(lax.ppermute(x, "tensor", [(i, (i + 2 * j) % count) for i in range(count)]) for x in pair)
+
+
+def with_swapped(pair):
+    return tuple(pair) + swap_core(pair)
 
 
 def chunk_order(me, ndp):
@@ -687,14 +910,38 @@
     return jnp.stack(order)
 
 
-def sum_over_dp(grads):
-    ndp = grads.shape[0]
-    half = ndp // 2
-    got = lax.ppermute(grads[:half], "dp", [(i, i ^ 1) for i in range(ndp)])
-    pair = (got.astype(F32) + grads[half:].astype(F32)).astype(BF)
+def exchange_x(x):
+    return lax.ppermute(x, "dp", [(i, i ^ 1) for i in range(lax.axis_size("dp"))])
+
+
+def sum_z(x):
+    ndp = lax.axis_size("dp")
     groups = [list(range(0, ndp, 2)), list(range(1, ndp, 2))]
-    out = lax.psum_scatter(pair.reshape((-1, grads.shape[2])), "dp", scatter_dimension=0, axis_index_groups=groups, tiled=True)
-    return out.astype(F32)
+    return lax.psum_scatter(x, "dp", scatter_dimension=0, axis_index_groups=groups, tiled=True)
+
+
+def finish_x(both, parity):
+    C = both.shape[0] // 2
+    got = exchange_x(lax.dynamic_slice_in_dim(both, (1 - parity) * C, C, 0))
+    return got.astype(F32) + lax.dynamic_slice_in_dim(both, parity * C, C, 0).astype(F32)
+
+
+def share_steps(x):
+    count = lax.axis_size("dp")
+    steps = [1 << bit for bit in range(1, count.bit_length() - 1)] + [1]
+    x = x[None]
+    for step in steps:
+        x = jnp.concatenate([x, lax.ppermute(x, "dp", [(i, i ^ step) for i in range(count)])])
+        yield x
+
+
+def shared_at(s, a, count):
+    apart = a ^ s[PLACE]
+    return (apart >> 1) + (apart & 1) * (count // 2)
+
+
+def share_over_dp(x):
+    return list(share_steps(x))[-1]
 
 
 def sum_everywhere(x):
@@ -740,112 +987,160 @@
     sig_bias = jax.nn.sigmoid(gate_bias)
     mix = jnp.broadcast_to(sig_bias[:, None, None], (hh, 1, HEAD))
 
-    x = tokens.astype(F32)
-    inv1 = lax.rsqrt(jnp.mean(x * x, axis=-1, keepdims=True) + EPSILON)
-    normed1 = (x * inv1 * gain1).astype(BF)
-    rows1 = gather_rows(normed1, chips)
-    qkv = None
-    sums = 0.0
-    for j, (a, b) in enumerate(rows1):
-        *qkv, column_sums = qkv_call(sc, j, chips, a, b, w_query, w_key, w_value, qkv)
+    ORDERED.clear()
+    per = max(1, hh // 2)
+
+    gain1 = gain1[None]
+    gain2 = gain2[None]
+    chip_range = range(1, chips)
+    parity = place % 2
+    R = tokens.shape[0]
+    four = min(4, ndp // 2)
+
+    def norm1_kernel(x_ref, g_ref, o_ref):
+        o_ref[...] = (unit_rows(x_ref[...].astype(F32))[0] * g_ref[...]).astype(BF)
+
+    normed1 = rows_call(norm1_kernel, [[BF]], sc, [tokens], [gain1])[0]
+    rows1 = [with_swapped(normed1)]
+    far1 = [shift_chip(normed1, -j) for j in chip_range]
+    own_cot = (cotangent[: R // 2], cotangent[R // 2 :])
+    cot_rows = [with_swapped(own_cot)]
+    *qkv, sums = qkv_call(sc, 0, chips, rows1[0], w_query, w_key, w_value, None)
+    *far1, own_cot = hold_pairs(sc, far1 + [own_cot])
+    far_cot = [shift_chip(own_cot, -j) for j in chip_range]
+    for j in chip_range:
+        rows1.append(with_swapped(far1[j - 1]))
+        *qkv, column_sums = qkv_call(sc, j, chips, rows1[j], w_query, w_key, w_value, qkv)
         sums = sums + column_sums
     q, k, v = qkv
-    cot_rows = gather_rows(cotangent, chips, wait=rows1[-1][0])
 
     own = jnp.concatenate([sums.reshape(hh, HEAD), jnp.full((8 - hh, HEAD), keep, F32)])
-    gathered = lax.all_gather(own, "dp")
+    gathered = share_over_dp(own)
     maps, norm = maps_call(sc, k, v, gathered)
     all_maps = lax.all_gather(maps, "dp")
-    local, lse = attn_fwd_call(sc, q, k, v)
+    attended = [attn_fwd_call(sc, q, k, v, h, per) for h in range(0, hh, per)]
+    far_cot = hold_pairs(sc, far_cot)
+    cot_rows += [with_swapped(pair) for pair in far_cot]
+    grad_inner = [grad_inner_call(sc, block, w_down) for block in cot_rows]
     memory = chain_call(sc, gathered, all_maps)
 
-    grad_inner = [grad_inner_call(sc, a, b, w_down) for a, b in cot_rows]
-    partial, mixed, diff = [None] * chips, [None] * chips, [None] * chips
-    for j in reversed(range(chips)):
-        a, b, mixed[j], diff[j] = mixout_call(sc, j, chips, q, local, memory, norm, mix, w_out)
-        partial[j] = (a, b)
-    hidden = x + scatter_rows(partial)
-    inv2 = lax.rsqrt(jnp.mean(hidden * hidden, axis=-1, keepdims=True) + EPSILON)
-    unit2 = hidden * inv2
-    normed2 = (unit2 * gain2).astype(BF)
-    rows2 = gather_rows(normed2, chips)
-
-    inner, grad_gate, grad_up = [], [], []
-    for (a, b), gi in zip(rows2, grad_inner):
-        one, two, three = ffn_a_call(sc, a, b, w_gate, w_up, gi)
-        inner.append(one)
-        grad_gate.append(two)
-        grad_up.append(three)
-    back = [None] * chips
-    for j in reversed(range(chips)):
-        back[j] = ffn_b_call(sc, grad_gate[j], grad_up[j], w_gate, w_up)
-    grad_normed2 = scatter_rows(back)
-    flat_rows2 = [piece for block in rows2 for piece in block]
-    flat_cot = [piece for block in cot_rows for piece in block]
-    grad_down = sum_over_dp(wgrad_call(sc, flat_cot, [inner], ndp))
-    grad_gate_up = sum_over_dp(wgrad_call(sc, flat_rows2, [grad_gate, grad_up], ndp))
-
-    gain2_part = jnp.sum(grad_normed2 * unit2, axis=0)
-    scaled2 = grad_normed2 * gain2
-    grad_hidden = cotangent.astype(F32) + inv2 * (
-        scaled2 - unit2 * jnp.mean(scaled2 * unit2, axis=-1, keepdims=True)
-    )
-    grad_rows = gather_rows(grad_hidden.astype(BF), chips)
-    grads = None
-    cot_part, bias_part = 0.0, 0.0
-    for j, (a, b) in enumerate(grad_rows):
-        *grads, cot_j, bias_j = gradmix_call(sc, j, chips, a, b, w_out, diff[j], q, norm, mix, grads)
+    mixed, diff = [None] * chips, [None] * chips
+
+    def mixout(j):
+        *block, mixed[j], diff[j] = mixout_call(sc, j, chips, q, [one[0] for one in attended], memory, norm, mix, w_out)
+        return block
+
+    def scatter(make):
+        blocks = [make(j) for j in chip_range] + [make(0)]
+        got = []
+        for j in chip_range:
+            block = blocks[j - 1]
+            sums = add_rows(sc, [tuple(block[:2]), swap_core(block[2:])], True)
+            got.append(shift_chip(sums, j))
+        block = blocks[-1]
+        return [tuple(block[:2]), swap_core(block[2:]), *got]
+
+    hidden, normed2 = norm_call(sc, [tokens, *scatter(mixout)], gain2)
+    rows2 = [with_swapped(normed2)]
+    far2 = [shift_chip(normed2, -j) for j in chip_range]
+    ffn = [ffn_a_call(sc, rows2[0], w_gate, w_up, grad_inner[0])]
+    far2 = hold_pairs(sc, far2)
+    for j in chip_range:
+        rows2.append(with_swapped(far2[j - 1]))
+        ffn.append(ffn_a_call(sc, rows2[j], w_gate, w_up, grad_inner[j]))
+    inner, grad_gate, grad_up = zip(*ffn)
+
+    (w_up_parts,) = wgrad_call(sc, rows2, [grad_up], ndp, 0)
+    both_up = sum_z(w_up_parts.reshape((-1, w_up_parts.shape[2])))
+    back = scatter(lambda j: ffn_b_call(sc, grad_gate[j], grad_up[j], w_gate, w_up))
+    far_gate, near_gate = wgrad_call(sc, rows2, [grad_gate], ndp, 1)
+    far_gate = exchange_x(far_gate)
+    far_down, near_down = wgrad_call(sc, cot_rows, [inner], ndp, 1)
+    far_down = exchange_x(far_down)
+    grad_hidden, grad_low, gain2_part = norm_back_call(sc, cotangent, hidden, back, gain2, True)
+    grad_rows = [with_swapped(grad_low)]
+    far_grad = [shift_chip(grad_low, -j) for j in chip_range]
+    down_far = [down_call(sc, inner[j], w_down) for j in chip_range]
+    *grads, cot_part, bias_part = gradmix_call(sc, 0, chips, grad_rows[0], w_out, diff[0], q, norm, mix, None)
+    down_near = down_call(sc, inner[0], w_down)
+    far_grad = hold_pairs(sc, far_grad)
+    pair_gate = pair_call(sc, [(far_gate, near_gate)])
+    sum_gate = sum_z(pair_gate)
+    require(both_up)
+    sum_up = finish_x(both_up, parity)
+    for j in chip_range:
+        grad_rows.append(with_swapped(far_grad[j - 1]))
+        *grads, cot_j, bias_j = gradmix_call(sc, j, chips, grad_rows[j], w_out, diff[j], q, norm, mix, grads)
         cot_part = cot_part + cot_j
         bias_part = bias_part + bias_j
+    down_blocks = iter(down_far + [down_near])
+    down = scatter(lambda j: next(down_blocks))
     grad_local, grad_read = grads
-    all_cots = lax.all_gather(cot_part.astype(BF), "dp")
-
-    down = [down_call(sc, block, w_down) for block in inner]
-    output = (hidden + scatter_rows(down, wait=grad_rows[-1][0])).astype(BF)
-    flat_grad = [piece for block in grad_rows for piece in block]
-    grad_out = sum_over_dp(wgrad_call(sc, flat_grad, [mixed], ndp))
-
-    per = max(1, hh // 2)
-    local_grads = [
-        attn_bwd_call(sc, q, k, v, grad_local, local, lse, h, per) for h in range(0, hh, per)
-    ]
+
+    local_grads = []
+    steps = share_steps(cot_part.astype(BF))
+    all_cots = None
+    for h in range(hh):
+        local_grads.append(attn_bwd_call(sc, q, k, v, grad_local, attended[h // per], h, h % per))
+        if h in (0, max(2, hh - 2)):
+            all_cots = next(steps)
+            require(all_cots)
+    for all_cots in steps:
+        pass
+    far_out, near_out = wgrad_call(sc, grad_rows, [mixed], ndp, 1)
+    far_out = exchange_x(far_out)
+    pair_down = pair_call(sc, [(far_down, near_down)])
+    sum_down = sum_z(pair_down)
     memory_cot, norm_part = memory_cot_call(sc, gathered, all_maps, all_cots, q, k, grad_read, memory, norm)
-    norm_pad = jnp.concatenate([norm_part.reshape(hh, HEAD), jnp.zeros((8 - hh, HEAD), F32)])
-    norm_parts = lax.all_gather(norm_pad, "dp")
+    norm_parts = share_over_dp(jnp.concatenate([norm_part.reshape(hh, HEAD), jnp.zeros((8 - hh, HEAD), F32)]))
+    require(sum_gate)
     gq, gk, gv = combine_call(
         sc, chips, q, k, v, grad_read, local_grads, memory, norm, memory_cot, gathered, norm_parts
     )
-    flat_rows1 = [piece for block in rows1 for piece in block]
-    grad_qkv = sum_over_dp(wgrad_call(sc, flat_rows1, [[gq], [gk], [gv]], ndp))
-    back1 = [None] * chips
-    for j in reversed(range(chips)):
-        back1[j] = grad_normed_call(sc, j, gq, gk, gv, w_query, w_key, w_value, chips)
-    grad_normed1 = scatter_rows(back1)
-    unit1 = x * inv1
-    gain1_part = jnp.sum(grad_normed1 * unit1, axis=0)
-    scaled1 = grad_normed1 * gain1
-    grad_tokens = grad_hidden + inv1 * (
-        scaled1 - unit1 * jnp.mean(scaled1 * unit1, axis=-1, keepdims=True)
-    )
+    gain1_sums = []
+
+    def back_rows(j):
+        *block, sums = grad_normed_call(sc, j, gq, gk, gv, w_query, w_key, w_value, rows1[j], chips)
+        gain1_sums.append(sums)
+        return block
+
+    parts1 = {}
+
+    def make1(name, grad):
+        far, near = wgrad_call(sc, rows1, [[grad]], ndp, 1)
+        parts1[name] = exchange_x(far), near
+
+    make1("v", gv)
+    make1("k", gk)
+    back1 = scatter(back_rows)
+    require(sum_up)
+    sum_okv = sum_z(pair_call(sc, [(far_out, near_out), parts1["k"], parts1["v"]]))
+    make1("q", gq)
+    output = add_rows(sc, [hidden, *down], False)
+    require(sum_down)
+    (grad_tokens,) = norm_back_call(sc, grad_hidden, tokens, back1, gain1, False)
+    require(sum_okv)
+    sum_okv = sum_okv.astype(F32)
+    sum_query = sum_z(pair_call(sc, [parts1["q"]]))
+    gain1_part = sum(gain1_sums) / gain1
 
     bias_here = jnp.sum(bias_part.reshape(hh, HEAD), axis=1) * sig_bias * (1.0 - sig_bias)
     bias_full = lax.dynamic_update_slice(jnp.zeros((HEADS,), F32), bias_here, (here * hh,))
-    small = sum_everywhere(jnp.concatenate([gain1_part, gain2_part, bias_full]))
-    D = gain1.shape[0]
-    F = w_gate.shape[1]
+    small = sum_everywhere(jnp.concatenate([gain1_part[0], gain2_part[0], bias_full]))
+    D = gain1.shape[1]
     return (
         output,
         grad_tokens,
         small[:D],
-        grad_qkv[:, :E],
-        grad_qkv[:, E : 2 * E],
-        grad_qkv[:, 2 * E :],
-        grad_out.T,
+        sum_query.astype(F32),
+        sum_okv[:, E : 2 * E],
+        sum_okv[:, 2 * E :],
+        sum_okv[:, :E].T,
         small[2 * D :],
         small[D : 2 * D],
-        grad_gate_up[:, :F],
-        grad_gate_up[:, F:],
-        grad_down.T,
+        sum_gate.astype(F32),
+        sum_up,
+        sum_down.astype(F32).T,
     )
 
 

time: 1300 us -> 929 us (0.71)
  waiting for transfers between devices: 647 us -> 237 us
  Pallas kernels: 441 us -> 572 us
  blocking collectives: 65.7 us -> 0 us
  other arithmetic: 67.9 us -> 15.2 us
  starting transfers between devices: 20.6 us -> 53.3 us
    ppermute x20 -> x48, waiting for transfers between devices: 274 us -> 53.6 us  [the longest x7 25.7 us: exchange_x(): lax.ppermute(x, 'dp', [(i, i ^ 1) for i in range(lax.axis_size('dp'))])]
    ppermute x8 -> x16, waiting for transfers between devices: 338 us -> 134 us  [shift_chip(): lax.ppermute(x, 'tensor', [(i, (i + 2 * j) % count) for i in range(count)])]
    pallas_call x27 -> x50, Pallas kernels: 441 us -> 572 us  [run(): out = made(*operands, *ORDERED)]
    all_gather x2 -> x0, blocking collectives: 65.7 us -> none  [the longest x1 33.3 us: body(): norm_parts = lax.all_gather(norm_pad, 'dp')]
    convert_element_type x13 -> x3, other arithmetic: 45.5 us -> 3.53 us  [the longest x1 1.8 us: body(): sum_query.astype(F32)]
    reduce_scatter x4 -> x5, waiting for transfers between devices: 0.01 us -> 36.1 us  [sum_z(): lax.psum_scatter(x, 'dp', scatter_dimension=0, axis_index_groups=groups,...]
    all_gather x1, waiting for transfers between devices: 31.2 us -> 0.02 us  [body(): all_maps = lax.all_gather(maps, 'dp')]
    ppermute x20 -> x48, starting transfers between devices: 6.23 us -> 28.7 us  [the longest x9 13.7 us: share_steps(): lax.ppermute(x, 'dp', [(i, i ^ step) for i in range(count)])]
  transfers between devices with their start and end apart: 39 -> 75, of which waited for: 16 -> 32; matrix products, arithmetic and copies ran while one was open for 7% -> 3% of each run, Pallas kernels for 32% -> 49%
where the time goes in v2:
time: 929 us; the launch traced here: 920 us
  Pallas kernels  572 us (62%)
  waiting for transfers between devices  237 us (26%)
  starting transfers between devices  53.3 us (6%)
  local copies, waits for them, and re-layouts  25.9 us (3%)
  between operations  16.5 us (2%)
  other arithmetic  15.2 us (2%)
    pallas_call x50, Pallas kernels, run(): out = made(*operands, *ORDERED)  572 us
    ppermute x16, waiting for transfers between devices, shift_chip(): lax.ppermute(x, 'tensor', [(i, (i + 2 * j) % count) for i in range(count)])  134 us
    reduce_scatter x5, waiting for transfers between devices, sum_z(): lax.psum_scatter(x, 'dp', scatter_dimension=0, axis_index_groups=groups,...  36.1 us
    ppermute x7, waiting for transfers between devices, exchange_x(): lax.ppermute(x, 'dp', [(i, i ^ 1) for i in range(lax.axis_size('dp'))])  25.7 us
    unnamed x104, local copies, waits for them, and re-layouts  19.2 us
  transfers between devices with their start and end apart: 75, of which 32 were waited for; matrix products, arithmetic and copies ran while one was open for 3% of the time, Pallas kernels for 49%

profile of v2, /device:TPU:0, one launch (start us, length us, event | category | flops | bytes accessed | tf_op | source)
XLA Modules:
  0.0 919.8 jit_solution(1600506870539811849)
XLA Ops:
  25.3 12.8 %shard_map.230 = (bf16[2048,512]{1,0:T(8,128)(2,1)}, bf16[2048,512]{1,0:T(8,128)(2,1)}, bf16[2048,512]{1,0:T(8,128)(2,1)}, f32[1,512]{1,0:T(1,128)}) custom-call(s32[12]{0:T(128)} %concatenate.45.refs_0_, bf16[256,2048]{1,0:T(8,128)(2,1)} %get-tuple-element.134.refs_1_.refs_7_, bf16[256,2048]{1,0:T(8,128)(2,1)} %get-tuple-element.135.refs_2_.refs_8_, ...), custom_call_target="tpu_custom_call" | custom-call | flops 128849018880 | bytes 272629760 | tf_op jit(solution)/shard_map/pallas_call | solution.py:66
  41.5 21.8 %collective-permute-done.1.refs_2_ = bf16[256,2048]{1,0:T(8,128)(2,1)S(1)} collective-permute-done((bf16[256,2048]{1,0:T(8,128)(2,1)}, bf16[256,2048]{1,0:T(8,128)(2,1)S(1)}, u32[]{:S(2)}, u32[]{:S(2)}) %collective-permute-start.1) | collective-permute-done | bytes 1048608 | tf_op jit(solution)/shard_map/ppermute | solution.py:900
  70.4 12.6 %shard_map.232 = (bf16[2048,512]{1,0:T(8,128)(2,1)}, bf16[2048,512]{1,0:T(8,128)(2,1)}, bf16[2048,512]{1,0:T(8,128)(2,1)}, f32[1,512]{1,0:T(1,128)}) custom-call(s32[12]{0:T(128)} %concatenate.45.refs_0_, bf16[256,2048]{1,0:T(8,128)(2,1)} %get-tuple-element.137.refs_1_.refs_11_.refs_5_.refs_7_, ...), custom_call_target="tpu_custom_call", output_to_operand_aliasing={{0}: (8, {}), {1}: (9, {}), {2}: (10, {})} | custom-call | flops 128849018880 | bytes 272629760 | tf_op jit(solution)/shard_map/pallas_call | solution.py:66
  125.7 14.6 %collective-permute-done.10.refs_2_ = bf16[256,2048]{1,0:T(8,128)(2,1)} collective-permute-done((bf16[256,2048]{1,0:T(8,128)(2,1)}, bf16[256,2048]{1,0:T(8,128)(2,1)}, u32[]{:S(2)}, u32[]{:S(2)}) %collective-permute-start.10) | collective-permute-done | bytes 1048608 | tf_op jit(solution)/shard_map/ppermute | solution.py:900
  141.6 14.3 %shard_map.237.refs_6_.refs_7_ = bf16[1024,2048]{1,0:T(8,128)(2,1)} custom-call(s32[12]{0:T(128)} %concatenate.45.refs_0_, bf16[256,2048]{1,0:T(8,128)(2,1)} %get-tuple-element.281.refs_1_, bf16[256,2048]{1,0:T(8,128)(2,1)} %get-tuple-element.280.refs_2_, bf16[256,2048]{1,0:T(8,128)(2,1)} %collective-permute-done.13.refs_3_, ...), custom_call_target="tpu_custom_call" | custom-call | flops 171798691840 | bytes 335544320 | tf_op jit(solution)/shard_map/pallas_call | solution.py:66
  155.8 14.7 %shard_map.238.refs_3_.refs_7_ = bf16[1024,2048]{1,0:T(8,128)(2,1)} custom-call(s32[12]{0:T(128)} %concatenate.45.refs_0_, bf16[256,2048]{1,0:T(8,128)(2,1)} %get-tuple-element.154.refs_6_.refs_1_.refs_5_, bf16[256,2048]{1,0:T(8,128)(2,1)} %get-tuple-element.155.refs_2_.refs_6_, bf16[256,2048]{1,0:T(8,128)(2,1)} %collective-permute-done.11.refs_3_.refs_7_, ...), custom_call_target="tpu_custom_call" | custom-call | flops 171798691840 | bytes 335544320 | tf_op jit(solution)/shard_map/pallas_call | solution.py:66
  204.1 24.2 %collective-permute-done.19.refs_6_ = bf16[256,2048]{1,0:T(8,128)(2,1)S(1)} collective-permute-done((bf16[256,2048]{1,0:T(8,128)(2,1)}, bf16[256,2048]{1,0:T(8,128)(2,1)S(1)}, u32[]{:S(2)}, u32[]{:S(2)}) %collective-permute-start.19) | collective-permute-done | bytes 1048608 | tf_op jit(solution)/shard_map/ppermute | solution.py:900
  228.2 21.6 %collective-permute-done.20.refs_7_ = bf16[256,2048]{1,0:T(8,128)(2,1)S(1)} collective-permute-done((bf16[256,2048]{1,0:T(8,128)(2,1)}, bf16[256,2048]{1,0:T(8,128)(2,1)S(1)}, u32[]{:S(2)}, u32[]{:S(2)}) %collective-permute-start.20) | collective-permute-done | bytes 1048608 | tf_op jit(solution)/shard_map/ppermute | solution.py:900
  264.4 27.4 %shard_map.244 = (bf16[1024,2048]{1,0:T(8,128)(2,1)}, bf16[1024,2048]{1,0:T(8,128)(2,1)}, bf16[1024,2048]{1,0:T(8,128)(2,1)}) custom-call(s32[12]{0:T(128)} %concatenate.45.refs_0_, bf16[256,2048]{1,0:T(8,128)(2,1)} %get-tuple-element.169.refs_1_, bf16[256,2048]{1,0:T(8,128)(2,1)} %get-tuple-element.170.refs_2_.refs_8_, bf16[256,2048]{1,0:T(8,128)(2,1)} %copy-done.46, ...), custom_call_target="tpu_custom_call" | custom-call | flops 343597383680 | bytes 754974720 | tf_op jit(solution)/shard_map/pallas_call | solution.py:66
  291.9 15.7 %collective-permute-done.24.refs_2_ = bf16[256,2048]{1,0:T(8,128)(2,1)} collective-permute-done((bf16[256,2048]{1,0:T(8,128)(2,1)}, bf16[256,2048]{1,0:T(8,128)(2,1)}, u32[]{:S(2)}, u32[]{:S(2)}) %collective-permute-start.24) | collective-permute-done | bytes 1048608 | tf_op jit(solution)/shard_map/ppermute | solution.py:900
  313.7 27.5 %shard_map.246 = (bf16[1024,2048]{1,0:T(8,128)(2,1)}, bf16[1024,2048]{1,0:T(8,128)(2,1)}, bf16[1024,2048]{1,0:T(8,128)(2,1)}) custom-call(s32[12]{0:T(128)} %concatenate.45.refs_0_, bf16[256,2048]{1,0:T(8,128)(2,1)} %get-tuple-element.174.refs_1_.refs_8_.refs_5_, bf16[256,2048]{1,0:T(8,128)(2,1)} %get-tuple-element.175.refs_2_.refs_6_, ...), custom_call_target="tpu_custom_call" | custom-call | flops 343597383680 | bytes 754974720 | tf_op jit(solution)/shard_map/pallas_call | solution.py:66
  341.1 25.8 %shard_map.247.refs_5_ = bf16[8,256,2048]{2,1,0:T(8,128)(2,1)} custom-call(s32[12]{0:T(128)} %concatenate.45.refs_0_, bf16[256,2048]{1,0:T(8,128)(2,1)} %get-tuple-element.169.refs_1_, bf16[256,2048]{1,0:T(8,128)(2,1)} %get-tuple-element.170.refs_2_.refs_8_, bf16[256,2048]{1,0:T(8,128)(2,1)} %copy-done.46, bf16[256,2048]{1,0:T(8,128)(2,1)} %copy-done.47, ...), custom_call_target="tpu_custom_call" | custom-call | flops 343597383680 | bytes 503316480 | tf_op jit(solution)/shard_map/pallas_call | solution.py:66
  366.9 24.4 %shard_map.248 = (bf16[256,2048]{1,0:T(8,128)(2,1)}, bf16[256,2048]{1,0:T(8,128)(2,1)}, bf16[256,2048]{1,0:T(8,128)(2,1)}, bf16[256,2048]{1,0:T(8,128)(2,1)}) custom-call(s32[12]{0:T(128)} %concatenate.45.refs_0_, bf16[1024,2048]{1,0:T(8,128)(2,1)} %get-tuple-element.176.refs_1_.refs_10_, bf16[1024,2048]{1,0:T(8,128)(2,1)} %get-tuple-element.177.refs_10_.refs_11_.refs_2_, ...), custom_call_target="tpu_custom_call" | custom-call | flops 343597383680 | bytes 587202560 | tf_op jit(solution)/shard_map/pallas_call | solution.py:66
  391.8 24.4 %shard_map.249 = (bf16[256,2048]{1,0:T(8,128)(2,1)}, bf16[256,2048]{1,0:T(8,128)(2,1)}, bf16[256,2048]{1,0:T(8,128)(2,1)}, bf16[256,2048]{1,0:T(8,128)(2,1)}) custom-call(s32[12]{0:T(128)} %concatenate.45.refs_0_, bf16[1024,2048]{1,0:T(8,128)(2,1)} %get-tuple-element.172.refs_1_.refs_9_, bf16[1024,2048]{1,0:T(8,128)(2,1)} %get-tuple-element.173.refs_3_.refs_9_.refs_2_, ...), custom_call_target="tpu_custom_call" | custom-call | flops 343597383680 | bytes 587202560 | tf_op jit(solution)/shard_map/pallas_call | solution.py:66
  425.3 27.0 %shard_map.251 = (bf16[4,256,2048]{2,1,0:T(8,128)(2,1)}, bf16[4,256,2048]{2,1,0:T(8,128)(2,1)}) custom-call(s32[12]{0:T(128)} %concatenate.45.refs_0_, bf16[256,2048]{1,0:T(8,128)(2,1)} %get-tuple-element.169.refs_1_, bf16[256,2048]{1,0:T(8,128)(2,1)} %get-tuple-element.170.refs_2_.refs_8_, bf16[256,2048]{1,0:T(8,128)(2,1)} %copy-done.46, ...), custom_call_target="tpu_custom_call" | custom-call | flops 343597383680 | bytes 503316480 | tf_op jit(solution)/shard_map/pallas_call | solution.py:66
  452.8 27.1 %shard_map.252 = (bf16[4,256,2048]{2,1,0:T(8,128)(2,1)}, bf16[4,256,2048]{2,1,0:T(8,128)(2,1)}) custom-call(s32[12]{0:T(128)} %concatenate.45.refs_0_, bf16[256,2048]{1,0:T(8,128)(2,1)} %get-tuple-element.281.refs_1_, bf16[256,2048]{1,0:T(8,128)(2,1)} %get-tuple-element.280.refs_2_, bf16[256,2048]{1,0:T(8,128)(2,1)} %collective-permute-done.13.refs_3_, ...), custom_call_target="tpu_custom_call" | custom-call | flops 343597383680 | bytes 503316480 | tf_op jit(solution)/shard_map/pallas_call | solution.py:66
  492.8 13.8 %shard_map.254 = (bf16[256,2048]{1,0:T(8,128)(2,1)}, bf16[256,2048]{1,0:T(8,128)(2,1)}, bf16[256,2048]{1,0:T(8,128)(2,1)}, bf16[256,2048]{1,0:T(8,128)(2,1)}) custom-call(s32[12]{0:T(128)} %concatenate.45.refs_0_, bf16[1024,2048]{1,0:T(8,128)(2,1)} %get-tuple-element.188.refs_10_.refs_1_, bf16[2048,2048]{1,0:T(8,128)(2,1)} %refs_2_.4, ...), custom_call_target="tpu_custom_call" | custom-call | flops 171798691840 | bytes 335544320 | tf_op jit(solution)/shard_map/pallas_call | solution.py:66
  515.0 13.8 %shard_map.256 = (bf16[256,2048]{1,0:T(8,128)(2,1)}, bf16[256,2048]{1,0:T(8,128)(2,1)}, bf16[256,2048]{1,0:T(8,128)(2,1)}, bf16[256,2048]{1,0:T(8,128)(2,1)}) custom-call(s32[12]{0:T(128)} %concatenate.45.refs_0_, bf16[1024,2048]{1,0:T(8,128)(2,1)} %get-tuple-element.171.refs_9_.refs_1_, bf16[2048,2048]{1,0:T(8,128)(2,1)} %refs_2_.4, ...), custom_call_target="tpu_custom_call" | custom-call | flops 171798691840 | bytes 335544320 | tf_op jit(solution)/shard_map/pallas_call | solution.py:66
  578.6 12.3 %shard_map.261 = (f32[2048,128]{1,0:T(8,128)}, f32[2048,128]{1,0:T(8,128)}, f32[2048,128]{1,0:T(8,128)}) custom-call(s32[12]{0:T(128)} %concatenate.45.refs_0_, bf16[2048,512]{1,0:T(8,128)(2,1)} %get-tuple-element.142.refs_1_.refs_7_.refs_4_, bf16[2048,512]{1,0:T(8,128)(2,1)} %get-tuple-element.143.refs_1_.refs_2_.refs_5_, ...), custom_call_target="tpu_custom_call" | custom-call | flops 128849018880 | bytes 136314880 | tf_op jit(solution)/shard_map/pallas_call | solution.py:66
  593.9 12.6 %shard_map.262 = (f32[2048,128]{1,0:T(8,128)}, f32[2048,128]{1,0:T(8,128)}, f32[2048,128]{1,0:T(8,128)}) custom-call(s32[12]{0:T(128)} %concatenate.45.refs_0_, bf16[2048,512]{1,0:T(8,128)(2,1)} %get-tuple-element.142.refs_1_.refs_7_.refs_4_, bf16[2048,512]{1,0:T(8,128)(2,1)} %get-tuple-element.143.refs_1_.refs_2_.refs_5_, ...), custom_call_target="tpu_custom_call" | custom-call | flops 128849018880 | bytes 136314880 | tf_op jit(solution)/shard_map/pallas_call | solution.py:66
  606.6 12.5 %shard_map.263 = (f32[2048,128]{1,0:T(8,128)}, f32[2048,128]{1,0:T(8,128)}, f32[2048,128]{1,0:T(8,128)}) custom-call(s32[12]{0:T(128)} %concatenate.45.refs_0_, bf16[2048,512]{1,0:T(8,128)(2,1)} %get-tuple-element.142.refs_1_.refs_7_.refs_4_, bf16[2048,512]{1,0:T(8,128)(2,1)} %get-tuple-element.143.refs_1_.refs_2_.refs_5_, ...), custom_call_target="tpu_custom_call" | custom-call | flops 128849018880 | bytes 136314880 | tf_op jit(solution)/shard_map/pallas_call | solution.py:66
  628.1 12.8 %shard_map.264 = (f32[2048,128]{1,0:T(8,128)}, f32[2048,128]{1,0:T(8,128)}, f32[2048,128]{1,0:T(8,128)}) custom-call(s32[12]{0:T(128)} %concatenate.45.refs_0_, bf16[2048,512]{1,0:T(8,128)(2,1)} %get-tuple-element.142.refs_1_.refs_7_.refs_4_, bf16[2048,512]{1,0:T(8,128)(2,1)} %get-tuple-element.143.refs_1_.refs_2_.refs_5_, ...), custom_call_target="tpu_custom_call" | custom-call | flops 128849018880 | bytes 136314880 | tf_op jit(solution)/shard_map/pallas_call | solution.py:66
  640.9 11.8 %shard_map.265 = (bf16[4,256,512]{2,1,0:T(8,128)(2,1)}, bf16[4,256,512]{2,1,0:T(8,128)(2,1)}) custom-call(s32[12]{0:T(128)} %concatenate.45.refs_0_, bf16[256,2048]{1,0:T(8,128)(2,1)} %get-tuple-element.191.refs_1_, bf16[256,2048]{1,0:T(8,128)(2,1)} %get-tuple-element.192.refs_2_, bf16[256,2048]{1,0:T(8,128)(2,1)} %collective-permute-done.33.refs_3_, ...), custom_call_target="tpu_custom_call" | custom-call | flops 85899345920 | bytes 251658240 | tf_op jit(solution)/shard_map/pallas_call | solution.py:66
  687.0 14.4 %shard_map.268 = (bf16[2048,512]{1,0:T(8,128)(2,1)}, bf16[2048,512]{1,0:T(8,128)(2,1)}, bf16[2048,512]{1,0:T(8,128)(2,1)}) custom-call(s32[12]{0:T(128)} %concatenate.45.refs_0_, bf16[2048,512]{1,0:T(8,128)(2,1)} %get-tuple-element.142.refs_1_.refs_7_.refs_4_, bf16[2048,512]{1,0:T(8,128)(2,1)} %get-tuple-element.143.refs_1_.refs_2_.refs_5_, ...), custom_call_target="tpu_custom_call" | custom-call | flops 37580963840 | bytes 545259520 | tf_op jit(solution)/shard_map/pallas_call | solution.py:66
  701.3 11.8 %shard_map.269 = (bf16[4,256,512]{2,1,0:T(8,128)(2,1)}, bf16[4,256,512]{2,1,0:T(8,128)(2,1)}) custom-call(s32[12]{0:T(128)} %concatenate.45.refs_0_, bf16[256,2048]{1,0:T(8,128)(2,1)} %get-tuple-element.134.refs_1_.refs_7_, bf16[256,2048]{1,0:T(8,128)(2,1)} %get-tuple-element.135.refs_2_.refs_8_, bf16[256,2048]{1,0:T(8,128)(2,1)} %copy-done.41, ...), custom_call_target="tpu_custom_call" | custom-call | flops 85899345920 | bytes 251658240 | tf_op jit(solution)/shard_map/pallas_call | solution.py:66
  713.2 11.9 %shard_map.270 = (bf16[4,256,512]{2,1,0:T(8,128)(2,1)}, bf16[4,256,512]{2,1,0:T(8,128)(2,1)}) custom-call(s32[12]{0:T(128)} %concatenate.45.refs_0_, bf16[256,2048]{1,0:T(8,128)(2,1)} %get-tuple-element.134.refs_1_.refs_7_, bf16[256,2048]{1,0:T(8,128)(2,1)} %get-tuple-element.135.refs_2_.refs_8_, bf16[256,2048]{1,0:T(8,128)(2,1)} %copy-done.41, ...), custom_call_target="tpu_custom_call" | custom-call | flops 85899345920 | bytes 251658240 | tf_op jit(solution)/shard_map/pallas_call | solution.py:66
  725.0 12.2 %shard_map.271 = (bf16[256,2048]{1,0:T(8,128)(2,1)}, bf16[256,2048]{1,0:T(8,128)(2,1)}, bf16[256,2048]{1,0:T(8,128)(2,1)}, bf16[256,2048]{1,0:T(8,128)(2,1)}, f32[1,2048]{1,0:T(1,128)}) custom-call(s32[12]{0:T(128)} %concatenate.45.refs_0_, bf16[2048,512]{1,0:T(8,128)(2,1)} %get-tuple-element.233.refs_1_.refs_9_, ...), custom_call_target="tpu_custom_call" | custom-call | flops 128849018880 | bytes 272629760 | tf_op jit(solution)/shard_map/pallas_call | solution.py:66
  745.9 12.1 %shard_map.272 = (bf16[256,2048]{1,0:T(8,128)(2,1)}, bf16[256,2048]{1,0:T(8,128)(2,1)}, bf16[256,2048]{1,0:T(8,128)(2,1)}, bf16[256,2048]{1,0:T(8,128)(2,1)}, f32[1,2048]{1,0:T(1,128)}) custom-call(s32[12]{0:T(128)} %concatenate.45.refs_0_, bf16[2048,512]{1,0:T(8,128)(2,1)} %get-tuple-element.233.refs_1_.refs_9_, ...), custom_call_target="tpu_custom_call" | custom-call | flops 128849018880 | bytes 272629760 | tf_op jit(solution)/shard_map/pallas_call | solution.py:66
  768.4 19.7 %collective-permute-done.54.refs_3_ = bf16[4,256,512]{2,1,0:T(8,128)(2,1)S(1)} collective-permute-done((bf16[4,256,512]{2,1,0:T(8,128)(2,1)}, bf16[4,256,512]{2,1,0:T(8,128)(2,1)S(1)}, u32[]{:S(2)}, u32[]{:S(2)}) %collective-permute-start.54) | collective-permute-done | bytes 1048608 | tf_op jit(solution)/shard_map/ppermute | solution.py:914
  798.2 11.9 %shard_map.275 = (bf16[4,256,512]{2,1,0:T(8,128)(2,1)}, bf16[4,256,512]{2,1,0:T(8,128)(2,1)}) custom-call(s32[12]{0:T(128)} %concatenate.45.refs_0_, bf16[256,2048]{1,0:T(8,128)(2,1)} %get-tuple-element.134.refs_1_.refs_7_, bf16[256,2048]{1,0:T(8,128)(2,1)} %get-tuple-element.135.refs_2_.refs_8_, bf16[256,2048]{1,0:T(8,128)(2,1)} %copy-done.41, ...), custom_call_target="tpu_custom_call" | custom-call | flops 85899345920 | bytes 251658240 | tf_op jit(solution)/shard_map/pallas_call | solution.py:66
  818.7 24.5 %collective-permute-done.61.refs_7_ = bf16[256,2048]{1,0:T(8,128)(2,1)} collective-permute-done((bf16[256,2048]{1,0:T(8,128)(2,1)}, bf16[256,2048]{1,0:T(8,128)(2,1)}, u32[]{:S(2)}, u32[]{:S(2)}) %collective-permute-start.61) | collective-permute-done | bytes 1048608 | tf_op jit(solution)/shard_map/ppermute | solution.py:900
  852.3 26.1 %reduce-scatter.12.cloned.1.call-done.refs_4_ = bf16[256,1536]{1,0:T(8,128)(2,1)} async-done(((bf16[1024,1536]{1,0:T(8,128)(2,1)}), bf16[256,1536]{1,0:T(8,128)(2,1)}) %reduce-scatter.12.cloned.1.call-update) | async-done | bytes 786448 | tf_op jit(solution)/shard_map/reduce_scatter | solution.py:920
  (316 shorter events, 333.4 us)
Async XLA Ops:
  7.2 163.4 %all-gather.3.cloned.1.call-start = ((), (), s32[]{:S(2)}) async-start(), calls=%async_computation.10 | async-start | bytes 2359296 | tf_op jit(solution)/shard_map/all_gather | solution.py:1020
  17.3 46.0 %collective-permute-start.1 = (bf16[256,2048]{1,0:T(8,128)(2,1)}, bf16[256,2048]{1,0:T(8,128)(2,1)S(1)}, u32[]{:S(2)}, u32[]{:S(2)}) collective-permute-start(bf16[256,2048]{1,0:T(8,128)(2,1)} %get-tuple-element.135.refs_2_.refs_8_), channel_id=1, source_target_pairs={{0,2},{1,3},{2,0},{3,1},{4,6},{5,7},{6,4},{7,5},{8,10},{9,11},{10,... | collective-permute-start | bytes 3145736 | tf_op jit(solution)/shard_map/ppermute | solution.py:900
  90.1 51.4 %collective-permute-start.14 = (bf16[256,2048]{1,0:T(8,128)(2,1)}, bf16[256,2048]{1,0:T(8,128)(2,1)}, u32[]{:S(2)}, u32[]{:S(2)}) collective-permute-start(bf16[256,2048]{1,0:T(8,128)(2,1)} %get-tuple-element.280.refs_2_), channel_id=1, source_target_pairs={{0,1},{1,0},{2,3},{3,2},{4,5},{5,4},{6,7},{7,6},{8,9},{9,8},{10,11... | collective-permute-start | bytes 3145736 | tf_op jit(solution)/shard_map/ppermute | solution.py:895
  90.1 51.4 %collective-permute-start.13 = (bf16[256,2048]{1,0:T(8,128)(2,1)}, bf16[256,2048]{1,0:T(8,128)(2,1)}, u32[]{:S(2)}, u32[]{:S(2)}) collective-permute-start(bf16[256,2048]{1,0:T(8,128)(2,1)} %get-tuple-element.281.refs_1_), channel_id=1, source_target_pairs={{0,1},{1,0},{2,3},{3,2},{4,5},{5,4},{6,7},{7,6},{8,9},{9,8},{10,11... | collective-permute-start | bytes 3145736 | tf_op jit(solution)/shard_map/ppermute | solution.py:895
  95.6 44.7 %collective-permute-start.10 = (bf16[256,2048]{1,0:T(8,128)(2,1)}, bf16[256,2048]{1,0:T(8,128)(2,1)}, u32[]{:S(2)}, u32[]{:S(2)}) collective-permute-start(bf16[256,2048]{1,0:T(8,128)(2,1)} %get-tuple-element.152), channel_id=1, source_target_pairs={{0,2},{1,3},{2,0},{3,1},{4,6},{5,7},{6,4},{7,5},{8,10},{9,11},{10,... | collective-permute-start | bytes 3145736 | tf_op jit(solution)/shard_map/ppermute | solution.py:900
  103.7 456.8 %reduce-scatter.6.cloned.1.call-start = ((), (), s32[]{:S(2)}) async-start(), calls=%async_computation.5 | async-start | bytes 10485760 | tf_op jit(solution)/shard_map/reduce_scatter | solution.py:920
  203.5 46.3 %collective-permute-start.20 = (bf16[256,2048]{1,0:T(8,128)(2,1)}, bf16[256,2048]{1,0:T(8,128)(2,1)S(1)}, u32[]{:S(2)}, u32[]{:S(2)}) collective-permute-start(bf16[256,2048]{1,0:T(8,128)(2,1)} %get-tuple-element.167.refs_9_), channel_id=1, source_target_pairs={{0,2},{1,3},{2,0},{3,1},{4,6},{5,7},{6,4},{7,5},{8,10},{9,11},{10,... | collective-permute-start | bytes 3145736 | tf_op jit(solution)/shard_map/ppermute | solution.py:900
  261.1 46.4 %collective-permute-start.24 = (bf16[256,2048]{1,0:T(8,128)(2,1)}, bf16[256,2048]{1,0:T(8,128)(2,1)}, u32[]{:S(2)}, u32[]{:S(2)}) collective-permute-start(bf16[256,2048]{1,0:T(8,128)(2,1)} %get-tuple-element.170.refs_2_.refs_8_), channel_id=1, source_target_pairs={{0,2},{1,3},{2,0},{3,1},{4,6},{5,7},{6,4},{7,5},{8,10},{9,11},{10,... | collective-permute-start | bytes 3145736 | tf_op jit(solution)/shard_map/ppermute | solution.py:900
  416.3 270.7 %reduce-scatter.8.cloned.1.call-start = ((), (), s32[]{:S(2)}) async-start(), calls=%async_computation.6 | async-start | bytes 5242880 | tf_op jit(solution)/shard_map/reduce_scatter | solution.py:920
  416.3 63.6 %collective-permute-start.27 = (bf16[256,2048]{1,0:T(8,128)(2,1)}, bf16[256,2048]{1,0:T(8,128)(2,1)}, u32[]{:S(2)}, u32[]{:S(2)}) collective-permute-start(bf16[256,2048]{1,0:T(8,128)(2,1)} %get-tuple-element.181), channel_id=1, source_target_pairs={{0,1},{1,0},{2,3},{3,2},{4,5},{5,4},{6,7},{7,6},{8,9},{9,8},{10,11... | collective-permute-start | bytes 3145736 | tf_op jit(solution)/shard_map/ppermute | solution.py:895
  416.5 63.4 %collective-permute-start.28 = (bf16[256,2048]{1,0:T(8,128)(2,1)}, bf16[256,2048]{1,0:T(8,128)(2,1)}, u32[]{:S(2)}, u32[]{:S(2)}) collective-permute-start(bf16[256,2048]{1,0:T(8,128)(2,1)} %get-tuple-element.182.refs_5_), channel_id=1, source_target_pairs={{0,1},{1,0},{2,3},{3,2},{4,5},{5,4},{6,7},{7,6},{8,9},{9,8},{10,11... | collective-permute-start | bytes 3145736 | tf_op jit(solution)/shard_map/ppermute | solution.py:895
  423.3 56.6 %collective-permute-start.31 = (bf16[256,2048]{1,0:T(8,128)(2,1)}, bf16[256,2048]{1,0:T(8,128)(2,1)}, u32[]{:S(2)}, u32[]{:S(2)}) collective-permute-start(bf16[256,2048]{1,0:T(8,128)(2,1)} %get-tuple-element.186), channel_id=1, source_target_pairs={{0,2},{1,3},{2,0},{3,1},{4,6},{5,7},{6,4},{7,5},{8,10},{9,11},{10,... | collective-permute-start | bytes 3145736 | tf_op jit(solution)/shard_map/ppermute | solution.py:900
  424.7 55.2 %collective-permute-start.32 = (bf16[256,2048]{1,0:T(8,128)(2,1)}, bf16[256,2048]{1,0:T(8,128)(2,1)}, u32[]{:S(2)}, u32[]{:S(2)}) collective-permute-start(bf16[256,2048]{1,0:T(8,128)(2,1)} %get-tuple-element.187.refs_11_), channel_id=1, source_target_pairs={{0,2},{1,3},{2,0},{3,1},{4,6},{5,7},{6,4},{7,5},{8,10},{9,11},{10,... | collective-permute-start | bytes 3145736 | tf_op jit(solution)/shard_map/ppermute | solution.py:900
  452.3 93.9 %collective-permute-start.43 = (bf16[4,256,2048]{2,1,0:T(8,128)(2,1)}, bf16[4,256,2048]{2,1,0:T(8,128)(2,1)}, u32[]{:S(2)}, u32[]{:S(2)}) collective-permute-start(bf16[4,256,2048]{2,1,0:T(8,128)(2,1)} %get-tuple-element.207), channel_id=1, source_target_pairs={{0,4},{4,0},{8,12},{12,8},{16,20},{20,16},{24,28},{28,24},{1,5},{5... | collective-permute-start | bytes 12582920 | tf_op jit(solution)/shard_map/ppermute | solution.py:914
  490.4 38.4 %collective-permute-start.39 = (bf16[256,2048]{1,0:T(8,128)(2,1)}, bf16[256,2048]{1,0:T(8,128)(2,1)}, u32[]{:S(2)}, u32[]{:S(2)}) collective-permute-start(bf16[256,2048]{1,0:T(8,128)(2,1)} %get-tuple-element.191.refs_1_), channel_id=1, source_target_pairs={{0,2},{1,3},{2,0},{3,1},{4,6},{5,7},{6,4},{7,5},{8,10},{9,11},{10,... | collective-permute-start | bytes 3145736 | tf_op jit(solution)/shard_map/ppermute | solution.py:900
  492.0 45.4 %collective-permute-start.40 = (bf16[256,2048]{1,0:T(8,128)(2,1)}, bf16[256,2048]{1,0:T(8,128)(2,1)}, u32[]{:S(2)}, u32[]{:S(2)}) collective-permute-start(bf16[256,2048]{1,0:T(8,128)(2,1)} %get-tuple-element.192.refs_2_), channel_id=1, source_target_pairs={{0,2},{1,3},{2,0},{3,1},{4,6},{5,7},{6,4},{7,5},{8,10},{9,11},{10,... | collective-permute-start | bytes 3145736 | tf_op jit(solution)/shard_map/ppermute | solution.py:900
  538.6 114.1 %collective-permute-start.49 = (bf16[4,256,2048]{2,1,0:T(8,128)(2,1)}, bf16[4,256,2048]{2,1,0:T(8,128)(2,1)}, u32[]{:S(2)}, u32[]{:S(2)}) collective-permute-start(bf16[4,256,2048]{2,1,0:T(8,128)(2,1)} %get-tuple-element.227), channel_id=1, source_target_pairs={{0,4},{4,0},{8,12},{12,8},{16,20},{20,16},{24,28},{28,24},{1,5},{5... | collective-permute-start | bytes 12582920 | tf_op jit(solution)/shard_map/ppermute | solution.py:914
  552.9 290.3 %reduce-scatter.10.cloned.1.call-start = ((), (), s32[]{:S(2)}) async-start(), calls=%async_computation.7 | async-start | bytes 5242880 | tf_op jit(solution)/shard_map/reduce_scatter | solution.py:920
  591.7 33.1 %collective-permute-start.47 = (bf16[2,4,128,128]{3,2,1,0:T(8,128)(2,1)}, bf16[2,4,128,128]{3,2,1,0:T(8,128)(2,1)}, u32[]{:S(2)}, u32[]{:S(2)}) collective-permute-start(bf16[2,4,128,128]{3,2,1,0:T(8,128)(2,1)} %pad_maximum_fusion.2.refs_8_), channel_id=1, source_target_pairs={{0,16},{4,20},{8,24},{12,28},{16,0},{20,4},{24,8},{28,12},{1,17},{... | collective-permute-start | bytes 786440 | tf_op jit(solution)/shard_map/ppermute | solution.py:934
  626.6 32.9 %collective-permute-start.48 = (bf16[4,4,128,128]{3,2,1,0:T(8,128)(2,1)}, bf16[4,4,128,128]{3,2,1,0:T(8,128)(2,1)}, u32[]{:S(2)}, u32[]{:S(2)}) collective-permute-start(bf16[4,4,128,128]{3,2,1,0:T(8,128)(2,1)} %pad_maximum_fusion.1.refs_8_), channel_id=1, source_target_pairs={{0,4},{4,0},{8,12},{12,8},{16,20},{20,16},{24,28},{28,24},{1,5},{5... | collective-permute-start | bytes 1572872 | tf_op jit(solution)/shard_map/ppermute | solution.py:934
  684.0 53.9 %collective-permute-start.58 = (bf16[256,2048]{1,0:T(8,128)(2,1)}, bf16[256,2048]{1,0:T(8,128)(2,1)}, u32[]{:S(2)}, u32[]{:S(2)}) collective-permute-start(bf16[256,2048]{1,0:T(8,128)(2,1)} %constant_dynamic-slice_fusion), channel_id=1, source_target_pairs={{0,4},{4,0},{8,12},{12,8},{16,20},{20,16},{24,28},{28,24},{1,5},{5... | collective-permute-start | bytes 3145736 | tf_op jit(solution)/shard_map/ppermute | solution.py:914
  685.5 53.0 %collective-permute-start.53 = (bf16[4,256,512]{2,1,0:T(8,128)(2,1)}, bf16[4,256,512]{2,1,0:T(8,128)(2,1)}, u32[]{:S(2)}, u32[]{:S(2)}) collective-permute-start(bf16[4,256,512]{2,1,0:T(8,128)(2,1)} %get-tuple-element.234), channel_id=1, source_target_pairs={{0,4},{4,0},{8,12},{12,8},{16,20},{20,16},{24,28},{28,24},{1,5},{5... | collective-permute-start | bytes 3145736 | tf_op jit(solution)/shard_map/ppermute | solution.py:914
  737.8 57.2 %collective-permute-start.36 = (bf16[256,2048]{1,0:T(8,128)(2,1)S(1)}, bf16[256,2048]{1,0:T(8,128)(2,1)}, u32[]{:S(2)}, u32[]{:S(2)}) collective-permute-start(bf16[256,2048]{1,0:T(8,128)(2,1)S(1)} %copy-done.17), channel_id=1, source_target_pairs={{0,1},{1,0},{2,3},{3,2},{4,5},{5,4},{6,7},{7,6},{8,9},{9,8},{10,11... | collective-permute-start | bytes 3145736 | tf_op jit(solution)/shard_map/ppermute | solution.py:895
  737.9 140.5 %reduce-scatter.12.cloned.1.call-start = ((), (), s32[]{:S(2)}) async-start(), calls=%async_computation.8 | async-start | bytes 3932160 | tf_op jit(solution)/shard_map/reduce_scatter | solution.py:920
  738.0 56.9 %collective-permute-start.35 = (bf16[256,2048]{1,0:T(8,128)(2,1)}, bf16[256,2048]{1,0:T(8,128)(2,1)}, u32[]{:S(2)}, u32[]{:S(2)}) collective-permute-start(bf16[256,2048]{1,0:T(8,128)(2,1)} %get-tuple-element.198), channel_id=1, source_target_pairs={{0,1},{1,0},{2,3},{3,2},{4,5},{5,4},{6,7},{7,6},{8,9},{9,8},{10,11... | collective-permute-start | bytes 3145736 | tf_op jit(solution)/shard_map/ppermute | solution.py:895
  738.5 59.0 %collective-permute-start.44 = (bf16[256,2048]{1,0:T(8,128)(2,1)}, bf16[256,2048]{1,0:T(8,128)(2,1)}, u32[]{:S(2)}, u32[]{:S(2)}) collective-permute-start(bf16[256,2048]{1,0:T(8,128)(2,1)} %get-tuple-element.209), channel_id=1, source_target_pairs={{0,2},{1,3},{2,0},{3,1},{4,6},{5,7},{6,4},{7,5},{8,10},{9,11},{10,... | collective-permute-start | bytes 3145736 | tf_op jit(solution)/shard_map/ppermute | solution.py:900
  744.7 43.4 %collective-permute-start.54 = (bf16[4,256,512]{2,1,0:T(8,128)(2,1)}, bf16[4,256,512]{2,1,0:T(8,128)(2,1)S(1)}, u32[]{:S(2)}, u32[]{:S(2)}) collective-permute-start(bf16[4,256,512]{2,1,0:T(8,128)(2,1)} %get-tuple-element.238), channel_id=1, source_target_pairs={{0,4},{4,0},{8,12},{12,8},{16,20},{20,16},{24,28},{28,24},{1,5},{5... | collective-permute-start | bytes 3145736 | tf_op jit(solution)/shard_map/ppermute | solution.py:914
  766.9 43.2 %collective-permute-start.45 = (bf16[256,2048]{1,0:T(8,128)(2,1)}, bf16[256,2048]{1,0:T(8,128)(2,1)S(1)}, u32[]{:S(2)}, u32[]{:S(2)}) collective-permute-start(bf16[256,2048]{1,0:T(8,128)(2,1)} %get-tuple-element.210.refs_7_), channel_id=1, source_target_pairs={{0,2},{1,3},{2,0},{3,1},{4,6},{5,7},{6,4},{7,5},{8,10},{9,11},{10,... | collective-permute-start | bytes 3145736 | tf_op jit(solution)/shard_map/ppermute | solution.py:900
  794.9 116.1 %reduce-scatter.14.cloned.1.call-start = ((), (), s32[]{:S(2)}) async-start(), calls=%async_computation.9 | async-start | bytes 1310720 | tf_op jit(solution)/shard_map/reduce_scatter | solution.py:920
  796.1 47.2 %collective-permute-start.62 = (bf16[256,2048]{1,0:T(8,128)(2,1)S(1)}, bf16[256,2048]{1,0:T(8,128)(2,1)}, u32[]{:S(2)}, u32[]{:S(2)}) collective-permute-start(bf16[256,2048]{1,0:T(8,128)(2,1)S(1)} %copy-done.12), channel_id=1, source_target_pairs={{0,2},{1,3},{2,0},{3,1},{4,6},{5,7},{6,4},{7,5},{8,10},{9,11},{10,... | collective-permute-start | bytes 3145736 | tf_op jit(solution)/shard_map/ppermute | solution.py:900
  797.5 45.7 %collective-permute-start.61 = (bf16[256,2048]{1,0:T(8,128)(2,1)}, bf16[256,2048]{1,0:T(8,128)(2,1)}, u32[]{:S(2)}, u32[]{:S(2)}) collective-permute-start(bf16[256,2048]{1,0:T(8,128)(2,1)} %get-tuple-element.254), channel_id=1, source_target_pairs={{0,2},{1,3},{2,0},{3,1},{4,6},{5,7},{6,4},{7,5},{8,10},{9,11},{10,... | collective-permute-start | bytes 3145736 | tf_op jit(solution)/shard_map/ppermute | solution.py:900
  810.0 42.3 %collective-permute-start.68 = (bf16[4,256,512]{2,1,0:T(8,128)(2,1)}, bf16[4,256,512]{2,1,0:T(8,128)(2,1)S(1)}, u32[]{:S(2)}, u32[]{:S(2)}) collective-permute-start(bf16[4,256,512]{2,1,0:T(8,128)(2,1)} %get-tuple-element.255), channel_id=1, source_target_pairs={{0,4},{4,0},{8,12},{12,8},{16,20},{20,16},{24,28},{28,24},{1,5},{5... | collective-permute-start | bytes 3145736 | tf_op jit(solution)/shard_map/ppermute | solution.py:914
  (93 other events, 1215.5 us)
Sparse Core Ops, SparseCore 0:
  103.8 50.2 all-gather.2
  416.4 143.9 reduce-scatter.5
  563.3 85.9 reduce-scatter.7
  738.0 77.4 reduce-scatter.9
  817.7 60.7 reduce-scatter.11
  882.9 28.0 reduce-scatter.13

commit v3 on v2

--- a/solution.py
+++ b/solution.py
@@ -1087,12 +1087,16 @@
             require(all_cots)
     for all_cots in steps:
         pass
+    pair_down = pair_call(sc, [(far_down, near_down)])
+    sum_down = sum_z(pair_down)
+    require(sum_up)
+    memory_cot, norm_part = memory_cot_call(sc, gathered, all_maps, all_cots, q, k, grad_read, memory, norm)
+    steps = share_steps(jnp.concatenate([norm_part.reshape(hh, HEAD), jnp.zeros((8 - hh, HEAD), F32)]))
+    require(next(steps))
     far_out, near_out = wgrad_call(sc, grad_rows, [mixed], ndp, 1)
     far_out = exchange_x(far_out)
-    pair_down = pair_call(sc, [(far_down, near_down)])
-    sum_down = sum_z(pair_down)
-    memory_cot, norm_part = memory_cot_call(sc, gathered, all_maps, all_cots, q, k, grad_read, memory, norm)
-    norm_parts = share_over_dp(jnp.concatenate([norm_part.reshape(hh, HEAD), jnp.zeros((8 - hh, HEAD), F32)]))
+    for norm_parts in steps:
+        pass
     require(sum_gate)
     gq, gk, gv = combine_call(
         sc, chips, q, k, v, grad_read, local_grads, memory, norm, memory_cot, gathered, norm_parts
@@ -1112,16 +1116,15 @@
 
     make1("v", gv)
     make1("k", gk)
+    output = add_rows(sc, [hidden, *down], False)
     back1 = scatter(back_rows)
-    require(sum_up)
-    sum_okv = sum_z(pair_call(sc, [(far_out, near_out), parts1["k"], parts1["v"]]))
+    require(sum_down)
+    sum_ovk = sum_z(pair_call(sc, [(far_out, near_out), parts1["v"], parts1["k"]]))
     make1("q", gq)
-    output = add_rows(sc, [hidden, *down], False)
-    require(sum_down)
     (grad_tokens,) = norm_back_call(sc, grad_hidden, tokens, back1, gain1, False)
-    require(sum_okv)
-    sum_okv = sum_okv.astype(F32)
-    sum_query = sum_z(pair_call(sc, [parts1["q"]]))
+    require(sum_ovk)
+    sum_ovk = sum_ovk.astype(F32)
+    sum_query = sum_z(pair_call(sc, [parts1["q"]])).astype(F32)
     gain1_part = sum(gain1_sums) / gain1
 
     bias_here = jnp.sum(bias_part.reshape(hh, HEAD), axis=1) * sig_bias * (1.0 - sig_bias)
@@ -1132,10 +1135,10 @@
         output,
         grad_tokens,
         small[:D],
-        sum_query.astype(F32),
-        sum_okv[:, E : 2 * E],
-        sum_okv[:, 2 * E :],
-        sum_okv[:, :E].T,
+        sum_query,
+        sum_ovk[:, 2 * E :],
+        sum_ovk[:, E : 2 * E],
+        sum_ovk[:, :E].T,
         small[2 * D :],
         small[D : 2 * D],
         sum_gate.astype(F32),

time: 929 us -> 909 us (0.978)
  waiting for transfers between devices: 237 us -> 216 us
    ppermute x7, waiting for transfers between devices: 25.7 us -> 9.41 us  [exchange_x(): lax.ppermute(x, 'dp', [(i, i ^ 1) for i in range(lax.axis_size('dp'))])]
    reduce_scatter x5, waiting for transfers between devices: 36.1 us -> 23.2 us  [sum_z(): lax.psum_scatter(x, 'dp', scatter_dimension=0, axis_index_groups=groups,...]
    ppermute x9, waiting for transfers between devices: 15.4 us -> 27.9 us  [share_steps(): lax.ppermute(x, 'dp', [(i, i ^ step) for i in range(count)])]
    unnamed x104 -> x96, local copies, waits for them, and re-layouts: 19.2 us -> 17.8 us
  transfers between devices with their start and end apart: 75 -> 75, of which waited for: 32 -> 31; matrix products, arithmetic and copies ran while one was open for 3% -> 3% of each run, Pallas kernels for 49% -> 50%
where the time goes in v3:
time: 909 us; the launch traced here: 900 us
  Pallas kernels  572 us (63%)
  waiting for transfers between devices  216 us (24%)
  starting transfers between devices  54.8 us (6%)
  local copies, waits for them, and re-layouts  25.8 us (3%)
  between operations  16.4 us (2%)
  other arithmetic  14.2 us (2%)
    pallas_call x50, Pallas kernels, run(): out = made(*operands, *ORDERED)  572 us
    ppermute x16, waiting for transfers between devices, shift_chip(): lax.ppermute(x, 'tensor', [(i, (i + 2 * j) % count) for i in range(count)])  134 us
    ppermute x9, waiting for transfers between devices, share_steps(): lax.ppermute(x, 'dp', [(i, i ^ step) for i in range(count)])  27.9 us
    reduce_scatter x5, waiting for transfers between devices, sum_z(): lax.psum_scatter(x, 'dp', scatter_dimension=0, axis_index_groups=groups,...  23.2 us
  transfers between devices with their start and end apart: 75, of which 31 were waited for; matrix products, arithmetic and copies ran while one was open for 3% of the time, Pallas kernels for 50%

profile of v3, /device:TPU:0, one launch (start us, length us, event | category | flops | bytes accessed | tf_op | source)
XLA Modules:
  0.0 899.6 jit_solution(3637084601325768827)
XLA Ops:
  25.3 12.8 %shard_map.230 = (bf16[2048,512]{1,0:T(8,128)(2,1)}, bf16[2048,512]{1,0:T(8,128)(2,1)}, bf16[2048,512]{1,0:T(8,128)(2,1)}, f32[1,512]{1,0:T(1,128)}) custom-call(s32[12]{0:T(128)} %concatenate.45.refs_0_, bf16[256,2048]{1,0:T(8,128)(2,1)} %get-tuple-element.134.refs_1_.refs_7_, bf16[256,2048]{1,0:T(8,128)(2,1)} %get-tuple-element.135.refs_2_.refs_8_, ...), custom_call_target="tpu_custom_call" | custom-call | flops 128849018880 | bytes 272629760 | tf_op jit(solution)/shard_map/pallas_call | solution.py:66
  41.4 21.8 %collective-permute-done.1.refs_2_ = bf16[256,2048]{1,0:T(8,128)(2,1)S(1)} collective-permute-done((bf16[256,2048]{1,0:T(8,128)(2,1)}, bf16[256,2048]{1,0:T(8,128)(2,1)S(1)}, u32[]{:S(2)}, u32[]{:S(2)}) %collective-permute-start.1) | collective-permute-done | bytes 1048608 | tf_op jit(solution)/shard_map/ppermute | solution.py:900
  70.3 12.6 %shard_map.232 = (bf16[2048,512]{1,0:T(8,128)(2,1)}, bf16[2048,512]{1,0:T(8,128)(2,1)}, bf16[2048,512]{1,0:T(8,128)(2,1)}, f32[1,512]{1,0:T(1,128)}) custom-call(s32[12]{0:T(128)} %concatenate.45.refs_0_, bf16[256,2048]{1,0:T(8,128)(2,1)} %get-tuple-element.137.refs_1_.refs_11_.refs_5_.refs_7_, ...), custom_call_target="tpu_custom_call", output_to_operand_aliasing={{0}: (8, {}), {1}: (9, {}), {2}: (10, {})} | custom-call | flops 128849018880 | bytes 272629760 | tf_op jit(solution)/shard_map/pallas_call | solution.py:66
  125.7 14.6 %collective-permute-done.10.refs_2_ = bf16[256,2048]{1,0:T(8,128)(2,1)} collective-permute-done((bf16[256,2048]{1,0:T(8,128)(2,1)}, bf16[256,2048]{1,0:T(8,128)(2,1)}, u32[]{:S(2)}, u32[]{:S(2)}) %collective-permute-start.10) | collective-permute-done | bytes 1048608 | tf_op jit(solution)/shard_map/ppermute | solution.py:900
  141.5 14.3 %shard_map.237.refs_6_.refs_7_ = bf16[1024,2048]{1,0:T(8,128)(2,1)} custom-call(s32[12]{0:T(128)} %concatenate.45.refs_0_, bf16[256,2048]{1,0:T(8,128)(2,1)} %get-tuple-element.281.refs_1_, bf16[256,2048]{1,0:T(8,128)(2,1)} %get-tuple-element.280.refs_2_, bf16[256,2048]{1,0:T(8,128)(2,1)} %collective-permute-done.13.refs_3_, ...), custom_call_target="tpu_custom_call" | custom-call | flops 171798691840 | bytes 335544320 | tf_op jit(solution)/shard_map/pallas_call | solution.py:66
  155.8 14.7 %shard_map.238.refs_3_.refs_7_ = bf16[1024,2048]{1,0:T(8,128)(2,1)} custom-call(s32[12]{0:T(128)} %concatenate.45.refs_0_, bf16[256,2048]{1,0:T(8,128)(2,1)} %get-tuple-element.154.refs_6_.refs_1_.refs_5_, bf16[256,2048]{1,0:T(8,128)(2,1)} %get-tuple-element.155.refs_2_.refs_6_, bf16[256,2048]{1,0:T(8,128)(2,1)} %collective-permute-done.11.refs_3_.refs_7_, ...), custom_call_target="tpu_custom_call" | custom-call | flops 171798691840 | bytes 335544320 | tf_op jit(solution)/shard_map/pallas_call | solution.py:66
  204.0 24.2 %collective-permute-done.19.refs_6_ = bf16[256,2048]{1,0:T(8,128)(2,1)S(1)} collective-permute-done((bf16[256,2048]{1,0:T(8,128)(2,1)}, bf16[256,2048]{1,0:T(8,128)(2,1)S(1)}, u32[]{:S(2)}, u32[]{:S(2)}) %collective-permute-start.19) | collective-permute-done | bytes 1048608 | tf_op jit(solution)/shard_map/ppermute | solution.py:900
  228.2 21.6 %collective-permute-done.20.refs_7_ = bf16[256,2048]{1,0:T(8,128)(2,1)S(1)} collective-permute-done((bf16[256,2048]{1,0:T(8,128)(2,1)}, bf16[256,2048]{1,0:T(8,128)(2,1)S(1)}, u32[]{:S(2)}, u32[]{:S(2)}) %collective-permute-start.20) | collective-permute-done | bytes 1048608 | tf_op jit(solution)/shard_map/ppermute | solution.py:900
  264.4 27.3 %shard_map.244 = (bf16[1024,2048]{1,0:T(8,128)(2,1)}, bf16[1024,2048]{1,0:T(8,128)(2,1)}, bf16[1024,2048]{1,0:T(8,128)(2,1)}) custom-call(s32[12]{0:T(128)} %concatenate.45.refs_0_, bf16[256,2048]{1,0:T(8,128)(2,1)} %get-tuple-element.169.refs_1_, bf16[256,2048]{1,0:T(8,128)(2,1)} %get-tuple-element.170.refs_2_.refs_8_, bf16[256,2048]{1,0:T(8,128)(2,1)} %copy-done.42, ...), custom_call_target="tpu_custom_call" | custom-call | flops 343597383680 | bytes 754974720 | tf_op jit(solution)/shard_map/pallas_call | solution.py:66
  291.7 15.8 %collective-permute-done.24.refs_2_ = bf16[256,2048]{1,0:T(8,128)(2,1)} collective-permute-done((bf16[256,2048]{1,0:T(8,128)(2,1)}, bf16[256,2048]{1,0:T(8,128)(2,1)}, u32[]{:S(2)}, u32[]{:S(2)}) %collective-permute-start.24) | collective-permute-done | bytes 1048608 | tf_op jit(solution)/shard_map/ppermute | solution.py:900
  313.6 27.5 %shard_map.246 = (bf16[1024,2048]{1,0:T(8,128)(2,1)}, bf16[1024,2048]{1,0:T(8,128)(2,1)}, bf16[1024,2048]{1,0:T(8,128)(2,1)}) custom-call(s32[12]{0:T(128)} %concatenate.45.refs_0_, bf16[256,2048]{1,0:T(8,128)(2,1)} %get-tuple-element.174.refs_1_.refs_8_.refs_5_, bf16[256,2048]{1,0:T(8,128)(2,1)} %get-tuple-element.175.refs_2_.refs_6_, ...), custom_call_target="tpu_custom_call" | custom-call | flops 343597383680 | bytes 754974720 | tf_op jit(solution)/shard_map/pallas_call | solution.py:66
  341.1 25.7 %shard_map.247.refs_5_ = bf16[8,256,2048]{2,1,0:T(8,128)(2,1)} custom-call(s32[12]{0:T(128)} %concatenate.45.refs_0_, bf16[256,2048]{1,0:T(8,128)(2,1)} %get-tuple-element.169.refs_1_, bf16[256,2048]{1,0:T(8,128)(2,1)} %get-tuple-element.170.refs_2_.refs_8_, bf16[256,2048]{1,0:T(8,128)(2,1)} %copy-done.42, bf16[256,2048]{1,0:T(8,128)(2,1)} %copy-done.43, ...), custom_call_target="tpu_custom_call" | custom-call | flops 343597383680 | bytes 503316480 | tf_op jit(solution)/shard_map/pallas_call | solution.py:66
  366.8 24.5 %shard_map.248 = (bf16[256,2048]{1,0:T(8,128)(2,1)}, bf16[256,2048]{1,0:T(8,128)(2,1)}, bf16[256,2048]{1,0:T(8,128)(2,1)}, bf16[256,2048]{1,0:T(8,128)(2,1)}) custom-call(s32[12]{0:T(128)} %concatenate.45.refs_0_, bf16[1024,2048]{1,0:T(8,128)(2,1)} %get-tuple-element.176.refs_1_.refs_10_, bf16[1024,2048]{1,0:T(8,128)(2,1)} %get-tuple-element.177.refs_10_.refs_11_.refs_2_, ...), custom_call_target="tpu_custom_call" | custom-call | flops 343597383680 | bytes 587202560 | tf_op jit(solution)/shard_map/pallas_call | solution.py:66
  391.8 24.4 %shard_map.249 = (bf16[256,2048]{1,0:T(8,128)(2,1)}, bf16[256,2048]{1,0:T(8,128)(2,1)}, bf16[256,2048]{1,0:T(8,128)(2,1)}, bf16[256,2048]{1,0:T(8,128)(2,1)}) custom-call(s32[12]{0:T(128)} %concatenate.45.refs_0_, bf16[1024,2048]{1,0:T(8,128)(2,1)} %get-tuple-element.172.refs_1_.refs_9_, bf16[1024,2048]{1,0:T(8,128)(2,1)} %get-tuple-element.173.refs_3_.refs_9_.refs_2_, ...), custom_call_target="tpu_custom_call" | custom-call | flops 343597383680 | bytes 587202560 | tf_op jit(solution)/shard_map/pallas_call | solution.py:66
  425.2 27.0 %shard_map.251 = (bf16[4,256,2048]{2,1,0:T(8,128)(2,1)}, bf16[4,256,2048]{2,1,0:T(8,128)(2,1)}) custom-call(s32[12]{0:T(128)} %concatenate.45.refs_0_, bf16[256,2048]{1,0:T(8,128)(2,1)} %get-tuple-element.169.refs_1_, bf16[256,2048]{1,0:T(8,128)(2,1)} %get-tuple-element.170.refs_2_.refs_8_, bf16[256,2048]{1,0:T(8,128)(2,1)} %copy-done.42, ...), custom_call_target="tpu_custom_call" | custom-call | flops 343597383680 | bytes 503316480 | tf_op jit(solution)/shard_map/pallas_call | solution.py:66
  452.7 27.0 %shard_map.252 = (bf16[4,256,2048]{2,1,0:T(8,128)(2,1)}, bf16[4,256,2048]{2,1,0:T(8,128)(2,1)}) custom-call(s32[12]{0:T(128)} %concatenate.45.refs_0_, bf16[256,2048]{1,0:T(8,128)(2,1)} %get-tuple-element.281.refs_1_, bf16[256,2048]{1,0:T(8,128)(2,1)} %get-tuple-element.280.refs_2_, bf16[256,2048]{1,0:T(8,128)(2,1)} %collective-permute-done.13.refs_3_, ...), custom_call_target="tpu_custom_call" | custom-call | flops 343597383680 | bytes 503316480 | tf_op jit(solution)/shard_map/pallas_call | solution.py:66
  492.4 13.8 %shard_map.254 = (bf16[256,2048]{1,0:T(8,128)(2,1)}, bf16[256,2048]{1,0:T(8,128)(2,1)}, bf16[256,2048]{1,0:T(8,128)(2,1)}, bf16[256,2048]{1,0:T(8,128)(2,1)}) custom-call(s32[12]{0:T(128)} %concatenate.45.refs_0_, bf16[1024,2048]{1,0:T(8,128)(2,1)} %get-tuple-element.188.refs_10_.refs_1_, bf16[2048,2048]{1,0:T(8,128)(2,1)} %refs_2_.4, ...), custom_call_target="tpu_custom_call" | custom-call | flops 171798691840 | bytes 335544320 | tf_op jit(solution)/shard_map/pallas_call | solution.py:66
  514.8 13.8 %shard_map.256 = (bf16[256,2048]{1,0:T(8,128)(2,1)}, bf16[256,2048]{1,0:T(8,128)(2,1)}, bf16[256,2048]{1,0:T(8,128)(2,1)}, bf16[256,2048]{1,0:T(8,128)(2,1)}) custom-call(s32[12]{0:T(128)} %concatenate.45.refs_0_, bf16[1024,2048]{1,0:T(8,128)(2,1)} %get-tuple-element.171.refs_9_.refs_1_, bf16[2048,2048]{1,0:T(8,128)(2,1)} %refs_2_.4, ...), custom_call_target="tpu_custom_call" | custom-call | flops 171798691840 | bytes 335544320 | tf_op jit(solution)/shard_map/pallas_call | solution.py:66
  582.7 12.4 %shard_map.261 = (f32[2048,128]{1,0:T(8,128)}, f32[2048,128]{1,0:T(8,128)}, f32[2048,128]{1,0:T(8,128)}) custom-call(s32[12]{0:T(128)} %concatenate.45.refs_0_, bf16[2048,512]{1,0:T(8,128)(2,1)} %get-tuple-element.142.refs_1_.refs_7_.refs_4_, bf16[2048,512]{1,0:T(8,128)(2,1)} %get-tuple-element.143.refs_1_.refs_2_.refs_5_, ...), custom_call_target="tpu_custom_call" | custom-call | flops 128849018880 | bytes 136314880 | tf_op jit(solution)/shard_map/pallas_call | solution.py:66
  598.2 12.6 %shard_map.262 = (f32[2048,128]{1,0:T(8,128)}, f32[2048,128]{1,0:T(8,128)}, f32[2048,128]{1,0:T(8,128)}) custom-call(s32[12]{0:T(128)} %concatenate.45.refs_0_, bf16[2048,512]{1,0:T(8,128)(2,1)} %get-tuple-element.142.refs_1_.refs_7_.refs_4_, bf16[2048,512]{1,0:T(8,128)(2,1)} %get-tuple-element.143.refs_1_.refs_2_.refs_5_, ...), custom_call_target="tpu_custom_call" | custom-call | flops 128849018880 | bytes 136314880 | tf_op jit(solution)/shard_map/pallas_call | solution.py:66
  610.8 12.6 %shard_map.263 = (f32[2048,128]{1,0:T(8,128)}, f32[2048,128]{1,0:T(8,128)}, f32[2048,128]{1,0:T(8,128)}) custom-call(s32[12]{0:T(128)} %concatenate.45.refs_0_, bf16[2048,512]{1,0:T(8,128)(2,1)} %get-tuple-element.142.refs_1_.refs_7_.refs_4_, bf16[2048,512]{1,0:T(8,128)(2,1)} %get-tuple-element.143.refs_1_.refs_2_.refs_5_, ...), custom_call_target="tpu_custom_call" | custom-call | flops 128849018880 | bytes 136314880 | tf_op jit(solution)/shard_map/pallas_call | solution.py:66
  629.9 12.8 %shard_map.264 = (f32[2048,128]{1,0:T(8,128)}, f32[2048,128]{1,0:T(8,128)}, f32[2048,128]{1,0:T(8,128)}) custom-call(s32[12]{0:T(128)} %concatenate.45.refs_0_, bf16[2048,512]{1,0:T(8,128)(2,1)} %get-tuple-element.142.refs_1_.refs_7_.refs_4_, bf16[2048,512]{1,0:T(8,128)(2,1)} %get-tuple-element.143.refs_1_.refs_2_.refs_5_, ...), custom_call_target="tpu_custom_call" | custom-call | flops 128849018880 | bytes 136314880 | tf_op jit(solution)/shard_map/pallas_call | solution.py:66
  649.4 18.6 %collective-permute-done.48 = bf16[4,4,128,128]{3,2,1,0:T(8,128)(2,1)S(1)} collective-permute-done((bf16[4,4,128,128]{3,2,1,0:T(8,128)(2,1)S(1)}, bf16[4,4,128,128]{3,2,1,0:T(8,128)(2,1)S(1)}, u32[]{:S(2)}, u32[]{:S(2)}) %collective-permute-start.48) | collective-permute-done | bytes 524320 | tf_op jit(solution)/shard_map/ppermute | solution.py:934
  693.9 12.4 %shard_map.267 = (bf16[4,256,512]{2,1,0:T(8,128)(2,1)}, bf16[4,256,512]{2,1,0:T(8,128)(2,1)}) custom-call(s32[12]{0:T(128)} %concatenate.45.refs_0_, bf16[256,2048]{1,0:T(8,128)(2,1)} %get-tuple-element.191.refs_1_, bf16[256,2048]{1,0:T(8,128)(2,1)} %get-tuple-element.192.refs_2_, bf16[256,2048]{1,0:T(8,128)(2,1)} %collective-permute-done.33.refs_3_, ...), custom_call_target="tpu_custom_call" | custom-call | flops 85899345920 | bytes 251658240 | tf_op jit(solution)/shard_map/pallas_call | solution.py:66
  708.6 14.2 %shard_map.268 = (bf16[2048,512]{1,0:T(8,128)(2,1)}, bf16[2048,512]{1,0:T(8,128)(2,1)}, bf16[2048,512]{1,0:T(8,128)(2,1)}) custom-call(s32[12]{0:T(128)} %concatenate.45.refs_0_, bf16[2048,512]{1,0:T(8,128)(2,1)} %get-tuple-element.142.refs_1_.refs_7_.refs_4_, bf16[2048,512]{1,0:T(8,128)(2,1)} %get-tuple-element.143.refs_1_.refs_2_.refs_5_, ...), custom_call_target="tpu_custom_call" | custom-call | flops 37580963840 | bytes 545259520 | tf_op jit(solution)/shard_map/pallas_call | solution.py:66
  722.8 12.0 %shard_map.269 = (bf16[4,256,512]{2,1,0:T(8,128)(2,1)}, bf16[4,256,512]{2,1,0:T(8,128)(2,1)}) custom-call(s32[12]{0:T(128)} %concatenate.45.refs_0_, bf16[256,2048]{1,0:T(8,128)(2,1)} %get-tuple-element.134.refs_1_.refs_7_, bf16[256,2048]{1,0:T(8,128)(2,1)} %get-tuple-element.135.refs_2_.refs_8_, bf16[256,2048]{1,0:T(8,128)(2,1)} %copy-done.37, ...), custom_call_target="tpu_custom_call" | custom-call | flops 85899345920 | bytes 251658240 | tf_op jit(solution)/shard_map/pallas_call | solution.py:66
  734.8 11.9 %shard_map.270 = (bf16[4,256,512]{2,1,0:T(8,128)(2,1)}, bf16[4,256,512]{2,1,0:T(8,128)(2,1)}) custom-call(s32[12]{0:T(128)} %concatenate.45.refs_0_, bf16[256,2048]{1,0:T(8,128)(2,1)} %get-tuple-element.134.refs_1_.refs_7_, bf16[256,2048]{1,0:T(8,128)(2,1)} %get-tuple-element.135.refs_2_.refs_8_, bf16[256,2048]{1,0:T(8,128)(2,1)} %copy-done.37, ...), custom_call_target="tpu_custom_call" | custom-call | flops 85899345920 | bytes 251658240 | tf_op jit(solution)/shard_map/pallas_call | solution.py:66
  755.7 12.2 %shard_map.272 = (bf16[256,2048]{1,0:T(8,128)(2,1)}, bf16[256,2048]{1,0:T(8,128)(2,1)}, bf16[256,2048]{1,0:T(8,128)(2,1)}, bf16[256,2048]{1,0:T(8,128)(2,1)}, f32[1,2048]{1,0:T(1,128)}) custom-call(s32[12]{0:T(128)} %concatenate.45.refs_0_, bf16[2048,512]{1,0:T(8,128)(2,1)} %get-tuple-element.238.refs_1_.refs_9_, ...), custom_call_target="tpu_custom_call" | custom-call | flops 128849018880 | bytes 272629760 | tf_op jit(solution)/shard_map/pallas_call | solution.py:66
  768.5 11.9 %shard_map.273 = (bf16[256,2048]{1,0:T(8,128)(2,1)}, bf16[256,2048]{1,0:T(8,128)(2,1)}, bf16[256,2048]{1,0:T(8,128)(2,1)}, bf16[256,2048]{1,0:T(8,128)(2,1)}, f32[1,2048]{1,0:T(1,128)}) custom-call(s32[12]{0:T(128)} %concatenate.45.refs_0_, bf16[2048,512]{1,0:T(8,128)(2,1)} %get-tuple-element.238.refs_1_.refs_9_, ...), custom_call_target="tpu_custom_call" | custom-call | flops 128849018880 | bytes 272629760 | tf_op jit(solution)/shard_map/pallas_call | solution.py:66
  798.7 12.0 %shard_map.276 = (bf16[4,256,512]{2,1,0:T(8,128)(2,1)}, bf16[4,256,512]{2,1,0:T(8,128)(2,1)}) custom-call(s32[12]{0:T(128)} %concatenate.45.refs_0_, bf16[256,2048]{1,0:T(8,128)(2,1)} %get-tuple-element.134.refs_1_.refs_7_, bf16[256,2048]{1,0:T(8,128)(2,1)} %get-tuple-element.135.refs_2_.refs_8_, bf16[256,2048]{1,0:T(8,128)(2,1)} %copy-done.37, ...), custom_call_target="tpu_custom_call" | custom-call | flops 85899345920 | bytes 251658240 | tf_op jit(solution)/shard_map/pallas_call | solution.py:66
  813.8 21.9 %collective-permute-done.59.refs_8_ = bf16[256,2048]{1,0:T(8,128)(2,1)} collective-permute-done((bf16[256,2048]{1,0:T(8,128)(2,1)}, bf16[256,2048]{1,0:T(8,128)(2,1)}, u32[]{:S(2)}, u32[]{:S(2)}) %collective-permute-start.59) | collective-permute-done | bytes 1048608 | tf_op jit(solution)/shard_map/ppermute | solution.py:900
  845.0 13.1 %reduce-scatter.12.cloned.1.call-done.refs_4_ = bf16[256,1536]{1,0:T(8,128)(2,1)} async-done(((bf16[1024,1536]{1,0:T(8,128)(2,1)}), bf16[256,1536]{1,0:T(8,128)(2,1)}) %reduce-scatter.12.cloned.1.call-update) | async-done | bytes 786448 | tf_op jit(solution)/shard_map/reduce_scatter | solution.py:920
  (308 shorter events, 329.1 us)
Async XLA Ops:
  7.2 163.4 %all-gather.3.cloned.1.call-start = ((), (), s32[]{:S(2)}) async-start(), calls=%async_computation.10 | async-start | bytes 2359296 | tf_op jit(solution)/shard_map/all_gather | solution.py:1020
  17.2 46.0 %collective-permute-start.1 = (bf16[256,2048]{1,0:T(8,128)(2,1)}, bf16[256,2048]{1,0:T(8,128)(2,1)S(1)}, u32[]{:S(2)}, u32[]{:S(2)}) collective-permute-start(bf16[256,2048]{1,0:T(8,128)(2,1)} %get-tuple-element.135.refs_2_.refs_8_), channel_id=1, source_target_pairs={{0,2},{1,3},{2,0},{3,1},{4,6},{5,7},{6,4},{7,5},{8,10},{9,11},{10,... | collective-permute-start | bytes 3145736 | tf_op jit(solution)/shard_map/ppermute | solution.py:900
  90.1 51.4 %collective-permute-start.14 = (bf16[256,2048]{1,0:T(8,128)(2,1)}, bf16[256,2048]{1,0:T(8,128)(2,1)}, u32[]{:S(2)}, u32[]{:S(2)}) collective-permute-start(bf16[256,2048]{1,0:T(8,128)(2,1)} %get-tuple-element.280.refs_2_), channel_id=1, source_target_pairs={{0,1},{1,0},{2,3},{3,2},{4,5},{5,4},{6,7},{7,6},{8,9},{9,8},{10,11... | collective-permute-start | bytes 3145736 | tf_op jit(solution)/shard_map/ppermute | solution.py:895
  90.1 51.4 %collective-permute-start.13 = (bf16[256,2048]{1,0:T(8,128)(2,1)}, bf16[256,2048]{1,0:T(8,128)(2,1)}, u32[]{:S(2)}, u32[]{:S(2)}) collective-permute-start(bf16[256,2048]{1,0:T(8,128)(2,1)} %get-tuple-element.281.refs_1_), channel_id=1, source_target_pairs={{0,1},{1,0},{2,3},{3,2},{4,5},{5,4},{6,7},{7,6},{8,9},{9,8},{10,11... | collective-permute-start | bytes 3145736 | tf_op jit(solution)/shard_map/ppermute | solution.py:895
  95.6 44.7 %collective-permute-start.10 = (bf16[256,2048]{1,0:T(8,128)(2,1)}, bf16[256,2048]{1,0:T(8,128)(2,1)}, u32[]{:S(2)}, u32[]{:S(2)}) collective-permute-start(bf16[256,2048]{1,0:T(8,128)(2,1)} %get-tuple-element.152), channel_id=1, source_target_pairs={{0,2},{1,3},{2,0},{3,1},{4,6},{5,7},{6,4},{7,5},{8,10},{9,11},{10,... | collective-permute-start | bytes 3145736 | tf_op jit(solution)/shard_map/ppermute | solution.py:900
  103.6 456.8 %reduce-scatter.6.cloned.1.call-start = ((), (), s32[]{:S(2)}) async-start(), calls=%async_computation.5 | async-start | bytes 10485760 | tf_op jit(solution)/shard_map/reduce_scatter | solution.py:920
  203.5 46.3 %collective-permute-start.20 = (bf16[256,2048]{1,0:T(8,128)(2,1)}, bf16[256,2048]{1,0:T(8,128)(2,1)S(1)}, u32[]{:S(2)}, u32[]{:S(2)}) collective-permute-start(bf16[256,2048]{1,0:T(8,128)(2,1)} %get-tuple-element.167.refs_9_), channel_id=1, source_target_pairs={{0,2},{1,3},{2,0},{3,1},{4,6},{5,7},{6,4},{7,5},{8,10},{9,11},{10,... | collective-permute-start | bytes 3145736 | tf_op jit(solution)/shard_map/ppermute | solution.py:900
  261.1 46.4 %collective-permute-start.24 = (bf16[256,2048]{1,0:T(8,128)(2,1)}, bf16[256,2048]{1,0:T(8,128)(2,1)}, u32[]{:S(2)}, u32[]{:S(2)}) collective-permute-start(bf16[256,2048]{1,0:T(8,128)(2,1)} %get-tuple-element.170.refs_2_.refs_8_), channel_id=1, source_target_pairs={{0,2},{1,3},{2,0},{3,1},{4,6},{5,7},{6,4},{7,5},{8,10},{9,11},{10,... | collective-permute-start | bytes 3145736 | tf_op jit(solution)/shard_map/ppermute | solution.py:900
  416.2 292.4 %reduce-scatter.8.cloned.1.call-start = ((), (), s32[]{:S(2)}) async-start(), calls=%async_computation.6 | async-start | bytes 5242880 | tf_op jit(solution)/shard_map/reduce_scatter | solution.py:920
  416.3 63.4 %collective-permute-start.27 = (bf16[256,2048]{1,0:T(8,128)(2,1)}, bf16[256,2048]{1,0:T(8,128)(2,1)}, u32[]{:S(2)}, u32[]{:S(2)}) collective-permute-start(bf16[256,2048]{1,0:T(8,128)(2,1)} %get-tuple-element.181), channel_id=1, source_target_pairs={{0,1},{1,0},{2,3},{3,2},{4,5},{5,4},{6,7},{7,6},{8,9},{9,8},{10,11... | collective-permute-start | bytes 3145736 | tf_op jit(solution)/shard_map/ppermute | solution.py:895
  416.5 63.2 %collective-permute-start.28 = (bf16[256,2048]{1,0:T(8,128)(2,1)}, bf16[256,2048]{1,0:T(8,128)(2,1)}, u32[]{:S(2)}, u32[]{:S(2)}) collective-permute-start(bf16[256,2048]{1,0:T(8,128)(2,1)} %get-tuple-element.182.refs_5_), channel_id=1, source_target_pairs={{0,1},{1,0},{2,3},{3,2},{4,5},{5,4},{6,7},{7,6},{8,9},{9,8},{10,11... | collective-permute-start | bytes 3145736 | tf_op jit(solution)/shard_map/ppermute | solution.py:895
  423.2 56.5 %collective-permute-start.31 = (bf16[256,2048]{1,0:T(8,128)(2,1)}, bf16[256,2048]{1,0:T(8,128)(2,1)}, u32[]{:S(2)}, u32[]{:S(2)}) collective-permute-start(bf16[256,2048]{1,0:T(8,128)(2,1)} %get-tuple-element.186), channel_id=1, source_target_pairs={{0,2},{1,3},{2,0},{3,1},{4,6},{5,7},{6,4},{7,5},{8,10},{9,11},{10,... | collective-permute-start | bytes 3145736 | tf_op jit(solution)/shard_map/ppermute | solution.py:900
  424.6 55.1 %collective-permute-start.32 = (bf16[256,2048]{1,0:T(8,128)(2,1)}, bf16[256,2048]{1,0:T(8,128)(2,1)}, u32[]{:S(2)}, u32[]{:S(2)}) collective-permute-start(bf16[256,2048]{1,0:T(8,128)(2,1)} %get-tuple-element.187.refs_11_), channel_id=1, source_target_pairs={{0,2},{1,3},{2,0},{3,1},{4,6},{5,7},{6,4},{7,5},{8,10},{9,11},{10,... | collective-permute-start | bytes 3145736 | tf_op jit(solution)/shard_map/ppermute | solution.py:900
  452.2 93.9 %collective-permute-start.43 = (bf16[4,256,2048]{2,1,0:T(8,128)(2,1)}, bf16[4,256,2048]{2,1,0:T(8,128)(2,1)}, u32[]{:S(2)}, u32[]{:S(2)}) collective-permute-start(bf16[4,256,2048]{2,1,0:T(8,128)(2,1)} %get-tuple-element.207), channel_id=1, source_target_pairs={{0,4},{4,0},{8,12},{12,8},{16,20},{20,16},{24,28},{28,24},{1,5},{5... | collective-permute-start | bytes 12582920 | tf_op jit(solution)/shard_map/ppermute | solution.py:914
  490.1 38.4 %collective-permute-start.39 = (bf16[256,2048]{1,0:T(8,128)(2,1)}, bf16[256,2048]{1,0:T(8,128)(2,1)}, u32[]{:S(2)}, u32[]{:S(2)}) collective-permute-start(bf16[256,2048]{1,0:T(8,128)(2,1)} %get-tuple-element.191.refs_1_), channel_id=1, source_target_pairs={{0,2},{1,3},{2,0},{3,1},{4,6},{5,7},{6,4},{7,5},{8,10},{9,11},{10,... | collective-permute-start | bytes 3145736 | tf_op jit(solution)/shard_map/ppermute | solution.py:900
  491.7 45.4 %collective-permute-start.40 = (bf16[256,2048]{1,0:T(8,128)(2,1)}, bf16[256,2048]{1,0:T(8,128)(2,1)}, u32[]{:S(2)}, u32[]{:S(2)}) collective-permute-start(bf16[256,2048]{1,0:T(8,128)(2,1)} %get-tuple-element.192.refs_2_), channel_id=1, source_target_pairs={{0,2},{1,3},{2,0},{3,1},{4,6},{5,7},{6,4},{7,5},{8,10},{9,11},{10,... | collective-permute-start | bytes 3145736 | tf_op jit(solution)/shard_map/ppermute | solution.py:900
  538.4 104.3 %collective-permute-start.49 = (bf16[4,256,2048]{2,1,0:T(8,128)(2,1)}, bf16[4,256,2048]{2,1,0:T(8,128)(2,1)}, u32[]{:S(2)}, u32[]{:S(2)}) collective-permute-start(bf16[4,256,2048]{2,1,0:T(8,128)(2,1)} %get-tuple-element.227), channel_id=1, source_target_pairs={{0,4},{4,0},{8,12},{12,8},{16,20},{20,16},{24,28},{28,24},{1,5},{5... | collective-permute-start | bytes 12582920 | tf_op jit(solution)/shard_map/ppermute | solution.py:914
  539.9 35.3 %collective-permute-start.38 = (bf16[256,2048]{1,0:T(8,128)(2,1)}, bf16[256,2048]{1,0:T(8,128)(2,1)S(1)}, u32[]{:S(2)}, u32[]{:S(2)}) collective-permute-start(bf16[256,2048]{1,0:T(8,128)(2,1)} %get-tuple-element.194.refs_10_), channel_id=1, source_target_pairs={{0,1},{1,0},{2,3},{3,2},{4,5},{5,4},{6,7},{7,6},{8,9},{9,8},{10,11... | collective-permute-start | bytes 3145736 | tf_op jit(solution)/shard_map/ppermute | solution.py:895
  552.8 240.1 %reduce-scatter.10.cloned.1.call-start = ((), (), s32[]{:S(2)}) async-start(), calls=%async_computation.7 | async-start | bytes 5242880 | tf_op jit(solution)/shard_map/reduce_scatter | solution.py:920
  562.8 107.2 %collective-permute-start.50 = (bf16[256,2048]{1,0:T(8,128)(2,1)}, bf16[256,2048]{1,0:T(8,128)(2,1)}, u32[]{:S(2)}, u32[]{:S(2)}) collective-permute-start(bf16[256,2048]{1,0:T(8,128)(2,1)} %constant_dynamic-slice_fusion), channel_id=1, source_target_pairs={{0,4},{4,0},{8,12},{12,8},{16,20},{20,16},{24,28},{28,24},{1,5},{5... | collective-permute-start | bytes 3145736 | tf_op jit(solution)/shard_map/ppermute | solution.py:914
  628.5 39.5 %collective-permute-start.48 = (bf16[4,4,128,128]{3,2,1,0:T(8,128)(2,1)S(1)}, bf16[4,4,128,128]{3,2,1,0:T(8,128)(2,1)S(1)}, u32[]{:S(2)}, u32[]{:S(2)}) collective-permute-start(bf16[4,4,128,128]{3,2,1,0:T(8,128)(2,1)S(1)} %pad_maximum_fusion.1.refs_8_), channel_id=1, source_target_pairs={{0,4},{4,0},{8,12},{12,8},{16,20},{20,16},{24,28},{28,24},{1,5},{5... | collective-permute-start | bytes 1572872 | tf_op jit(solution)/shard_map/ppermute | solution.py:934
  690.7 56.2 %collective-permute-start.36 = (bf16[256,2048]{1,0:T(8,128)(2,1)}, bf16[256,2048]{1,0:T(8,128)(2,1)}, u32[]{:S(2)}, u32[]{:S(2)}) collective-permute-start(bf16[256,2048]{1,0:T(8,128)(2,1)} %get-tuple-element.199.refs_3_), channel_id=1, source_target_pairs={{0,1},{1,0},{2,3},{3,2},{4,5},{5,4},{6,7},{7,6},{8,9},{9,8},{10,11... | collective-permute-start | bytes 3145736 | tf_op jit(solution)/shard_map/ppermute | solution.py:895
  690.7 56.0 %collective-permute-start.35 = (bf16[256,2048]{1,0:T(8,128)(2,1)}, bf16[256,2048]{1,0:T(8,128)(2,1)}, u32[]{:S(2)}, u32[]{:S(2)}) collective-permute-start(bf16[256,2048]{1,0:T(8,128)(2,1)} %get-tuple-element.198), channel_id=1, source_target_pairs={{0,1},{1,0},{2,3},{3,2},{4,5},{5,4},{6,7},{7,6},{8,9},{9,8},{10,11... | collective-permute-start | bytes 3145736 | tf_op jit(solution)/shard_map/ppermute | solution.py:895
  691.2 57.6 %collective-permute-start.45 = (bf16[256,2048]{1,0:T(8,128)(2,1)}, bf16[256,2048]{1,0:T(8,128)(2,1)}, u32[]{:S(2)}, u32[]{:S(2)}) collective-permute-start(bf16[256,2048]{1,0:T(8,128)(2,1)} %get-tuple-element.210.refs_7_), channel_id=1, source_target_pairs={{0,2},{1,3},{2,0},{3,1},{4,6},{5,7},{6,4},{7,5},{8,10},{9,11},{10,... | collective-permute-start | bytes 3145736 | tf_op jit(solution)/shard_map/ppermute | solution.py:900
  692.7 56.1 %collective-permute-start.44 = (bf16[256,2048]{1,0:T(8,128)(2,1)}, bf16[256,2048]{1,0:T(8,128)(2,1)}, u32[]{:S(2)}, u32[]{:S(2)}) collective-permute-start(bf16[256,2048]{1,0:T(8,128)(2,1)} %get-tuple-element.209), channel_id=1, source_target_pairs={{0,2},{1,3},{2,0},{3,1},{4,6},{5,7},{6,4},{7,5},{8,10},{9,11},{10,... | collective-permute-start | bytes 3145736 | tf_op jit(solution)/shard_map/ppermute | solution.py:900
  693.2 164.9 %reduce-scatter.12.cloned.1.call-start = ((), (), s32[]{:S(2)}) async-start(), calls=%async_computation.8 | async-start | bytes 3932160 | tf_op jit(solution)/shard_map/reduce_scatter | solution.py:920
  706.3 81.2 %collective-permute-start.60 = (bf16[4,256,512]{2,1,0:T(8,128)(2,1)}, bf16[4,256,512]{2,1,0:T(8,128)(2,1)}, u32[]{:S(2)}, u32[]{:S(2)}) collective-permute-start(bf16[4,256,512]{2,1,0:T(8,128)(2,1)} %get-tuple-element.251), channel_id=1, source_target_pairs={{0,4},{4,0},{8,12},{12,8},{16,20},{20,16},{24,28},{28,24},{1,5},{5... | collective-permute-start | bytes 3145736 | tf_op jit(solution)/shard_map/ppermute | solution.py:914
  746.7 42.4 %collective-permute-start.61 = (bf16[4,256,512]{2,1,0:T(8,128)(2,1)}, bf16[4,256,512]{2,1,0:T(8,128)(2,1)}, u32[]{:S(2)}, u32[]{:S(2)}) collective-permute-start(bf16[4,256,512]{2,1,0:T(8,128)(2,1)} %get-tuple-element.252), channel_id=1, source_target_pairs={{0,4},{4,0},{8,12},{12,8},{16,20},{20,16},{24,28},{28,24},{1,5},{5... | collective-permute-start | bytes 3145736 | tf_op jit(solution)/shard_map/ppermute | solution.py:914
  746.9 46.0 %collective-permute-start.62 = (bf16[4,256,512]{2,1,0:T(8,128)(2,1)}, bf16[4,256,512]{2,1,0:T(8,128)(2,1)}, u32[]{:S(2)}, u32[]{:S(2)}) collective-permute-start(bf16[4,256,512]{2,1,0:T(8,128)(2,1)} %get-tuple-element.253), channel_id=1, source_target_pairs={{0,4},{4,0},{8,12},{12,8},{16,20},{20,16},{24,28},{28,24},{1,5},{5... | collective-permute-start | bytes 3145736 | tf_op jit(solution)/shard_map/ppermute | solution.py:914
  789.1 46.6 %collective-permute-start.59 = (bf16[256,2048]{1,0:T(8,128)(2,1)}, bf16[256,2048]{1,0:T(8,128)(2,1)}, u32[]{:S(2)}, u32[]{:S(2)}) collective-permute-start(bf16[256,2048]{1,0:T(8,128)(2,1)} %get-tuple-element.250.refs_7_), channel_id=1, source_target_pairs={{0,2},{1,3},{2,0},{3,1},{4,6},{5,7},{6,4},{7,5},{8,10},{9,11},{10,... | collective-permute-start | bytes 3145736 | tf_op jit(solution)/shard_map/ppermute | solution.py:900
  798.7 92.0 %reduce-scatter.14.cloned.1.call-start = ((), (), s32[]{:S(2)}) async-start(), calls=%async_computation.9 | async-start | bytes 1310720 | tf_op jit(solution)/shard_map/reduce_scatter | solution.py:920
  810.7 34.3 %collective-permute-start.68 = (bf16[4,256,512]{2,1,0:T(8,128)(2,1)}, bf16[4,256,512]{2,1,0:T(8,128)(2,1)}, u32[]{:S(2)}, u32[]{:S(2)}) collective-permute-start(bf16[4,256,512]{2,1,0:T(8,128)(2,1)} %get-tuple-element.255), channel_id=1, source_target_pairs={{0,4},{4,0},{8,12},{12,8},{16,20},{20,16},{24,28},{28,24},{1,5},{5... | collective-permute-start | bytes 3145736 | tf_op jit(solution)/shard_map/ppermute | solution.py:914
  (89 other events, 1152.5 us)
Sparse Core Ops, SparseCore 0:
  103.7 50.2 all-gather.2
  416.4 144.0 reduce-scatter.5
  563.3 85.8 reduce-scatter.7
  693.4 75.5 reduce-scatter.9
  798.7 59.3 reduce-scatter.11
  862.6 28.0 reduce-scatter.13

commit v4 on v3

--- a/solution.py
+++ b/solution.py
@@ -1089,7 +1089,6 @@
         pass
     pair_down = pair_call(sc, [(far_down, near_down)])
     sum_down = sum_z(pair_down)
-    require(sum_up)
     memory_cot, norm_part = memory_cot_call(sc, gathered, all_maps, all_cots, q, k, grad_read, memory, norm)
     steps = share_steps(jnp.concatenate([norm_part.reshape(hh, HEAD), jnp.zeros((8 - hh, HEAD), F32)]))
     require(next(steps))

time: 909 us -> 885 us (0.974)
  waiting for transfers between devices: 216 us -> 195 us
    ppermute x9, waiting for transfers between devices: 27.9 us -> 12.1 us  [share_steps(): lax.ppermute(x, 'dp', [(i, i ^ step) for i in range(count)])]
  transfers between devices with their start and end apart: 75 -> 75, of which waited for: 31 -> 29; matrix products, arithmetic and copies ran while one was open for 3% -> 3% of each run, Pallas kernels for 50% -> 52%
where the time goes in v4:
time: 885 us; the launch traced here: 876 us
  Pallas kernels  573 us (65%)
  waiting for transfers between devices  195 us (22%)
  starting transfers between devices  53.3 us (6%)
  local copies, waits for them, and re-layouts  24.5 us (3%)
  between operations  16.4 us (2%)
  other arithmetic  14.3 us (2%)
    pallas_call x50, Pallas kernels, run(): out = made(*operands, *ORDERED)  573 us
    ppermute x16, waiting for transfers between devices, shift_chip(): lax.ppermute(x, 'tensor', [(i, (i + 2 * j) % count) for i in range(count)])  131 us
    reduce_scatter x5, waiting for transfers between devices, sum_z(): lax.psum_scatter(x, 'dp', scatter_dimension=0, axis_index_groups=groups,...  23.2 us
    unnamed x92, local copies, waits for them, and re-layouts  17.8 us
  transfers between devices with their start and end apart: 75, of which 29 were waited for; matrix products, arithmetic and copies ran while one was open for 3% of the time, Pallas kernels for 52%

profile of v4, /device:TPU:0, one launch (start us, length us, event | category | flops | bytes accessed | tf_op | source)
XLA Modules:
  0.0 875.6 jit_solution(7565100794688925809)
XLA Ops:
  25.3 12.8 %shard_map.230 = (bf16[2048,512]{1,0:T(8,128)(2,1)}, bf16[2048,512]{1,0:T(8,128)(2,1)}, bf16[2048,512]{1,0:T(8,128)(2,1)}, f32[1,512]{1,0:T(1,128)}) custom-call(s32[12]{0:T(128)} %concatenate.45.refs_0_, bf16[256,2048]{1,0:T(8,128)(2,1)} %get-tuple-element.134.refs_1_.refs_7_, bf16[256,2048]{1,0:T(8,128)(2,1)} %get-tuple-element.135.refs_2_.refs_8_, ...), custom_call_target="tpu_custom_call" | custom-call | flops 128849018880 | bytes 272629760 | tf_op jit(solution)/shard_map/pallas_call | solution.py:66
  41.4 21.8 %collective-permute-done.1.refs_2_ = bf16[256,2048]{1,0:T(8,128)(2,1)S(1)} collective-permute-done((bf16[256,2048]{1,0:T(8,128)(2,1)}, bf16[256,2048]{1,0:T(8,128)(2,1)S(1)}, u32[]{:S(2)}, u32[]{:S(2)}) %collective-permute-start.1) | collective-permute-done | bytes 1048608 | tf_op jit(solution)/shard_map/ppermute | solution.py:900
  70.3 12.6 %shard_map.232 = (bf16[2048,512]{1,0:T(8,128)(2,1)}, bf16[2048,512]{1,0:T(8,128)(2,1)}, bf16[2048,512]{1,0:T(8,128)(2,1)}, f32[1,512]{1,0:T(1,128)}) custom-call(s32[12]{0:T(128)} %concatenate.45.refs_0_, bf16[256,2048]{1,0:T(8,128)(2,1)} %get-tuple-element.137.refs_1_.refs_11_.refs_5_.refs_7_, ...), custom_call_target="tpu_custom_call", output_to_operand_aliasing={{0}: (8, {}), {1}: (9, {}), {2}: (10, {})} | custom-call | flops 128849018880 | bytes 272629760 | tf_op jit(solution)/shard_map/pallas_call | solution.py:66
  125.7 14.6 %collective-permute-done.10.refs_2_ = bf16[256,2048]{1,0:T(8,128)(2,1)} collective-permute-done((bf16[256,2048]{1,0:T(8,128)(2,1)}, bf16[256,2048]{1,0:T(8,128)(2,1)}, u32[]{:S(2)}, u32[]{:S(2)}) %collective-permute-start.10) | collective-permute-done | bytes 1048608 | tf_op jit(solution)/shard_map/ppermute | solution.py:900
  141.5 14.3 %shard_map.237.refs_6_.refs_7_ = bf16[1024,2048]{1,0:T(8,128)(2,1)} custom-call(s32[12]{0:T(128)} %concatenate.45.refs_0_, bf16[256,2048]{1,0:T(8,128)(2,1)} %get-tuple-element.281.refs_1_, bf16[256,2048]{1,0:T(8,128)(2,1)} %get-tuple-element.280.refs_2_, bf16[256,2048]{1,0:T(8,128)(2,1)} %collective-permute-done.13.refs_3_, ...), custom_call_target="tpu_custom_call" | custom-call | flops 171798691840 | bytes 335544320 | tf_op jit(solution)/shard_map/pallas_call | solution.py:66
  155.8 14.7 %shard_map.238.refs_3_.refs_7_ = bf16[1024,2048]{1,0:T(8,128)(2,1)} custom-call(s32[12]{0:T(128)} %concatenate.45.refs_0_, bf16[256,2048]{1,0:T(8,128)(2,1)} %get-tuple-element.154.refs_6_.refs_1_.refs_5_, bf16[256,2048]{1,0:T(8,128)(2,1)} %get-tuple-element.155.refs_2_.refs_6_, bf16[256,2048]{1,0:T(8,128)(2,1)} %collective-permute-done.11.refs_3_.refs_7_, ...), custom_call_target="tpu_custom_call" | custom-call | flops 171798691840 | bytes 335544320 | tf_op jit(solution)/shard_map/pallas_call | solution.py:66
  204.1 24.2 %collective-permute-done.19.refs_6_ = bf16[256,2048]{1,0:T(8,128)(2,1)S(1)} collective-permute-done((bf16[256,2048]{1,0:T(8,128)(2,1)}, bf16[256,2048]{1,0:T(8,128)(2,1)S(1)}, u32[]{:S(2)}, u32[]{:S(2)}) %collective-permute-start.19) | collective-permute-done | bytes 1048608 | tf_op jit(solution)/shard_map/ppermute | solution.py:900
  228.3 21.6 %collective-permute-done.20.refs_7_ = bf16[256,2048]{1,0:T(8,128)(2,1)S(1)} collective-permute-done((bf16[256,2048]{1,0:T(8,128)(2,1)}, bf16[256,2048]{1,0:T(8,128)(2,1)S(1)}, u32[]{:S(2)}, u32[]{:S(2)}) %collective-permute-start.20) | collective-permute-done | bytes 1048608 | tf_op jit(solution)/shard_map/ppermute | solution.py:900
  264.5 27.3 %shard_map.244 = (bf16[1024,2048]{1,0:T(8,128)(2,1)}, bf16[1024,2048]{1,0:T(8,128)(2,1)}, bf16[1024,2048]{1,0:T(8,128)(2,1)}) custom-call(s32[12]{0:T(128)} %concatenate.45.refs_0_, bf16[256,2048]{1,0:T(8,128)(2,1)} %get-tuple-element.169.refs_1_, bf16[256,2048]{1,0:T(8,128)(2,1)} %get-tuple-element.170.refs_2_.refs_8_, bf16[256,2048]{1,0:T(8,128)(2,1)} %copy-done.40, ...), custom_call_target="tpu_custom_call" | custom-call | flops 343597383680 | bytes 754974720 | tf_op jit(solution)/shard_map/pallas_call | solution.py:66
  291.8 15.8 %collective-permute-done.24.refs_2_ = bf16[256,2048]{1,0:T(8,128)(2,1)} collective-permute-done((bf16[256,2048]{1,0:T(8,128)(2,1)}, bf16[256,2048]{1,0:T(8,128)(2,1)}, u32[]{:S(2)}, u32[]{:S(2)}) %collective-permute-start.24) | collective-permute-done | bytes 1048608 | tf_op jit(solution)/shard_map/ppermute | solution.py:900
  313.6 27.5 %shard_map.246 = (bf16[1024,2048]{1,0:T(8,128)(2,1)}, bf16[1024,2048]{1,0:T(8,128)(2,1)}, bf16[1024,2048]{1,0:T(8,128)(2,1)}) custom-call(s32[12]{0:T(128)} %concatenate.45.refs_0_, bf16[256,2048]{1,0:T(8,128)(2,1)} %get-tuple-element.174.refs_1_.refs_8_.refs_5_, bf16[256,2048]{1,0:T(8,128)(2,1)} %get-tuple-element.175.refs_2_.refs_6_, ...), custom_call_target="tpu_custom_call" | custom-call | flops 343597383680 | bytes 754974720 | tf_op jit(solution)/shard_map/pallas_call | solution.py:66
  341.1 25.8 %shard_map.247.refs_5_ = bf16[8,256,2048]{2,1,0:T(8,128)(2,1)} custom-call(s32[12]{0:T(128)} %concatenate.45.refs_0_, bf16[256,2048]{1,0:T(8,128)(2,1)} %get-tuple-element.169.refs_1_, bf16[256,2048]{1,0:T(8,128)(2,1)} %get-tuple-element.170.refs_2_.refs_8_, bf16[256,2048]{1,0:T(8,128)(2,1)} %copy-done.40, bf16[256,2048]{1,0:T(8,128)(2,1)} %copy-done.41, ...), custom_call_target="tpu_custom_call" | custom-call | flops 343597383680 | bytes 503316480 | tf_op jit(solution)/shard_map/pallas_call | solution.py:66
  366.9 24.5 %shard_map.248 = (bf16[256,2048]{1,0:T(8,128)(2,1)}, bf16[256,2048]{1,0:T(8,128)(2,1)}, bf16[256,2048]{1,0:T(8,128)(2,1)}, bf16[256,2048]{1,0:T(8,128)(2,1)}) custom-call(s32[12]{0:T(128)} %concatenate.45.refs_0_, bf16[1024,2048]{1,0:T(8,128)(2,1)} %get-tuple-element.176.refs_1_.refs_10_, bf16[1024,2048]{1,0:T(8,128)(2,1)} %get-tuple-element.177.refs_10_.refs_11_.refs_2_, ...), custom_call_target="tpu_custom_call" | custom-call | flops 343597383680 | bytes 587202560 | tf_op jit(solution)/shard_map/pallas_call | solution.py:66
  391.9 24.4 %shard_map.249 = (bf16[256,2048]{1,0:T(8,128)(2,1)}, bf16[256,2048]{1,0:T(8,128)(2,1)}, bf16[256,2048]{1,0:T(8,128)(2,1)}, bf16[256,2048]{1,0:T(8,128)(2,1)}) custom-call(s32[12]{0:T(128)} %concatenate.45.refs_0_, bf16[1024,2048]{1,0:T(8,128)(2,1)} %get-tuple-element.172.refs_1_.refs_9_, bf16[1024,2048]{1,0:T(8,128)(2,1)} %get-tuple-element.173.refs_3_.refs_9_.refs_2_, ...), custom_call_target="tpu_custom_call" | custom-call | flops 343597383680 | bytes 587202560 | tf_op jit(solution)/shard_map/pallas_call | solution.py:66
  425.3 27.0 %shard_map.251 = (bf16[4,256,2048]{2,1,0:T(8,128)(2,1)}, bf16[4,256,2048]{2,1,0:T(8,128)(2,1)}) custom-call(s32[12]{0:T(128)} %concatenate.45.refs_0_, bf16[256,2048]{1,0:T(8,128)(2,1)} %get-tuple-element.169.refs_1_, bf16[256,2048]{1,0:T(8,128)(2,1)} %get-tuple-element.170.refs_2_.refs_8_, bf16[256,2048]{1,0:T(8,128)(2,1)} %copy-done.40, ...), custom_call_target="tpu_custom_call" | custom-call | flops 343597383680 | bytes 503316480 | tf_op jit(solution)/shard_map/pallas_call | solution.py:66
  452.7 27.1 %shard_map.252 = (bf16[4,256,2048]{2,1,0:T(8,128)(2,1)}, bf16[4,256,2048]{2,1,0:T(8,128)(2,1)}) custom-call(s32[12]{0:T(128)} %concatenate.45.refs_0_, bf16[256,2048]{1,0:T(8,128)(2,1)} %get-tuple-element.281.refs_1_, bf16[256,2048]{1,0:T(8,128)(2,1)} %get-tuple-element.280.refs_2_, bf16[256,2048]{1,0:T(8,128)(2,1)} %collective-permute-done.13.refs_3_, ...), custom_call_target="tpu_custom_call" | custom-call | flops 343597383680 | bytes 503316480 | tf_op jit(solution)/shard_map/pallas_call | solution.py:66
  492.6 13.8 %shard_map.254 = (bf16[256,2048]{1,0:T(8,128)(2,1)}, bf16[256,2048]{1,0:T(8,128)(2,1)}, bf16[256,2048]{1,0:T(8,128)(2,1)}, bf16[256,2048]{1,0:T(8,128)(2,1)}) custom-call(s32[12]{0:T(128)} %concatenate.45.refs_0_, bf16[1024,2048]{1,0:T(8,128)(2,1)} %get-tuple-element.188.refs_10_.refs_1_, bf16[2048,2048]{1,0:T(8,128)(2,1)} %refs_2_.4, ...), custom_call_target="tpu_custom_call" | custom-call | flops 171798691840 | bytes 335544320 | tf_op jit(solution)/shard_map/pallas_call | solution.py:66
  514.9 13.8 %shard_map.256 = (bf16[256,2048]{1,0:T(8,128)(2,1)}, bf16[256,2048]{1,0:T(8,128)(2,1)}, bf16[256,2048]{1,0:T(8,128)(2,1)}, bf16[256,2048]{1,0:T(8,128)(2,1)}) custom-call(s32[12]{0:T(128)} %concatenate.45.refs_0_, bf16[1024,2048]{1,0:T(8,128)(2,1)} %get-tuple-element.171.refs_9_.refs_1_, bf16[2048,2048]{1,0:T(8,128)(2,1)} %refs_2_.4, ...), custom_call_target="tpu_custom_call" | custom-call | flops 171798691840 | bytes 335544320 | tf_op jit(solution)/shard_map/pallas_call | solution.py:66
  578.8 12.4 %shard_map.261 = (f32[2048,128]{1,0:T(8,128)}, f32[2048,128]{1,0:T(8,128)}, f32[2048,128]{1,0:T(8,128)}) custom-call(s32[12]{0:T(128)} %concatenate.45.refs_0_, bf16[2048,512]{1,0:T(8,128)(2,1)} %get-tuple-element.142.refs_1_.refs_7_.refs_4_, bf16[2048,512]{1,0:T(8,128)(2,1)} %get-tuple-element.143.refs_1_.refs_2_.refs_5_, ...), custom_call_target="tpu_custom_call" | custom-call | flops 128849018880 | bytes 136314880 | tf_op jit(solution)/shard_map/pallas_call | solution.py:66
  594.1 12.6 %shard_map.262 = (f32[2048,128]{1,0:T(8,128)}, f32[2048,128]{1,0:T(8,128)}, f32[2048,128]{1,0:T(8,128)}) custom-call(s32[12]{0:T(128)} %concatenate.45.refs_0_, bf16[2048,512]{1,0:T(8,128)(2,1)} %get-tuple-element.142.refs_1_.refs_7_.refs_4_, bf16[2048,512]{1,0:T(8,128)(2,1)} %get-tuple-element.143.refs_1_.refs_2_.refs_5_, ...), custom_call_target="tpu_custom_call" | custom-call | flops 128849018880 | bytes 136314880 | tf_op jit(solution)/shard_map/pallas_call | solution.py:66
  606.7 12.5 %shard_map.263 = (f32[2048,128]{1,0:T(8,128)}, f32[2048,128]{1,0:T(8,128)}, f32[2048,128]{1,0:T(8,128)}) custom-call(s32[12]{0:T(128)} %concatenate.45.refs_0_, bf16[2048,512]{1,0:T(8,128)(2,1)} %get-tuple-element.142.refs_1_.refs_7_.refs_4_, bf16[2048,512]{1,0:T(8,128)(2,1)} %get-tuple-element.143.refs_1_.refs_2_.refs_5_, ...), custom_call_target="tpu_custom_call" | custom-call | flops 128849018880 | bytes 136314880 | tf_op jit(solution)/shard_map/pallas_call | solution.py:66
  627.4 12.7 %shard_map.264 = (f32[2048,128]{1,0:T(8,128)}, f32[2048,128]{1,0:T(8,128)}, f32[2048,128]{1,0:T(8,128)}) custom-call(s32[12]{0:T(128)} %concatenate.45.refs_0_, bf16[2048,512]{1,0:T(8,128)(2,1)} %get-tuple-element.142.refs_1_.refs_7_.refs_4_, bf16[2048,512]{1,0:T(8,128)(2,1)} %get-tuple-element.143.refs_1_.refs_2_.refs_5_, ...), custom_call_target="tpu_custom_call" | custom-call | flops 128849018880 | bytes 136314880 | tf_op jit(solution)/shard_map/pallas_call | solution.py:66
  649.0 11.6 %shard_map.266 = (f32[4,128,128]{2,1,0:T(8,128)}, f32[4,1,128]{2,1,0:T(1,128)}) custom-call(s32[12]{0:T(128)} %concatenate.45.refs_0_, f32[8,8,128]{2,1,0:T(8,128)} %pad_maximum_fusion.3.refs_3_.refs_1_.refs_20_, bf16[8,2,4,128,128]{4,3,2,1,0:T(8,128)(2,1)} %bitcast.45, bf16[8,4,128,128]{3,2,1,0:T(8,128)(2,1)} %pad_maximum_fusion.refs_3_, ...), custom_call_target="tpu_custom_call" | custom-call | flops 21474836480 | bytes 125829120 | tf_op jit(solution)/shard_map/pallas_call | solution.py:66
  670.3 12.3 %shard_map.267 = (bf16[4,256,512]{2,1,0:T(8,128)(2,1)}, bf16[4,256,512]{2,1,0:T(8,128)(2,1)}) custom-call(s32[12]{0:T(128)} %concatenate.45.refs_0_, bf16[256,2048]{1,0:T(8,128)(2,1)} %get-tuple-element.191.refs_1_, bf16[256,2048]{1,0:T(8,128)(2,1)} %get-tuple-element.192.refs_2_, bf16[256,2048]{1,0:T(8,128)(2,1)} %collective-permute-done.33.refs_3_, ...), custom_call_target="tpu_custom_call" | custom-call | flops 85899345920 | bytes 251658240 | tf_op jit(solution)/shard_map/pallas_call | solution.py:66
  684.7 14.2 %shard_map.268 = (bf16[2048,512]{1,0:T(8,128)(2,1)}, bf16[2048,512]{1,0:T(8,128)(2,1)}, bf16[2048,512]{1,0:T(8,128)(2,1)}) custom-call(s32[12]{0:T(128)} %concatenate.45.refs_0_, bf16[2048,512]{1,0:T(8,128)(2,1)} %get-tuple-element.142.refs_1_.refs_7_.refs_4_, bf16[2048,512]{1,0:T(8,128)(2,1)} %get-tuple-element.143.refs_1_.refs_2_.refs_5_, ...), custom_call_target="tpu_custom_call" | custom-call | flops 37580963840 | bytes 545259520 | tf_op jit(solution)/shard_map/pallas_call | solution.py:66
  698.9 12.0 %shard_map.269 = (bf16[4,256,512]{2,1,0:T(8,128)(2,1)}, bf16[4,256,512]{2,1,0:T(8,128)(2,1)}) custom-call(s32[12]{0:T(128)} %concatenate.45.refs_0_, bf16[256,2048]{1,0:T(8,128)(2,1)} %get-tuple-element.134.refs_1_.refs_7_, bf16[256,2048]{1,0:T(8,128)(2,1)} %get-tuple-element.135.refs_2_.refs_8_, bf16[256,2048]{1,0:T(8,128)(2,1)} %copy-done.35, ...), custom_call_target="tpu_custom_call" | custom-call | flops 85899345920 | bytes 251658240 | tf_op jit(solution)/shard_map/pallas_call | solution.py:66
  710.9 11.9 %shard_map.270 = (bf16[4,256,512]{2,1,0:T(8,128)(2,1)}, bf16[4,256,512]{2,1,0:T(8,128)(2,1)}) custom-call(s32[12]{0:T(128)} %concatenate.45.refs_0_, bf16[256,2048]{1,0:T(8,128)(2,1)} %get-tuple-element.134.refs_1_.refs_7_, bf16[256,2048]{1,0:T(8,128)(2,1)} %get-tuple-element.135.refs_2_.refs_8_, bf16[256,2048]{1,0:T(8,128)(2,1)} %copy-done.35, ...), custom_call_target="tpu_custom_call" | custom-call | flops 85899345920 | bytes 251658240 | tf_op jit(solution)/shard_map/pallas_call | solution.py:66
  731.8 12.1 %shard_map.272 = (bf16[256,2048]{1,0:T(8,128)(2,1)}, bf16[256,2048]{1,0:T(8,128)(2,1)}, bf16[256,2048]{1,0:T(8,128)(2,1)}, bf16[256,2048]{1,0:T(8,128)(2,1)}, f32[1,2048]{1,0:T(1,128)}) custom-call(s32[12]{0:T(128)} %concatenate.45.refs_0_, bf16[2048,512]{1,0:T(8,128)(2,1)} %get-tuple-element.238.refs_1_.refs_9_, ...), custom_call_target="tpu_custom_call" | custom-call | flops 128849018880 | bytes 272629760 | tf_op jit(solution)/shard_map/pallas_call | solution.py:66
  744.6 12.0 %shard_map.273 = (bf16[256,2048]{1,0:T(8,128)(2,1)}, bf16[256,2048]{1,0:T(8,128)(2,1)}, bf16[256,2048]{1,0:T(8,128)(2,1)}, bf16[256,2048]{1,0:T(8,128)(2,1)}, f32[1,2048]{1,0:T(1,128)}) custom-call(s32[12]{0:T(128)} %concatenate.45.refs_0_, bf16[2048,512]{1,0:T(8,128)(2,1)} %get-tuple-element.238.refs_1_.refs_9_, ...), custom_call_target="tpu_custom_call" | custom-call | flops 128849018880 | bytes 272629760 | tf_op jit(solution)/shard_map/pallas_call | solution.py:66
  774.7 12.2 %shard_map.276 = (bf16[4,256,512]{2,1,0:T(8,128)(2,1)}, bf16[4,256,512]{2,1,0:T(8,128)(2,1)}) custom-call(s32[12]{0:T(128)} %concatenate.45.refs_0_, bf16[256,2048]{1,0:T(8,128)(2,1)} %get-tuple-element.134.refs_1_.refs_7_, bf16[256,2048]{1,0:T(8,128)(2,1)} %get-tuple-element.135.refs_2_.refs_8_, bf16[256,2048]{1,0:T(8,128)(2,1)} %copy-done.35, ...), custom_call_target="tpu_custom_call" | custom-call | flops 85899345920 | bytes 251658240 | tf_op jit(solution)/shard_map/pallas_call | solution.py:66
  790.4 21.4 %collective-permute-done.58.refs_8_ = bf16[256,2048]{1,0:T(8,128)(2,1)} collective-permute-done((bf16[256,2048]{1,0:T(8,128)(2,1)}, bf16[256,2048]{1,0:T(8,128)(2,1)}, u32[]{:S(2)}, u32[]{:S(2)}) %collective-permute-start.58) | collective-permute-done | bytes 1048608 | tf_op jit(solution)/shard_map/ppermute | solution.py:900
  821.1 13.1 %reduce-scatter.12.cloned.1.call-done.refs_4_ = bf16[256,1536]{1,0:T(8,128)(2,1)} async-done(((bf16[1024,1536]{1,0:T(8,128)(2,1)}), bf16[256,1536]{1,0:T(8,128)(2,1)}) %reduce-scatter.12.cloned.1.call-update) | async-done | bytes 786448 | tf_op jit(solution)/shard_map/reduce_scatter | solution.py:920
  (304 shorter events, 312.7 us)
Async XLA Ops:
  7.2 163.4 %all-gather.3.cloned.1.call-start = ((), (), s32[]{:S(2)}) async-start(), calls=%async_computation.10 | async-start | bytes 2359296 | tf_op jit(solution)/shard_map/all_gather | solution.py:1020
  17.3 46.0 %collective-permute-start.1 = (bf16[256,2048]{1,0:T(8,128)(2,1)}, bf16[256,2048]{1,0:T(8,128)(2,1)S(1)}, u32[]{:S(2)}, u32[]{:S(2)}) collective-permute-start(bf16[256,2048]{1,0:T(8,128)(2,1)} %get-tuple-element.135.refs_2_.refs_8_), channel_id=1, source_target_pairs={{0,2},{1,3},{2,0},{3,1},{4,6},{5,7},{6,4},{7,5},{8,10},{9,11},{10,... | collective-permute-start | bytes 3145736 | tf_op jit(solution)/shard_map/ppermute | solution.py:900
  90.1 51.4 %collective-permute-start.14 = (bf16[256,2048]{1,0:T(8,128)(2,1)}, bf16[256,2048]{1,0:T(8,128)(2,1)}, u32[]{:S(2)}, u32[]{:S(2)}) collective-permute-start(bf16[256,2048]{1,0:T(8,128)(2,1)} %get-tuple-element.280.refs_2_), channel_id=1, source_target_pairs={{0,1},{1,0},{2,3},{3,2},{4,5},{5,4},{6,7},{7,6},{8,9},{9,8},{10,11... | collective-permute-start | bytes 3145736 | tf_op jit(solution)/shard_map/ppermute | solution.py:895
  90.1 51.4 %collective-permute-start.13 = (bf16[256,2048]{1,0:T(8,128)(2,1)}, bf16[256,2048]{1,0:T(8,128)(2,1)}, u32[]{:S(2)}, u32[]{:S(2)}) collective-permute-start(bf16[256,2048]{1,0:T(8,128)(2,1)} %get-tuple-element.281.refs_1_), channel_id=1, source_target_pairs={{0,1},{1,0},{2,3},{3,2},{4,5},{5,4},{6,7},{7,6},{8,9},{9,8},{10,11... | collective-permute-start | bytes 3145736 | tf_op jit(solution)/shard_map/ppermute | solution.py:895
  95.6 44.7 %collective-permute-start.10 = (bf16[256,2048]{1,0:T(8,128)(2,1)}, bf16[256,2048]{1,0:T(8,128)(2,1)}, u32[]{:S(2)}, u32[]{:S(2)}) collective-permute-start(bf16[256,2048]{1,0:T(8,128)(2,1)} %get-tuple-element.152), channel_id=1, source_target_pairs={{0,2},{1,3},{2,0},{3,1},{4,6},{5,7},{6,4},{7,5},{8,10},{9,11},{10,... | collective-permute-start | bytes 3145736 | tf_op jit(solution)/shard_map/ppermute | solution.py:900
  103.6 456.8 %reduce-scatter.6.cloned.1.call-start = ((), (), s32[]{:S(2)}) async-start(), calls=%async_computation.5 | async-start | bytes 10485760 | tf_op jit(solution)/shard_map/reduce_scatter | solution.py:920
  203.6 46.3 %collective-permute-start.20 = (bf16[256,2048]{1,0:T(8,128)(2,1)}, bf16[256,2048]{1,0:T(8,128)(2,1)S(1)}, u32[]{:S(2)}, u32[]{:S(2)}) collective-permute-start(bf16[256,2048]{1,0:T(8,128)(2,1)} %get-tuple-element.167.refs_9_), channel_id=1, source_target_pairs={{0,2},{1,3},{2,0},{3,1},{4,6},{5,7},{6,4},{7,5},{8,10},{9,11},{10,... | collective-permute-start | bytes 3145736 | tf_op jit(solution)/shard_map/ppermute | solution.py:900
  261.2 46.4 %collective-permute-start.24 = (bf16[256,2048]{1,0:T(8,128)(2,1)}, bf16[256,2048]{1,0:T(8,128)(2,1)}, u32[]{:S(2)}, u32[]{:S(2)}) collective-permute-start(bf16[256,2048]{1,0:T(8,128)(2,1)} %get-tuple-element.170.refs_2_.refs_8_), channel_id=1, source_target_pairs={{0,2},{1,3},{2,0},{3,1},{4,6},{5,7},{6,4},{7,5},{8,10},{9,11},{10,... | collective-permute-start | bytes 3145736 | tf_op jit(solution)/shard_map/ppermute | solution.py:900
  416.3 268.4 %reduce-scatter.8.cloned.1.call-start = ((), (), s32[]{:S(2)}) async-start(), calls=%async_computation.6 | async-start | bytes 5242880 | tf_op jit(solution)/shard_map/reduce_scatter | solution.py:920
  416.4 63.5 %collective-permute-start.27 = (bf16[256,2048]{1,0:T(8,128)(2,1)}, bf16[256,2048]{1,0:T(8,128)(2,1)}, u32[]{:S(2)}, u32[]{:S(2)}) collective-permute-start(bf16[256,2048]{1,0:T(8,128)(2,1)} %get-tuple-element.181), channel_id=1, source_target_pairs={{0,1},{1,0},{2,3},{3,2},{4,5},{5,4},{6,7},{7,6},{8,9},{9,8},{10,11... | collective-permute-start | bytes 3145736 | tf_op jit(solution)/shard_map/ppermute | solution.py:895
  416.6 63.2 %collective-permute-start.28 = (bf16[256,2048]{1,0:T(8,128)(2,1)}, bf16[256,2048]{1,0:T(8,128)(2,1)}, u32[]{:S(2)}, u32[]{:S(2)}) collective-permute-start(bf16[256,2048]{1,0:T(8,128)(2,1)} %get-tuple-element.182.refs_5_), channel_id=1, source_target_pairs={{0,1},{1,0},{2,3},{3,2},{4,5},{5,4},{6,7},{7,6},{8,9},{9,8},{10,11... | collective-permute-start | bytes 3145736 | tf_op jit(solution)/shard_map/ppermute | solution.py:895
  423.2 56.6 %collective-permute-start.31 = (bf16[256,2048]{1,0:T(8,128)(2,1)}, bf16[256,2048]{1,0:T(8,128)(2,1)}, u32[]{:S(2)}, u32[]{:S(2)}) collective-permute-start(bf16[256,2048]{1,0:T(8,128)(2,1)} %get-tuple-element.186), channel_id=1, source_target_pairs={{0,2},{1,3},{2,0},{3,1},{4,6},{5,7},{6,4},{7,5},{8,10},{9,11},{10,... | collective-permute-start | bytes 3145736 | tf_op jit(solution)/shard_map/ppermute | solution.py:900
  424.7 55.2 %collective-permute-start.32 = (bf16[256,2048]{1,0:T(8,128)(2,1)}, bf16[256,2048]{1,0:T(8,128)(2,1)}, u32[]{:S(2)}, u32[]{:S(2)}) collective-permute-start(bf16[256,2048]{1,0:T(8,128)(2,1)} %get-tuple-element.187.refs_11_), channel_id=1, source_target_pairs={{0,2},{1,3},{2,0},{3,1},{4,6},{5,7},{6,4},{7,5},{8,10},{9,11},{10,... | collective-permute-start | bytes 3145736 | tf_op jit(solution)/shard_map/ppermute | solution.py:900
  452.3 93.9 %collective-permute-start.43 = (bf16[4,256,2048]{2,1,0:T(8,128)(2,1)}, bf16[4,256,2048]{2,1,0:T(8,128)(2,1)}, u32[]{:S(2)}, u32[]{:S(2)}) collective-permute-start(bf16[4,256,2048]{2,1,0:T(8,128)(2,1)} %get-tuple-element.207), channel_id=1, source_target_pairs={{0,4},{4,0},{8,12},{12,8},{16,20},{20,16},{24,28},{28,24},{1,5},{5... | collective-permute-start | bytes 12582920 | tf_op jit(solution)/shard_map/ppermute | solution.py:914
  490.3 38.5 %collective-permute-start.39 = (bf16[256,2048]{1,0:T(8,128)(2,1)}, bf16[256,2048]{1,0:T(8,128)(2,1)}, u32[]{:S(2)}, u32[]{:S(2)}) collective-permute-start(bf16[256,2048]{1,0:T(8,128)(2,1)} %get-tuple-element.191.refs_1_), channel_id=1, source_target_pairs={{0,2},{1,3},{2,0},{3,1},{4,6},{5,7},{6,4},{7,5},{8,10},{9,11},{10,... | collective-permute-start | bytes 3145736 | tf_op jit(solution)/shard_map/ppermute | solution.py:900
  491.8 45.5 %collective-permute-start.40 = (bf16[256,2048]{1,0:T(8,128)(2,1)}, bf16[256,2048]{1,0:T(8,128)(2,1)}, u32[]{:S(2)}, u32[]{:S(2)}) collective-permute-start(bf16[256,2048]{1,0:T(8,128)(2,1)} %get-tuple-element.192.refs_2_), channel_id=1, source_target_pairs={{0,2},{1,3},{2,0},{3,1},{4,6},{5,7},{6,4},{7,5},{8,10},{9,11},{10,... | collective-permute-start | bytes 3145736 | tf_op jit(solution)/shard_map/ppermute | solution.py:900
  538.5 101.7 %collective-permute-start.49 = (bf16[4,256,2048]{2,1,0:T(8,128)(2,1)}, bf16[4,256,2048]{2,1,0:T(8,128)(2,1)}, u32[]{:S(2)}, u32[]{:S(2)}) collective-permute-start(bf16[4,256,2048]{2,1,0:T(8,128)(2,1)} %get-tuple-element.227), channel_id=1, source_target_pairs={{0,4},{4,0},{8,12},{12,8},{16,20},{20,16},{24,28},{28,24},{1,5},{5... | collective-permute-start | bytes 12582920 | tf_op jit(solution)/shard_map/ppermute | solution.py:914
  552.9 216.0 %reduce-scatter.10.cloned.1.call-start = ((), (), s32[]{:S(2)}) async-start(), calls=%async_computation.7 | async-start | bytes 5242880 | tf_op jit(solution)/shard_map/reduce_scatter | solution.py:920
  591.9 33.0 %collective-permute-start.47 = (bf16[2,4,128,128]{3,2,1,0:T(8,128)(2,1)}, bf16[2,4,128,128]{3,2,1,0:T(8,128)(2,1)}, u32[]{:S(2)}, u32[]{:S(2)}) collective-permute-start(bf16[2,4,128,128]{3,2,1,0:T(8,128)(2,1)} %pad_maximum_fusion.2.refs_8_), channel_id=1, source_target_pairs={{0,16},{4,20},{8,24},{12,28},{16,0},{20,4},{24,8},{28,12},{1,17},{... | collective-permute-start | bytes 786440 | tf_op jit(solution)/shard_map/ppermute | solution.py:934
  666.7 56.5 %collective-permute-start.36 = (bf16[256,2048]{1,0:T(8,128)(2,1)}, bf16[256,2048]{1,0:T(8,128)(2,1)}, u32[]{:S(2)}, u32[]{:S(2)}) collective-permute-start(bf16[256,2048]{1,0:T(8,128)(2,1)} %get-tuple-element.199.refs_3_), channel_id=1, source_target_pairs={{0,1},{1,0},{2,3},{3,2},{4,5},{5,4},{6,7},{7,6},{8,9},{9,8},{10,11... | collective-permute-start | bytes 3145736 | tf_op jit(solution)/shard_map/ppermute | solution.py:895
  666.7 56.0 %collective-permute-start.35 = (bf16[256,2048]{1,0:T(8,128)(2,1)}, bf16[256,2048]{1,0:T(8,128)(2,1)}, u32[]{:S(2)}, u32[]{:S(2)}) collective-permute-start(bf16[256,2048]{1,0:T(8,128)(2,1)} %get-tuple-element.198), channel_id=1, source_target_pairs={{0,1},{1,0},{2,3},{3,2},{4,5},{5,4},{6,7},{7,6},{8,9},{9,8},{10,11... | collective-permute-start | bytes 3145736 | tf_op jit(solution)/shard_map/ppermute | solution.py:895
  667.2 57.6 %collective-permute-start.45 = (bf16[256,2048]{1,0:T(8,128)(2,1)}, bf16[256,2048]{1,0:T(8,128)(2,1)}, u32[]{:S(2)}, u32[]{:S(2)}) collective-permute-start(bf16[256,2048]{1,0:T(8,128)(2,1)} %get-tuple-element.210.refs_7_), channel_id=1, source_target_pairs={{0,2},{1,3},{2,0},{3,1},{4,6},{5,7},{6,4},{7,5},{8,10},{9,11},{10,... | collective-permute-start | bytes 3145736 | tf_op jit(solution)/shard_map/ppermute | solution.py:900
  668.7 56.1 %collective-permute-start.44 = (bf16[256,2048]{1,0:T(8,128)(2,1)}, bf16[256,2048]{1,0:T(8,128)(2,1)}, u32[]{:S(2)}, u32[]{:S(2)}) collective-permute-start(bf16[256,2048]{1,0:T(8,128)(2,1)} %get-tuple-element.209), channel_id=1, source_target_pairs={{0,2},{1,3},{2,0},{3,1},{4,6},{5,7},{6,4},{7,5},{8,10},{9,11},{10,... | collective-permute-start | bytes 3145736 | tf_op jit(solution)/shard_map/ppermute | solution.py:900
  669.3 164.9 %reduce-scatter.12.cloned.1.call-start = ((), (), s32[]{:S(2)}) async-start(), calls=%async_computation.8 | async-start | bytes 3932160 | tf_op jit(solution)/shard_map/reduce_scatter | solution.py:920
  682.6 81.0 %collective-permute-start.59 = (bf16[4,256,512]{2,1,0:T(8,128)(2,1)}, bf16[4,256,512]{2,1,0:T(8,128)(2,1)}, u32[]{:S(2)}, u32[]{:S(2)}) collective-permute-start(bf16[4,256,512]{2,1,0:T(8,128)(2,1)} %get-tuple-element.251), channel_id=1, source_target_pairs={{0,4},{4,0},{8,12},{12,8},{16,20},{20,16},{24,28},{28,24},{1,5},{5... | collective-permute-start | bytes 3145736 | tf_op jit(solution)/shard_map/ppermute | solution.py:914
  722.8 42.4 %collective-permute-start.60 = (bf16[4,256,512]{2,1,0:T(8,128)(2,1)}, bf16[4,256,512]{2,1,0:T(8,128)(2,1)}, u32[]{:S(2)}, u32[]{:S(2)}) collective-permute-start(bf16[4,256,512]{2,1,0:T(8,128)(2,1)} %get-tuple-element.252), channel_id=1, source_target_pairs={{0,4},{4,0},{8,12},{12,8},{16,20},{20,16},{24,28},{28,24},{1,5},{5... | collective-permute-start | bytes 3145736 | tf_op jit(solution)/shard_map/ppermute | solution.py:914
  723.2 45.7 %collective-permute-start.61 = (bf16[4,256,512]{2,1,0:T(8,128)(2,1)}, bf16[4,256,512]{2,1,0:T(8,128)(2,1)}, u32[]{:S(2)}, u32[]{:S(2)}) collective-permute-start(bf16[4,256,512]{2,1,0:T(8,128)(2,1)} %get-tuple-element.253), channel_id=1, source_target_pairs={{0,4},{4,0},{8,12},{12,8},{16,20},{20,16},{24,28},{28,24},{1,5},{5... | collective-permute-start | bytes 3145736 | tf_op jit(solution)/shard_map/ppermute | solution.py:914
  756.7 33.7 %collective-permute-start.54 = (bf16[256,2048]{1,0:T(8,128)(2,1)}, bf16[256,2048]{1,0:T(8,128)(2,1)}, u32[]{:S(2)}, u32[]{:S(2)}) collective-permute-start(bf16[256,2048]{1,0:T(8,128)(2,1)} %get-tuple-element.243), channel_id=1, source_target_pairs={{0,1},{1,0},{2,3},{3,2},{4,5},{5,4},{6,7},{7,6},{8,9},{9,8},{10,11... | collective-permute-start | bytes 3145736 | tf_op jit(solution)/shard_map/ppermute | solution.py:895
  765.1 46.7 %collective-permute-start.58 = (bf16[256,2048]{1,0:T(8,128)(2,1)}, bf16[256,2048]{1,0:T(8,128)(2,1)}, u32[]{:S(2)}, u32[]{:S(2)}) collective-permute-start(bf16[256,2048]{1,0:T(8,128)(2,1)} %get-tuple-element.250.refs_7_), channel_id=1, source_target_pairs={{0,2},{1,3},{2,0},{3,1},{4,6},{5,7},{6,4},{7,5},{8,10},{9,11},{10,... | collective-permute-start | bytes 3145736 | tf_op jit(solution)/shard_map/ppermute | solution.py:900
  774.7 92.0 %reduce-scatter.14.cloned.1.call-start = ((), (), s32[]{:S(2)}) async-start(), calls=%async_computation.9 | async-start | bytes 1310720 | tf_op jit(solution)/shard_map/reduce_scatter | solution.py:920
  787.0 34.1 %collective-permute-start.67 = (bf16[4,256,512]{2,1,0:T(8,128)(2,1)}, bf16[4,256,512]{2,1,0:T(8,128)(2,1)}, u32[]{:S(2)}, u32[]{:S(2)}) collective-permute-start(bf16[4,256,512]{2,1,0:T(8,128)(2,1)} %get-tuple-element.255), channel_id=1, source_target_pairs={{0,4},{4,0},{8,12},{12,8},{16,20},{20,16},{24,28},{28,24},{1,5},{5... | collective-permute-start | bytes 3145736 | tf_op jit(solution)/shard_map/ppermute | solution.py:914
  789.0 65.1 %collective-permute-start.68 = (bf16[256,2048]{1,0:T(8,128)(2,1)}, bf16[256,2048]{1,0:T(8,128)(2,1)}, u32[]{:S(2)}, u32[]{:S(2)}) collective-permute-start(bf16[256,2048]{1,0:T(8,128)(2,1)} %constant_dynamic-slice_fusion), channel_id=1, source_target_pairs={{0,4},{4,0},{8,12},{12,8},{16,20},{20,16},{24,28},{28,24},{1,5},{5... | collective-permute-start | bytes 3145736 | tf_op jit(solution)/shard_map/ppermute | solution.py:914
  (87 other events, 1001.7 us)
Sparse Core Ops, SparseCore 0:
  103.7 50.2 all-gather.2
  416.4 143.9 reduce-scatter.5
  563.3 85.9 reduce-scatter.7
  669.4 75.6 reduce-scatter.9
  774.8 59.3 reduce-scatter.11
  838.6 28.0 reduce-scatter.13

commit v5 on v4

--- a/solution.py
+++ b/solution.py
@@ -120,7 +120,7 @@
 def rows_call(kernel, outs, sc, rows, shared, sums=0):
     first = rows[0]
     R, D = (2 * first[0].shape[0], first[0].shape[1]) if isinstance(first, tuple) else first.shape
-    n = min(128, R // 2)
+    n = min(64, R // 2)
     half = R // 2 // n
     block = pl.BlockSpec((n, D), lambda i, s: (i, 0))
     low = pl.BlockSpec((n, D), lambda i, s: (jnp.minimum(i, half - 1), 0))

time: 885 us -> 892 us (level)
  Pallas kernels: 573 us -> 586 us
  waiting for transfers between devices: 195 us -> 186 us
    pallas_call x50, Pallas kernels: 573 us -> 586 us  [run(): out = made(*operands, *ORDERED)]
  transfers between devices with their start and end apart: 75 -> 75, of which waited for: 29 -> 29; matrix products, arithmetic and copies ran while one was open for 3% -> 3% of each run, Pallas kernels for 52% -> 53%
where the time goes in v5:
time: 892 us; the launch traced here: 882 us
  Pallas kernels  586 us (66%)
  waiting for transfers between devices  186 us (21%)
  starting transfers between devices  54.8 us (6%)
  local copies, waits for them, and re-layouts  24.5 us (3%)
  between operations  16.4 us (2%)
  other arithmetic  14.3 us (2%)
    pallas_call x50, Pallas kernels, run(): out = made(*operands, *ORDERED)  586 us
    ppermute x16, waiting for transfers between devices, shift_chip(): lax.ppermute(x, 'tensor', [(i, (i + 2 * j) % count) for i in range(count)])  134 us
    reduce_scatter x5, waiting for transfers between devices, sum_z(): lax.psum_scatter(x, 'dp', scatter_dimension=0, axis_index_groups=groups,...  17.9 us
  transfers between devices with their start and end apart: 75, of which 29 were waited for; matrix products, arithmetic and copies ran while one was open for 3% of the time, Pallas kernels for 53%

profile of v5, /device:TPU:0, one launch (start us, length us, event | category | flops | bytes accessed | tf_op | source)
XLA Modules:
  0.0 882.1 jit_solution(17348335886691589096)
XLA Ops:
  27.2 12.8 %shard_map.230 = (bf16[2048,512]{1,0:T(8,128)(2,1)}, bf16[2048,512]{1,0:T(8,128)(2,1)}, bf16[2048,512]{1,0:T(8,128)(2,1)}, f32[1,512]{1,0:T(1,128)}) custom-call(s32[12]{0:T(128)} %concatenate.45.refs_0_, bf16[256,2048]{1,0:T(8,128)(2,1)} %get-tuple-element.134.refs_1_.refs_7_, bf16[256,2048]{1,0:T(8,128)(2,1)} %get-tuple-element.135.refs_2_.refs_8_, ...), custom_call_target="tpu_custom_call" | custom-call | flops 128849018880 | bytes 272629760 | tf_op jit(solution)/shard_map/pallas_call | solution.py:66
  43.3 21.8 %collective-permute-done.1.refs_2_ = bf16[256,2048]{1,0:T(8,128)(2,1)S(1)} collective-permute-done((bf16[256,2048]{1,0:T(8,128)(2,1)}, bf16[256,2048]{1,0:T(8,128)(2,1)S(1)}, u32[]{:S(2)}, u32[]{:S(2)}) %collective-permute-start.1) | collective-permute-done | bytes 1048608 | tf_op jit(solution)/shard_map/ppermute | solution.py:900
  72.2 12.6 %shard_map.232 = (bf16[2048,512]{1,0:T(8,128)(2,1)}, bf16[2048,512]{1,0:T(8,128)(2,1)}, bf16[2048,512]{1,0:T(8,128)(2,1)}, f32[1,512]{1,0:T(1,128)}) custom-call(s32[12]{0:T(128)} %concatenate.45.refs_0_, bf16[256,2048]{1,0:T(8,128)(2,1)} %get-tuple-element.137.refs_1_.refs_11_.refs_5_.refs_7_, ...), custom_call_target="tpu_custom_call", output_to_operand_aliasing={{0}: (8, {}), {1}: (9, {}), {2}: (10, {})} | custom-call | flops 128849018880 | bytes 272629760 | tf_op jit(solution)/shard_map/pallas_call | solution.py:66
  127.9 14.3 %collective-permute-done.10.refs_2_ = bf16[256,2048]{1,0:T(8,128)(2,1)} collective-permute-done((bf16[256,2048]{1,0:T(8,128)(2,1)}, bf16[256,2048]{1,0:T(8,128)(2,1)}, u32[]{:S(2)}, u32[]{:S(2)}) %collective-permute-start.10) | collective-permute-done | bytes 1048608 | tf_op jit(solution)/shard_map/ppermute | solution.py:900
  143.4 14.3 %shard_map.237.refs_6_.refs_7_ = bf16[1024,2048]{1,0:T(8,128)(2,1)} custom-call(s32[12]{0:T(128)} %concatenate.45.refs_0_, bf16[256,2048]{1,0:T(8,128)(2,1)} %get-tuple-element.281.refs_1_, bf16[256,2048]{1,0:T(8,128)(2,1)} %get-tuple-element.280.refs_2_, bf16[256,2048]{1,0:T(8,128)(2,1)} %collective-permute-done.13.refs_3_, ...), custom_call_target="tpu_custom_call" | custom-call | flops 171798691840 | bytes 335544320 | tf_op jit(solution)/shard_map/pallas_call | solution.py:66
  157.7 14.5 %shard_map.238.refs_3_.refs_7_ = bf16[1024,2048]{1,0:T(8,128)(2,1)} custom-call(s32[12]{0:T(128)} %concatenate.45.refs_0_, bf16[256,2048]{1,0:T(8,128)(2,1)} %get-tuple-element.154.refs_6_.refs_1_.refs_5_, bf16[256,2048]{1,0:T(8,128)(2,1)} %get-tuple-element.155.refs_2_.refs_6_, bf16[256,2048]{1,0:T(8,128)(2,1)} %collective-permute-done.11.refs_3_.refs_7_, ...), custom_call_target="tpu_custom_call" | custom-call | flops 171798691840 | bytes 335544320 | tf_op jit(solution)/shard_map/pallas_call | solution.py:66
  207.3 24.2 %collective-permute-done.19.refs_6_ = bf16[256,2048]{1,0:T(8,128)(2,1)S(1)} collective-permute-done((bf16[256,2048]{1,0:T(8,128)(2,1)}, bf16[256,2048]{1,0:T(8,128)(2,1)S(1)}, u32[]{:S(2)}, u32[]{:S(2)}) %collective-permute-start.19) | collective-permute-done | bytes 1048608 | tf_op jit(solution)/shard_map/ppermute | solution.py:900
  231.4 21.6 %collective-permute-done.20.refs_7_ = bf16[256,2048]{1,0:T(8,128)(2,1)S(1)} collective-permute-done((bf16[256,2048]{1,0:T(8,128)(2,1)}, bf16[256,2048]{1,0:T(8,128)(2,1)S(1)}, u32[]{:S(2)}, u32[]{:S(2)}) %collective-permute-start.20) | collective-permute-done | bytes 1048608 | tf_op jit(solution)/shard_map/ppermute | solution.py:900
  269.2 27.3 %shard_map.244 = (bf16[1024,2048]{1,0:T(8,128)(2,1)}, bf16[1024,2048]{1,0:T(8,128)(2,1)}, bf16[1024,2048]{1,0:T(8,128)(2,1)}) custom-call(s32[12]{0:T(128)} %concatenate.45.refs_0_, bf16[256,2048]{1,0:T(8,128)(2,1)} %get-tuple-element.169.refs_1_, bf16[256,2048]{1,0:T(8,128)(2,1)} %get-tuple-element.170.refs_2_.refs_8_, bf16[256,2048]{1,0:T(8,128)(2,1)} %copy-done.40, ...), custom_call_target="tpu_custom_call" | custom-call | flops 343597383680 | bytes 754974720 | tf_op jit(solution)/shard_map/pallas_call | solution.py:66
  296.5 15.8 %collective-permute-done.24.refs_2_ = bf16[256,2048]{1,0:T(8,128)(2,1)} collective-permute-done((bf16[256,2048]{1,0:T(8,128)(2,1)}, bf16[256,2048]{1,0:T(8,128)(2,1)}, u32[]{:S(2)}, u32[]{:S(2)}) %collective-permute-start.24) | collective-permute-done | bytes 1048608 | tf_op jit(solution)/shard_map/ppermute | solution.py:900
  318.3 27.6 %shard_map.246 = (bf16[1024,2048]{1,0:T(8,128)(2,1)}, bf16[1024,2048]{1,0:T(8,128)(2,1)}, bf16[1024,2048]{1,0:T(8,128)(2,1)}) custom-call(s32[12]{0:T(128)} %concatenate.45.refs_0_, bf16[256,2048]{1,0:T(8,128)(2,1)} %get-tuple-element.174.refs_1_.refs_8_.refs_5_, bf16[256,2048]{1,0:T(8,128)(2,1)} %get-tuple-element.175.refs_2_.refs_6_, ...), custom_call_target="tpu_custom_call" | custom-call | flops 343597383680 | bytes 754974720 | tf_op jit(solution)/shard_map/pallas_call | solution.py:66
  345.9 25.8 %shard_map.247.refs_5_ = bf16[8,256,2048]{2,1,0:T(8,128)(2,1)} custom-call(s32[12]{0:T(128)} %concatenate.45.refs_0_, bf16[256,2048]{1,0:T(8,128)(2,1)} %get-tuple-element.169.refs_1_, bf16[256,2048]{1,0:T(8,128)(2,1)} %get-tuple-element.170.refs_2_.refs_8_, bf16[256,2048]{1,0:T(8,128)(2,1)} %copy-done.40, bf16[256,2048]{1,0:T(8,128)(2,1)} %copy-done.41, ...), custom_call_target="tpu_custom_call" | custom-call | flops 343597383680 | bytes 503316480 | tf_op jit(solution)/shard_map/pallas_call | solution.py:66
  371.6 24.5 %shard_map.248 = (bf16[256,2048]{1,0:T(8,128)(2,1)}, bf16[256,2048]{1,0:T(8,128)(2,1)}, bf16[256,2048]{1,0:T(8,128)(2,1)}, bf16[256,2048]{1,0:T(8,128)(2,1)}) custom-call(s32[12]{0:T(128)} %concatenate.45.refs_0_, bf16[1024,2048]{1,0:T(8,128)(2,1)} %get-tuple-element.176.refs_1_.refs_10_, bf16[1024,2048]{1,0:T(8,128)(2,1)} %get-tuple-element.177.refs_10_.refs_11_.refs_2_, ...), custom_call_target="tpu_custom_call" | custom-call | flops 343597383680 | bytes 587202560 | tf_op jit(solution)/shard_map/pallas_call | solution.py:66
  396.6 24.4 %shard_map.249 = (bf16[256,2048]{1,0:T(8,128)(2,1)}, bf16[256,2048]{1,0:T(8,128)(2,1)}, bf16[256,2048]{1,0:T(8,128)(2,1)}, bf16[256,2048]{1,0:T(8,128)(2,1)}) custom-call(s32[12]{0:T(128)} %concatenate.45.refs_0_, bf16[1024,2048]{1,0:T(8,128)(2,1)} %get-tuple-element.172.refs_1_.refs_9_, bf16[1024,2048]{1,0:T(8,128)(2,1)} %get-tuple-element.173.refs_3_.refs_9_.refs_2_, ...), custom_call_target="tpu_custom_call" | custom-call | flops 343597383680 | bytes 587202560 | tf_op jit(solution)/shard_map/pallas_call | solution.py:66
  431.8 27.0 %shard_map.251 = (bf16[4,256,2048]{2,1,0:T(8,128)(2,1)}, bf16[4,256,2048]{2,1,0:T(8,128)(2,1)}) custom-call(s32[12]{0:T(128)} %concatenate.45.refs_0_, bf16[256,2048]{1,0:T(8,128)(2,1)} %get-tuple-element.169.refs_1_, bf16[256,2048]{1,0:T(8,128)(2,1)} %get-tuple-element.170.refs_2_.refs_8_, bf16[256,2048]{1,0:T(8,128)(2,1)} %copy-done.40, ...), custom_call_target="tpu_custom_call" | custom-call | flops 343597383680 | bytes 503316480 | tf_op jit(solution)/shard_map/pallas_call | solution.py:66
  459.3 27.1 %shard_map.252 = (bf16[4,256,2048]{2,1,0:T(8,128)(2,1)}, bf16[4,256,2048]{2,1,0:T(8,128)(2,1)}) custom-call(s32[12]{0:T(128)} %concatenate.45.refs_0_, bf16[256,2048]{1,0:T(8,128)(2,1)} %get-tuple-element.281.refs_1_, bf16[256,2048]{1,0:T(8,128)(2,1)} %get-tuple-element.280.refs_2_, bf16[256,2048]{1,0:T(8,128)(2,1)} %collective-permute-done.13.refs_3_, ...), custom_call_target="tpu_custom_call" | custom-call | flops 343597383680 | bytes 503316480 | tf_op jit(solution)/shard_map/pallas_call | solution.py:66
  486.5 11.4 %shard_map.253 = (f32[512,2048]{1,0:T(8,128)}, bf16[256,2048]{1,0:T(8,128)(2,1)}, bf16[256,2048]{1,0:T(8,128)(2,1)}, f32[1,2048]{1,0:T(1,128)}) custom-call(s32[12]{0:T(128)} %concatenate.45.refs_0_, bf16[512,2048]{1,0:T(8,128)(2,1)} %refs_1_.5, f32[512,2048]{1,0:T(8,128)} %get-tuple-element.168.refs_2_.refs_1_, ...), custom_call_target="tpu_custom_call" | custom-call | flops 209715200 | bytes 419430400 | tf_op jit(solution)/shard_map/pallas_call | solution.py:66
  500.2 13.8 %shard_map.254 = (bf16[256,2048]{1,0:T(8,128)(2,1)}, bf16[256,2048]{1,0:T(8,128)(2,1)}, bf16[256,2048]{1,0:T(8,128)(2,1)}, bf16[256,2048]{1,0:T(8,128)(2,1)}) custom-call(s32[12]{0:T(128)} %concatenate.45.refs_0_, bf16[1024,2048]{1,0:T(8,128)(2,1)} %get-tuple-element.188.refs_10_.refs_1_, bf16[2048,2048]{1,0:T(8,128)(2,1)} %refs_2_.4, ...), custom_call_target="tpu_custom_call" | custom-call | flops 171798691840 | bytes 335544320 | tf_op jit(solution)/shard_map/pallas_call | solution.py:66
  522.5 13.8 %shard_map.256 = (bf16[256,2048]{1,0:T(8,128)(2,1)}, bf16[256,2048]{1,0:T(8,128)(2,1)}, bf16[256,2048]{1,0:T(8,128)(2,1)}, bf16[256,2048]{1,0:T(8,128)(2,1)}) custom-call(s32[12]{0:T(128)} %concatenate.45.refs_0_, bf16[1024,2048]{1,0:T(8,128)(2,1)} %get-tuple-element.171.refs_9_.refs_1_, bf16[2048,2048]{1,0:T(8,128)(2,1)} %refs_2_.4, ...), custom_call_target="tpu_custom_call" | custom-call | flops 171798691840 | bytes 335544320 | tf_op jit(solution)/shard_map/pallas_call | solution.py:66
  585.1 12.4 %shard_map.261 = (f32[2048,128]{1,0:T(8,128)}, f32[2048,128]{1,0:T(8,128)}, f32[2048,128]{1,0:T(8,128)}) custom-call(s32[12]{0:T(128)} %concatenate.45.refs_0_, bf16[2048,512]{1,0:T(8,128)(2,1)} %get-tuple-element.142.refs_1_.refs_7_.refs_4_, bf16[2048,512]{1,0:T(8,128)(2,1)} %get-tuple-element.143.refs_1_.refs_2_.refs_5_, ...), custom_call_target="tpu_custom_call" | custom-call | flops 128849018880 | bytes 136314880 | tf_op jit(solution)/shard_map/pallas_call | solution.py:66
  600.4 12.6 %shard_map.262 = (f32[2048,128]{1,0:T(8,128)}, f32[2048,128]{1,0:T(8,128)}, f32[2048,128]{1,0:T(8,128)}) custom-call(s32[12]{0:T(128)} %concatenate.45.refs_0_, bf16[2048,512]{1,0:T(8,128)(2,1)} %get-tuple-element.142.refs_1_.refs_7_.refs_4_, bf16[2048,512]{1,0:T(8,128)(2,1)} %get-tuple-element.143.refs_1_.refs_2_.refs_5_, ...), custom_call_target="tpu_custom_call" | custom-call | flops 128849018880 | bytes 136314880 | tf_op jit(solution)/shard_map/pallas_call | solution.py:66
  613.0 12.5 %shard_map.263 = (f32[2048,128]{1,0:T(8,128)}, f32[2048,128]{1,0:T(8,128)}, f32[2048,128]{1,0:T(8,128)}) custom-call(s32[12]{0:T(128)} %concatenate.45.refs_0_, bf16[2048,512]{1,0:T(8,128)(2,1)} %get-tuple-element.142.refs_1_.refs_7_.refs_4_, bf16[2048,512]{1,0:T(8,128)(2,1)} %get-tuple-element.143.refs_1_.refs_2_.refs_5_, ...), custom_call_target="tpu_custom_call" | custom-call | flops 128849018880 | bytes 136314880 | tf_op jit(solution)/shard_map/pallas_call | solution.py:66
  633.1 12.7 %shard_map.264 = (f32[2048,128]{1,0:T(8,128)}, f32[2048,128]{1,0:T(8,128)}, f32[2048,128]{1,0:T(8,128)}) custom-call(s32[12]{0:T(128)} %concatenate.45.refs_0_, bf16[2048,512]{1,0:T(8,128)(2,1)} %get-tuple-element.142.refs_1_.refs_7_.refs_4_, bf16[2048,512]{1,0:T(8,128)(2,1)} %get-tuple-element.143.refs_1_.refs_2_.refs_5_, ...), custom_call_target="tpu_custom_call" | custom-call | flops 128849018880 | bytes 136314880 | tf_op jit(solution)/shard_map/pallas_call | solution.py:66
  654.7 11.6 %shard_map.266 = (f32[4,128,128]{2,1,0:T(8,128)}, f32[4,1,128]{2,1,0:T(1,128)}) custom-call(s32[12]{0:T(128)} %concatenate.45.refs_0_, f32[8,8,128]{2,1,0:T(8,128)} %pad_maximum_fusion.3.refs_3_.refs_1_.refs_20_, bf16[8,2,4,128,128]{4,3,2,1,0:T(8,128)(2,1)} %bitcast.45, bf16[8,4,128,128]{3,2,1,0:T(8,128)(2,1)} %pad_maximum_fusion.refs_3_, ...), custom_call_target="tpu_custom_call" | custom-call | flops 21474836480 | bytes 125829120 | tf_op jit(solution)/shard_map/pallas_call | solution.py:66
  675.9 12.4 %shard_map.267 = (bf16[4,256,512]{2,1,0:T(8,128)(2,1)}, bf16[4,256,512]{2,1,0:T(8,128)(2,1)}) custom-call(s32[12]{0:T(128)} %concatenate.45.refs_0_, bf16[256,2048]{1,0:T(8,128)(2,1)} %get-tuple-element.191.refs_1_, bf16[256,2048]{1,0:T(8,128)(2,1)} %get-tuple-element.192.refs_2_, bf16[256,2048]{1,0:T(8,128)(2,1)} %collective-permute-done.33.refs_3_, ...), custom_call_target="tpu_custom_call" | custom-call | flops 85899345920 | bytes 251658240 | tf_op jit(solution)/shard_map/pallas_call | solution.py:66
  690.4 14.2 %shard_map.268 = (bf16[2048,512]{1,0:T(8,128)(2,1)}, bf16[2048,512]{1,0:T(8,128)(2,1)}, bf16[2048,512]{1,0:T(8,128)(2,1)}) custom-call(s32[12]{0:T(128)} %concatenate.45.refs_0_, bf16[2048,512]{1,0:T(8,128)(2,1)} %get-tuple-element.142.refs_1_.refs_7_.refs_4_, bf16[2048,512]{1,0:T(8,128)(2,1)} %get-tuple-element.143.refs_1_.refs_2_.refs_5_, ...), custom_call_target="tpu_custom_call" | custom-call | flops 37580963840 | bytes 545259520 | tf_op jit(solution)/shard_map/pallas_call | solution.py:66
  704.7 12.0 %shard_map.269 = (bf16[4,256,512]{2,1,0:T(8,128)(2,1)}, bf16[4,256,512]{2,1,0:T(8,128)(2,1)}) custom-call(s32[12]{0:T(128)} %concatenate.45.refs_0_, bf16[256,2048]{1,0:T(8,128)(2,1)} %get-tuple-element.134.refs_1_.refs_7_, bf16[256,2048]{1,0:T(8,128)(2,1)} %get-tuple-element.135.refs_2_.refs_8_, bf16[256,2048]{1,0:T(8,128)(2,1)} %copy-done.35, ...), custom_call_target="tpu_custom_call" | custom-call | flops 85899345920 | bytes 251658240 | tf_op jit(solution)/shard_map/pallas_call | solution.py:66
  716.6 11.9 %shard_map.270 = (bf16[4,256,512]{2,1,0:T(8,128)(2,1)}, bf16[4,256,512]{2,1,0:T(8,128)(2,1)}) custom-call(s32[12]{0:T(128)} %concatenate.45.refs_0_, bf16[256,2048]{1,0:T(8,128)(2,1)} %get-tuple-element.134.refs_1_.refs_7_, bf16[256,2048]{1,0:T(8,128)(2,1)} %get-tuple-element.135.refs_2_.refs_8_, bf16[256,2048]{1,0:T(8,128)(2,1)} %copy-done.35, ...), custom_call_target="tpu_custom_call" | custom-call | flops 85899345920 | bytes 251658240 | tf_op jit(solution)/shard_map/pallas_call | solution.py:66
  739.1 12.1 %shard_map.272 = (bf16[256,2048]{1,0:T(8,128)(2,1)}, bf16[256,2048]{1,0:T(8,128)(2,1)}, bf16[256,2048]{1,0:T(8,128)(2,1)}, bf16[256,2048]{1,0:T(8,128)(2,1)}, f32[1,2048]{1,0:T(1,128)}) custom-call(s32[12]{0:T(128)} %concatenate.45.refs_0_, bf16[2048,512]{1,0:T(8,128)(2,1)} %get-tuple-element.238.refs_1_.refs_9_, ...), custom_call_target="tpu_custom_call" | custom-call | flops 128849018880 | bytes 272629760 | tf_op jit(solution)/shard_map/pallas_call | solution.py:66
  751.8 12.0 %shard_map.273 = (bf16[256,2048]{1,0:T(8,128)(2,1)}, bf16[256,2048]{1,0:T(8,128)(2,1)}, bf16[256,2048]{1,0:T(8,128)(2,1)}, bf16[256,2048]{1,0:T(8,128)(2,1)}, f32[1,2048]{1,0:T(1,128)}) custom-call(s32[12]{0:T(128)} %concatenate.45.refs_0_, bf16[2048,512]{1,0:T(8,128)(2,1)} %get-tuple-element.238.refs_1_.refs_9_, ...), custom_call_target="tpu_custom_call" | custom-call | flops 128849018880 | bytes 272629760 | tf_op jit(solution)/shard_map/pallas_call | solution.py:66
  780.6 12.1 %shard_map.276 = (bf16[4,256,512]{2,1,0:T(8,128)(2,1)}, bf16[4,256,512]{2,1,0:T(8,128)(2,1)}) custom-call(s32[12]{0:T(128)} %concatenate.45.refs_0_, bf16[256,2048]{1,0:T(8,128)(2,1)} %get-tuple-element.134.refs_1_.refs_7_, bf16[256,2048]{1,0:T(8,128)(2,1)} %get-tuple-element.135.refs_2_.refs_8_, bf16[256,2048]{1,0:T(8,128)(2,1)} %copy-done.35, ...), custom_call_target="tpu_custom_call" | custom-call | flops 85899345920 | bytes 251658240 | tf_op jit(solution)/shard_map/pallas_call | solution.py:66
  798.8 21.8 %collective-permute-done.58.refs_8_ = bf16[256,2048]{1,0:T(8,128)(2,1)} collective-permute-done((bf16[256,2048]{1,0:T(8,128)(2,1)}, bf16[256,2048]{1,0:T(8,128)(2,1)}, u32[]{:S(2)}, u32[]{:S(2)}) %collective-permute-start.58) | collective-permute-done | bytes 1048608 | tf_op jit(solution)/shard_map/ppermute | solution.py:900
  (304 shorter events, 320.9 us)
Async XLA Ops:
  7.2 165.0 %all-gather.3.cloned.1.call-start = ((), (), s32[]{:S(2)}) async-start(), calls=%async_computation.10 | async-start | bytes 2359296 | tf_op jit(solution)/shard_map/all_gather | solution.py:1020
  19.2 46.0 %collective-permute-start.1 = (bf16[256,2048]{1,0:T(8,128)(2,1)}, bf16[256,2048]{1,0:T(8,128)(2,1)S(1)}, u32[]{:S(2)}, u32[]{:S(2)}) collective-permute-start(bf16[256,2048]{1,0:T(8,128)(2,1)} %get-tuple-element.135.refs_2_.refs_8_), channel_id=1, source_target_pairs={{0,2},{1,3},{2,0},{3,1},{4,6},{5,7},{6,4},{7,5},{8,10},{9,11},{10,... | collective-permute-start | bytes 3145736 | tf_op jit(solution)/shard_map/ppermute | solution.py:900
  92.0 51.4 %collective-permute-start.14 = (bf16[256,2048]{1,0:T(8,128)(2,1)}, bf16[256,2048]{1,0:T(8,128)(2,1)}, u32[]{:S(2)}, u32[]{:S(2)}) collective-permute-start(bf16[256,2048]{1,0:T(8,128)(2,1)} %get-tuple-element.280.refs_2_), channel_id=1, source_target_pairs={{0,1},{1,0},{2,3},{3,2},{4,5},{5,4},{6,7},{7,6},{8,9},{9,8},{10,11... | collective-permute-start | bytes 3145736 | tf_op jit(solution)/shard_map/ppermute | solution.py:895
  92.0 51.4 %collective-permute-start.13 = (bf16[256,2048]{1,0:T(8,128)(2,1)}, bf16[256,2048]{1,0:T(8,128)(2,1)}, u32[]{:S(2)}, u32[]{:S(2)}) collective-permute-start(bf16[256,2048]{1,0:T(8,128)(2,1)} %get-tuple-element.281.refs_1_), channel_id=1, source_target_pairs={{0,1},{1,0},{2,3},{3,2},{4,5},{5,4},{6,7},{7,6},{8,9},{9,8},{10,11... | collective-permute-start | bytes 3145736 | tf_op jit(solution)/shard_map/ppermute | solution.py:895
  97.5 44.7 %collective-permute-start.10 = (bf16[256,2048]{1,0:T(8,128)(2,1)}, bf16[256,2048]{1,0:T(8,128)(2,1)}, u32[]{:S(2)}, u32[]{:S(2)}) collective-permute-start(bf16[256,2048]{1,0:T(8,128)(2,1)} %get-tuple-element.152), channel_id=1, source_target_pairs={{0,2},{1,3},{2,0},{3,1},{4,6},{5,7},{6,4},{7,5},{8,10},{9,11},{10,... | collective-permute-start | bytes 3145736 | tf_op jit(solution)/shard_map/ppermute | solution.py:900
  105.5 459.7 %reduce-scatter.6.cloned.1.call-start = ((), (), s32[]{:S(2)}) async-start(), calls=%async_computation.5 | async-start | bytes 10485760 | tf_op jit(solution)/shard_map/reduce_scatter | solution.py:920
  206.7 46.3 %collective-permute-start.20 = (bf16[256,2048]{1,0:T(8,128)(2,1)}, bf16[256,2048]{1,0:T(8,128)(2,1)S(1)}, u32[]{:S(2)}, u32[]{:S(2)}) collective-permute-start(bf16[256,2048]{1,0:T(8,128)(2,1)} %get-tuple-element.167.refs_9_), channel_id=1, source_target_pairs={{0,2},{1,3},{2,0},{3,1},{4,6},{5,7},{6,4},{7,5},{8,10},{9,11},{10,... | collective-permute-start | bytes 3145736 | tf_op jit(solution)/shard_map/ppermute | solution.py:900
  265.9 46.4 %collective-permute-start.24 = (bf16[256,2048]{1,0:T(8,128)(2,1)}, bf16[256,2048]{1,0:T(8,128)(2,1)}, u32[]{:S(2)}, u32[]{:S(2)}) collective-permute-start(bf16[256,2048]{1,0:T(8,128)(2,1)} %get-tuple-element.170.refs_2_.refs_8_), channel_id=1, source_target_pairs={{0,2},{1,3},{2,0},{3,1},{4,6},{5,7},{6,4},{7,5},{8,10},{9,11},{10,... | collective-permute-start | bytes 3145736 | tf_op jit(solution)/shard_map/ppermute | solution.py:900
  421.1 269.4 %reduce-scatter.8.cloned.1.call-start = ((), (), s32[]{:S(2)}) async-start(), calls=%async_computation.6 | async-start | bytes 5242880 | tf_op jit(solution)/shard_map/reduce_scatter | solution.py:920
  421.1 65.4 %collective-permute-start.27 = (bf16[256,2048]{1,0:T(8,128)(2,1)}, bf16[256,2048]{1,0:T(8,128)(2,1)}, u32[]{:S(2)}, u32[]{:S(2)}) collective-permute-start(bf16[256,2048]{1,0:T(8,128)(2,1)} %get-tuple-element.181), channel_id=1, source_target_pairs={{0,1},{1,0},{2,3},{3,2},{4,5},{5,4},{6,7},{7,6},{8,9},{9,8},{10,11... | collective-permute-start | bytes 3145736 | tf_op jit(solution)/shard_map/ppermute | solution.py:895
  421.3 65.2 %collective-permute-start.28 = (bf16[256,2048]{1,0:T(8,128)(2,1)}, bf16[256,2048]{1,0:T(8,128)(2,1)}, u32[]{:S(2)}, u32[]{:S(2)}) collective-permute-start(bf16[256,2048]{1,0:T(8,128)(2,1)} %get-tuple-element.182.refs_5_), channel_id=1, source_target_pairs={{0,1},{1,0},{2,3},{3,2},{4,5},{5,4},{6,7},{7,6},{8,9},{9,8},{10,11... | collective-permute-start | bytes 3145736 | tf_op jit(solution)/shard_map/ppermute | solution.py:895
  429.8 56.7 %collective-permute-start.31 = (bf16[256,2048]{1,0:T(8,128)(2,1)}, bf16[256,2048]{1,0:T(8,128)(2,1)}, u32[]{:S(2)}, u32[]{:S(2)}) collective-permute-start(bf16[256,2048]{1,0:T(8,128)(2,1)} %get-tuple-element.186), channel_id=1, source_target_pairs={{0,2},{1,3},{2,0},{3,1},{4,6},{5,7},{6,4},{7,5},{8,10},{9,11},{10,... | collective-permute-start | bytes 3145736 | tf_op jit(solution)/shard_map/ppermute | solution.py:900
  431.3 55.2 %collective-permute-start.32 = (bf16[256,2048]{1,0:T(8,128)(2,1)}, bf16[256,2048]{1,0:T(8,128)(2,1)}, u32[]{:S(2)}, u32[]{:S(2)}) collective-permute-start(bf16[256,2048]{1,0:T(8,128)(2,1)} %get-tuple-element.187.refs_11_), channel_id=1, source_target_pairs={{0,2},{1,3},{2,0},{3,1},{4,6},{5,7},{6,4},{7,5},{8,10},{9,11},{10,... | collective-permute-start | bytes 3145736 | tf_op jit(solution)/shard_map/ppermute | solution.py:900
  458.8 93.9 %collective-permute-start.43 = (bf16[4,256,2048]{2,1,0:T(8,128)(2,1)}, bf16[4,256,2048]{2,1,0:T(8,128)(2,1)}, u32[]{:S(2)}, u32[]{:S(2)}) collective-permute-start(bf16[4,256,2048]{2,1,0:T(8,128)(2,1)} %get-tuple-element.207), channel_id=1, source_target_pairs={{0,4},{4,0},{8,12},{12,8},{16,20},{20,16},{24,28},{28,24},{1,5},{5... | collective-permute-start | bytes 12582920 | tf_op jit(solution)/shard_map/ppermute | solution.py:914
  497.9 38.5 %collective-permute-start.39 = (bf16[256,2048]{1,0:T(8,128)(2,1)}, bf16[256,2048]{1,0:T(8,128)(2,1)}, u32[]{:S(2)}, u32[]{:S(2)}) collective-permute-start(bf16[256,2048]{1,0:T(8,128)(2,1)} %get-tuple-element.191.refs_1_), channel_id=1, source_target_pairs={{0,2},{1,3},{2,0},{3,1},{4,6},{5,7},{6,4},{7,5},{8,10},{9,11},{10,... | collective-permute-start | bytes 3145736 | tf_op jit(solution)/shard_map/ppermute | solution.py:900
  499.5 45.6 %collective-permute-start.40 = (bf16[256,2048]{1,0:T(8,128)(2,1)}, bf16[256,2048]{1,0:T(8,128)(2,1)}, u32[]{:S(2)}, u32[]{:S(2)}) collective-permute-start(bf16[256,2048]{1,0:T(8,128)(2,1)} %get-tuple-element.192.refs_2_), channel_id=1, source_target_pairs={{0,2},{1,3},{2,0},{3,1},{4,6},{5,7},{6,4},{7,5},{8,10},{9,11},{10,... | collective-permute-start | bytes 3145736 | tf_op jit(solution)/shard_map/ppermute | solution.py:900
  546.3 99.6 %collective-permute-start.49 = (bf16[4,256,2048]{2,1,0:T(8,128)(2,1)}, bf16[4,256,2048]{2,1,0:T(8,128)(2,1)}, u32[]{:S(2)}, u32[]{:S(2)}) collective-permute-start(bf16[4,256,2048]{2,1,0:T(8,128)(2,1)} %get-tuple-element.227), channel_id=1, source_target_pairs={{0,4},{4,0},{8,12},{12,8},{16,20},{20,16},{24,28},{28,24},{1,5},{5... | collective-permute-start | bytes 12582920 | tf_op jit(solution)/shard_map/ppermute | solution.py:914
  559.4 215.3 %reduce-scatter.10.cloned.1.call-start = ((), (), s32[]{:S(2)}) async-start(), calls=%async_computation.7 | async-start | bytes 5242880 | tf_op jit(solution)/shard_map/reduce_scatter | solution.py:920
  598.2 32.3 %collective-permute-start.47 = (bf16[2,4,128,128]{3,2,1,0:T(8,128)(2,1)}, bf16[2,4,128,128]{3,2,1,0:T(8,128)(2,1)}, u32[]{:S(2)}, u32[]{:S(2)}) collective-permute-start(bf16[2,4,128,128]{3,2,1,0:T(8,128)(2,1)} %pad_maximum_fusion.2.refs_8_), channel_id=1, source_target_pairs={{0,16},{4,20},{8,24},{12,28},{16,0},{20,4},{24,8},{28,12},{1,17},{... | collective-permute-start | bytes 786440 | tf_op jit(solution)/shard_map/ppermute | solution.py:934
  672.5 56.3 %collective-permute-start.36 = (bf16[256,2048]{1,0:T(8,128)(2,1)}, bf16[256,2048]{1,0:T(8,128)(2,1)}, u32[]{:S(2)}, u32[]{:S(2)}) collective-permute-start(bf16[256,2048]{1,0:T(8,128)(2,1)} %get-tuple-element.199.refs_3_), channel_id=1, source_target_pairs={{0,1},{1,0},{2,3},{3,2},{4,5},{5,4},{6,7},{7,6},{8,9},{9,8},{10,11... | collective-permute-start | bytes 3145736 | tf_op jit(solution)/shard_map/ppermute | solution.py:895
  672.5 56.0 %collective-permute-start.35 = (bf16[256,2048]{1,0:T(8,128)(2,1)}, bf16[256,2048]{1,0:T(8,128)(2,1)}, u32[]{:S(2)}, u32[]{:S(2)}) collective-permute-start(bf16[256,2048]{1,0:T(8,128)(2,1)} %get-tuple-element.198), channel_id=1, source_target_pairs={{0,1},{1,0},{2,3},{3,2},{4,5},{5,4},{6,7},{7,6},{8,9},{9,8},{10,11... | collective-permute-start | bytes 3145736 | tf_op jit(solution)/shard_map/ppermute | solution.py:895
  673.0 57.6 %collective-permute-start.45 = (bf16[256,2048]{1,0:T(8,128)(2,1)}, bf16[256,2048]{1,0:T(8,128)(2,1)}, u32[]{:S(2)}, u32[]{:S(2)}) collective-permute-start(bf16[256,2048]{1,0:T(8,128)(2,1)} %get-tuple-element.210.refs_7_), channel_id=1, source_target_pairs={{0,2},{1,3},{2,0},{3,1},{4,6},{5,7},{6,4},{7,5},{8,10},{9,11},{10,... | collective-permute-start | bytes 3145736 | tf_op jit(solution)/shard_map/ppermute | solution.py:900
  674.5 56.1 %collective-permute-start.44 = (bf16[256,2048]{1,0:T(8,128)(2,1)}, bf16[256,2048]{1,0:T(8,128)(2,1)}, u32[]{:S(2)}, u32[]{:S(2)}) collective-permute-start(bf16[256,2048]{1,0:T(8,128)(2,1)} %get-tuple-element.209), channel_id=1, source_target_pairs={{0,2},{1,3},{2,0},{3,1},{4,6},{5,7},{6,4},{7,5},{8,10},{9,11},{10,... | collective-permute-start | bytes 3145736 | tf_op jit(solution)/shard_map/ppermute | solution.py:900
  675.1 165.5 %reduce-scatter.12.cloned.1.call-start = ((), (), s32[]{:S(2)}) async-start(), calls=%async_computation.8 | async-start | bytes 3932160 | tf_op jit(solution)/shard_map/reduce_scatter | solution.py:920
  688.3 84.1 %collective-permute-start.59 = (bf16[4,256,512]{2,1,0:T(8,128)(2,1)}, bf16[4,256,512]{2,1,0:T(8,128)(2,1)}, u32[]{:S(2)}, u32[]{:S(2)}) collective-permute-start(bf16[4,256,512]{2,1,0:T(8,128)(2,1)} %get-tuple-element.251), channel_id=1, source_target_pairs={{0,4},{4,0},{8,12},{12,8},{16,20},{20,16},{24,28},{28,24},{1,5},{5... | collective-permute-start | bytes 3145736 | tf_op jit(solution)/shard_map/ppermute | solution.py:914
  728.5 45.3 %collective-permute-start.60 = (bf16[4,256,512]{2,1,0:T(8,128)(2,1)}, bf16[4,256,512]{2,1,0:T(8,128)(2,1)}, u32[]{:S(2)}, u32[]{:S(2)}) collective-permute-start(bf16[4,256,512]{2,1,0:T(8,128)(2,1)} %get-tuple-element.252), channel_id=1, source_target_pairs={{0,4},{4,0},{8,12},{12,8},{16,20},{20,16},{24,28},{28,24},{1,5},{5... | collective-permute-start | bytes 3145736 | tf_op jit(solution)/shard_map/ppermute | solution.py:914
  728.8 45.8 %collective-permute-start.61 = (bf16[4,256,512]{2,1,0:T(8,128)(2,1)}, bf16[4,256,512]{2,1,0:T(8,128)(2,1)}, u32[]{:S(2)}, u32[]{:S(2)}) collective-permute-start(bf16[4,256,512]{2,1,0:T(8,128)(2,1)} %get-tuple-element.253), channel_id=1, source_target_pairs={{0,4},{4,0},{8,12},{12,8},{16,20},{20,16},{24,28},{28,24},{1,5},{5... | collective-permute-start | bytes 3145736 | tf_op jit(solution)/shard_map/ppermute | solution.py:914
  763.9 32.3 %collective-permute-start.54 = (bf16[256,2048]{1,0:T(8,128)(2,1)}, bf16[256,2048]{1,0:T(8,128)(2,1)}, u32[]{:S(2)}, u32[]{:S(2)}) collective-permute-start(bf16[256,2048]{1,0:T(8,128)(2,1)} %get-tuple-element.243), channel_id=1, source_target_pairs={{0,1},{1,0},{2,3},{3,2},{4,5},{5,4},{6,7},{7,6},{8,9},{9,8},{10,11... | collective-permute-start | bytes 3145736 | tf_op jit(solution)/shard_map/ppermute | solution.py:895
  773.9 46.7 %collective-permute-start.58 = (bf16[256,2048]{1,0:T(8,128)(2,1)}, bf16[256,2048]{1,0:T(8,128)(2,1)}, u32[]{:S(2)}, u32[]{:S(2)}) collective-permute-start(bf16[256,2048]{1,0:T(8,128)(2,1)} %get-tuple-element.250.refs_7_), channel_id=1, source_target_pairs={{0,2},{1,3},{2,0},{3,1},{4,6},{5,7},{6,4},{7,5},{8,10},{9,11},{10,... | collective-permute-start | bytes 3145736 | tf_op jit(solution)/shard_map/ppermute | solution.py:900
  780.5 92.7 %reduce-scatter.14.cloned.1.call-start = ((), (), s32[]{:S(2)}) async-start(), calls=%async_computation.9 | async-start | bytes 1310720 | tf_op jit(solution)/shard_map/reduce_scatter | solution.py:920
  792.7 38.3 %collective-permute-start.67 = (bf16[4,256,512]{2,1,0:T(8,128)(2,1)}, bf16[4,256,512]{2,1,0:T(8,128)(2,1)}, u32[]{:S(2)}, u32[]{:S(2)}) collective-permute-start(bf16[4,256,512]{2,1,0:T(8,128)(2,1)} %get-tuple-element.255), channel_id=1, source_target_pairs={{0,4},{4,0},{8,12},{12,8},{16,20},{20,16},{24,28},{28,24},{1,5},{5... | collective-permute-start | bytes 3145736 | tf_op jit(solution)/shard_map/ppermute | solution.py:914
  795.0 65.6 %collective-permute-start.68 = (bf16[256,2048]{1,0:T(8,128)(2,1)}, bf16[256,2048]{1,0:T(8,128)(2,1)}, u32[]{:S(2)}, u32[]{:S(2)}) collective-permute-start(bf16[256,2048]{1,0:T(8,128)(2,1)} %constant_dynamic-slice_fusion), channel_id=1, source_target_pairs={{0,4},{4,0},{8,12},{12,8},{16,20},{20,16},{24,28},{28,24},{1,5},{5... | collective-permute-start | bytes 3145736 | tf_op jit(solution)/shard_map/ppermute | solution.py:914
  (87 other events, 994.6 us)
Sparse Core Ops, SparseCore 0:
  105.6 50.2 all-gather.2
  421.2 143.9 reduce-scatter.5
  568.1 85.9 reduce-scatter.7
  675.2 75.5 reduce-scatter.9
  780.6 59.9 reduce-scatter.11
  845.1 28.0 reduce-scatter.13
